TPU v7x, 32 devices: a whole 2x2x4 slice. The times are simulated.
32 devices in a mesh: wide: 16 (over z, y, core), narrow: 2 (over x).
Axes of the slice: x: 2, y: 2, z: 4, core: 2. Of those that a mesh axis runs over, the one named last changes fastest.
Arguments:
- tokens: bfloat16 [2048, 2048], P('wide', 'narrow'), may hold values from -6 to 6
- expert_ids: int32 [2048, 6], P('wide'), may hold values from 0 to 15, all different within a row; in each aligned block of 128 rows (0 to 127, 128 to 255, ...) at most 56 rows name the same one
- route_weights: bfloat16 [2048, 6], P('wide'), may hold values from 0.049804688 to 0.5
- w_gate: bfloat16 [16, 1408, 2048], P('wide', 'narrow'), may hold values from -0.125 to 0.125
- w_up: bfloat16 [16, 1408, 2048], P('wide', 'narrow'), may hold values from -0.125 to 0.125
- w_down: bfloat16 [16, 1408, 2048], P('wide', 'narrow'), may hold values from -0.15625 to 0.15625
Outputs:
- mixed: bfloat16 [2048, 2048], P('wide', 'narrow')
Inputs may be any that keep to these rules, and one draw needn't show every extreme that they name: `expert_ids`: within a row the 6 experts differ. Among the 128 tokens of one aligned block, no expert is named more than 56 times, a bound that some block reaches.
All inputs are finite; a program needn't handle non-finite values.
Results may differ from a plain program's by a relative error of at most 0.017.
Values may be sent and summed in bfloat16 or wider, within the bound.
No kernel may reach another device: no remote copies, remote signals or barrier semaphores. Data moves between devices by JAX's collectives and lax.ppermute only.
A program may use at most 64 MiB of HBM per device.

v0:
```python
import jax
import jax.numpy as jnp
from jax import lax
from jax.sharding import PartitionSpec as P


def local(tokens, expert_ids, route_weights, w_gate, w_up, w_down):
    tok_rows = expert_ids.shape[0]
    top_count = expert_ids.shape[1]
    local_experts = w_gate.shape[0]
    groups_wide = lax.axis_size("wide")
    experts_all = local_experts * groups_wide
    capacity = 7 * tok_rows * top_count // (6 * experts_all)
    slots_all = experts_all * capacity
    width = w_down.shape[2]
    flat_ids = expert_ids.reshape(-1)
    onehot = (flat_ids[:, None] == jnp.arange(experts_all, dtype=jnp.int32)[None, :]).astype(
        jnp.int32
    )
    running = jnp.cumsum(onehot, axis=0)
    slot_index = jnp.sum(running * onehot, axis=1) - 1
    destination = (flat_ids * capacity + slot_index).reshape(tok_rows, top_count)
    slot_table = (
        destination[:, :, None] == jnp.arange(slots_all, dtype=jnp.int32)[None, None, :]
    ).astype(jnp.float32)
    dispatch = jnp.sum(slot_table, axis=1).astype(jnp.bfloat16)
    whole = lax.all_gather(tokens, "narrow", axis=1, tiled=True)
    outgoing = jnp.einsum("ts,td->sd", dispatch, whole, preferred_element_type=jnp.float32).astype(
        jnp.bfloat16
    )
    received = lax.all_to_all(outgoing, "wide", split_axis=0, concat_axis=0, tiled=True)
    slot_rows = received.reshape(groups_wide, local_experts, capacity, width)
    gate_proj = jnp.einsum("secd,efd->secf", slot_rows, w_gate, preferred_element_type=jnp.float32)
    up_proj = jnp.einsum("secd,efd->secf", slot_rows, w_up, preferred_element_type=jnp.float32)
    hidden = (jax.nn.silu(gate_proj) * up_proj).astype(jnp.bfloat16)
    partial_value = jnp.einsum(
        "secf,efd->secd", hidden, w_down, preferred_element_type=jnp.float32
    ).astype(jnp.bfloat16)
    partial_value = partial_value.reshape(slots_all, width)
    summed = lax.psum_scatter(partial_value, "narrow", scatter_dimension=1, tiled=True).astype(
        jnp.float32
    )
    returned = lax.all_to_all(
        summed.astype(jnp.bfloat16), "wide", split_axis=0, concat_axis=0, tiled=True
    ).astype(summed.dtype)
    picked = returned[destination.reshape(-1)].reshape(tok_rows, top_count, -1)
    mixed = jnp.sum(route_weights.astype(jnp.float32)[:, :, None] * picked, axis=1)
    return mixed.astype(jnp.bfloat16)


def solution(mesh):
    in_specs = (
        P("wide", "narrow"),
        P("wide", None),
        P("wide", None),
        P("wide", "narrow", None),
        P("wide", "narrow", None),
        P("wide", "narrow", None),
    )
    out_specs = P("wide", "narrow")
    return jax.shard_map(local, mesh=mesh, in_specs=in_specs, out_specs=out_specs, check_vma=False)
```

profile of v0, /device:TPU:0, one launch (start us, length us, event | category | flops | bytes accessed | tf_op | source)
XLA Modules:
  0.0 245.0 jit_solution(7665369742651740645)
XLA Ops:
  6.5 0.0 copy-start
  6.5 0.0 reduce-scatter.2.cloned.1.call-start
  6.5 0.9 copy.15
  7.5 0.1 eq.42
  7.6 0.1 eq.38
  7.8 1.7 reduce-window.6
  9.5 0.3 slice_reduce_fusion
  9.8 0.1 fusion.18
  9.9 0.1 sub.9
  10.0 0.1 copy.19
  10.1 0.4 convert_reduce_fusion
  10.5 10.2 %all_gather.3 = bf16[128,2048]{1,0:T(8,128)(2,1)S(1)} all-gather(bf16[128,1024]{1,0:T(8,128)(2,1)} %param.6), channel_id=1, replica_groups=mesh['wide'=16,'narrow'=2] {'narrow'}, dimensions={1}, use_global_device_ids=true | all-gather | bytes 786432 | tf_op jit(solution)/shard_map/all_gather | solution.py:27
  20.7 1.1 convolution_convert_fusion.1
  21.8 0.0 copy-start.3
  21.8 87.2 %all_to_all.18 = bf16[16,56,2048]{2,1,0:T(8,128)(2,1)S(1)} all-to-all(bf16[16,56,2048]{2,1,0:T(8,128)(2,1)S(1)} %bitcast.87), channel_id=1, replica_groups=mesh['wide'=16,'narrow'=2] {'wide'}, dimensions={0} | all-to-all | bytes 7340032 | tf_op jit(solution)/shard_map/all_to_all | solution.py:31
  109.1 0.0 copy-start.1
  109.1 1.8 copy-done.1
  110.9 0.0 copy-done.3
  110.9 4.6 %fusion.1 = f32[16,56,704]{2,1,0:T(8,128)} fusion(bf16[16,56,2048]{2,1,0:T(8,128)(2,1)S(1)} %all_to_all.18, bf16[1,704,2048]{2,1,0:T(8,128)(2,1)S(1)} %copy-done.3), kind=kOutput, calls=%fused_computation.5 | convolution fusion | flops 2583691264 | bytes 9076736 | tf_op jit(solution)/shard_map/secd,efd->secf/dot_general | solution.py:34
  115.6 0.0 copy-done
  115.6 11.2 %convolution_convert_fusion = bf16[16,56,2048]{2,1,0:T(8,128)(2,1)} fusion(bf16[1,704,2048]{2,1,0:T(8,128)(2,1)S(1)} %copy-done, f32[16,56,704]{2,1,0:T(8,128)} %fusion.1, bf16[16,56,2048]{2,1,0:T(8,128)(2,1)} %copy-done.1, bf16[1,704,2048]{2,1,0:T(8,128)(2,1)} %param.9), kind=kOutput, calls=%fused_computation.2 | convolution fusion | flops 5173002240 | bytes 15630336 | tf_op jit(solution)/shard_map/secf,efd->secd/dot_general | solution.py:36
  126.8 0.0 reduce-scatter.2.cloned.1.call-update
  126.8 49.8 %reduce-scatter.2.cloned.1.call-done = bf16[896,1024]{1,0:T(8,128)(2,1)} async-done(((bf16[896,2048]{1,0:T(8,128)(2,1)}), bf16[896,1024]{1,0:T(8,128)(2,1)}) %reduce-scatter.2.cloned.1.call-update) | async-done | bytes 1835024 | tf_op jit(solution)/shard_map/reduce_scatter | solution.py:40
  176.5 5.7 %all-to-all-start.1 = ((bf16[16,56,1024]{2,1,0:T(8,128)(2,1)}), bf16[16,56,1024]{2,1,0:T(8,128)(2,1)}, u32[]{:S(2)}, u32[]{:S(2)}) async-start(bf16[16,56,1024]{2,1,0:T(8,128)(2,1)} %bitcast.89), calls=%async_computation.2 | async-start | bytes 3670016 | tf_op jit(solution)/shard_map/all_to_all | solution.py:43
  182.2 0.1 mul.42
  182.4 0.0 copy-done.2
  182.4 0.1 copy.14
  182.5 36.3 %all-to-all-done.1 = bf16[16,56,1024]{2,1,0:T(8,128)(2,1)} async-done(((bf16[16,56,1024]{2,1,0:T(8,128)(2,1)}), bf16[16,56,1024]{2,1,0:T(8,128)(2,1)}, u32[]{:S(2)}, u32[]{:S(2)}) %all-to-all-start.1) | async-done | bytes 1835040 | tf_op jit(solution)/shard_map/all_to_all | solution.py:43
  218.8 3.7 %bitcast_convert_fusion = f32[896,1024]{1,0:T(8,128)} fusion(bf16[16,56,1024]{2,1,0:T(8,128)(2,1)} %all-to-all-done.1), kind=kLoop, calls=%fused_computation.18 | loop fusion | flops 917504 | bytes 5505024 | tf_op jit(solution)/shard_map/convert_element_type | solution.py:45
  222.5 6.7 %gather_fusion = f32[768,1024]{1,0:T(8,128)} fusion(f32[896,1024]{1,0:T(8,128)} %bitcast_convert_fusion, s32[1024]{0:T(1024)S(1)} %pad_clamp_fusion), kind=kCustom, calls=%fused_computation | custom fusion | bytes 6294528 | tf_op jit(solution)/shard_map/gather | solution.py:46
  229.2 4.6 %reshape.101 = f32[128,6,1024]{2,1,0:T(8,128)} reshape(f32[768,1024]{1,0:T(8,128)} %gather_fusion) | data formatting | bytes 6291456 | tf_op jit(solution)/shard_map/reshape | solution.py:46
  233.8 4.3 %multiply_reduce_fusion = bf16[128,1024]{1,0:T(8,128)(2,1)} fusion(f32[128,6,1024]{2,1,0:T(8,128)} %reshape.101, f32[128,6]{1,0:T(8,128)S(1)} %copy.14), kind=kLoop, calls=%fused_computation.1 | loop fusion | flops 1441792 | bytes 3410944 | tf_op jit(solution)/shard_map/reduce_sum | solution.py:47
  (7 shorter events, 0.1 us)
Async XLA Ops:
  6.5 109.0 %copy-start = (bf16[1,704,2048]{2,1,0:T(8,128)(2,1)S(1)}, bf16[1,704,2048]{2,1,0:T(8,128)(2,1)}, u32[]{:S(2)}) copy-start(bf16[1,704,2048]{2,1,0:T(8,128)(2,1)} %param.11) | copy-start | bytes 8650756
  6.5 170.0 %reduce-scatter.2.cloned.1.call-start = ((), (), s32[]{:S(2)}) async-start(), calls=%async_computation.3 | async-start | bytes 5505024 | tf_op jit(solution)/shard_map/reduce_scatter | solution.py:40
  21.8 89.1 %copy-start.3 = (bf16[1,704,2048]{2,1,0:T(8,128)(2,1)S(1)}, bf16[1,704,2048]{2,1,0:T(8,128)(2,1)}, u32[]{:S(2)}) copy-start(bf16[1,704,2048]{2,1,0:T(8,128)(2,1)} %param.10) | copy-start | bytes 8650756
  109.1 1.8 copy-start.1
  126.7 55.6 %copy-start.2 = (bf16[128,6]{0,1:T(8,128)(2,1)S(1)}, bf16[128,6]{0,1:T(8,128)(2,1)}, u32[]{:S(2)}) copy-start(bf16[128,6]{0,1:T(8,128)(2,1)} %param.8) | copy-start | bytes 4612
  176.5 42.3 %all-to-all-start.1 = ((bf16[16,56,1024]{2,1,0:T(8,128)(2,1)}), bf16[16,56,1024]{2,1,0:T(8,128)(2,1)}, u32[]{:S(2)}, u32[]{:S(2)}) async-start(bf16[16,56,1024]{2,1,0:T(8,128)(2,1)} %bitcast.89), calls=%async_computation.2 | async-start | bytes 3670016 | tf_op jit(solution)/shard_map/all_to_all | solution.py:43
Sparse Core Ops, SparseCore 0:
  126.9 49.6 reduce-scatter.1
where the time goes:
time: 250 us; the launch traced here: 245 us
  blocking collectives  97.4 us (39%)
  waiting for transfers between devices  86.1 us (34%)
  matrix products  16.9 us (7%)
  local copies, waits for them, and re-layouts  15.1 us (6%)
  between operations  13.5 us (5%)
  other arithmetic  10.3 us (4%)
  starting transfers between devices  5.66 us (2%)
    all_to_all x1, blocking collectives, local(): lax.all_to_all(outgoing, 'wide', split_axis=0, concat_axis=0, tiled=True)  87.2 us
    reduce_scatter x1, waiting for transfers between devices, local(): lax.psum_scatter(partial_value, 'narrow', scatter_dimension=1, tiled=True)  49.8 us
    all_to_all x1, waiting for transfers between devices, local(): lax.all_to_all(summed.astype(jnp.bfloat16), 'wide', split_axis=0, concat_...  36.3 us
    dot_general x1, matrix products, local(): jnp.einsum('secf,efd->secd', hidden, w_down, preferred_element_type=jnp.f...  11.2 us
    all_gather x1, blocking collectives, local(): whole = lax.all_gather(tokens, 'narrow', axis=1, tiled=True)  10.2 us
    gather x1, local copies, waits for them, and re-layouts, local(): picked = returned[destination.reshape(-1)].reshape(tok_rows, top_count, -1)  6.72 us
    all_to_all x1, starting transfers between devices, local(): lax.all_to_all(summed.astype(jnp.bfloat16), 'wide', split_axis=0, concat_...  5.66 us
  transfers between devices with their start and end apart: 2, of which 2 were waited for; matrix products, arithmetic and copies ran while one was open for 0% of the time, Pallas kernels for 0%

commit v1 on v0

--- a/solution.py
+++ b/solution.py
@@ -1,10 +1,18 @@
+import functools
+
 import jax
 import jax.numpy as jnp
 from jax import lax
+from jax.experimental import pallas as pl
+from jax.experimental.pallas import tpu as pltpu
 from jax.sharding import PartitionSpec as P
 
-
-def local(tokens, expert_ids, route_weights, w_gate, w_up, w_down):
+CORE, Y, NEAR, FAR = 1, 2, 4, 8
+VMEM_BYTES = 48 << 20
+F32, BF16 = jnp.float32, jnp.bfloat16
+
+
+def general(tokens, expert_ids, route_weights, w_gate, w_up, w_down):
     tok_rows = expert_ids.shape[0]
     top_count = expert_ids.shape[1]
     local_experts = w_gate.shape[0]
@@ -48,6 +56,207 @@
     return mixed.astype(jnp.bfloat16)
 
 
+def kernel_call(body, out_shape, n_in, flops, bytes_accessed, scratch=()):
+    vmem = pl.BlockSpec(memory_space=pltpu.VMEM)
+    return pl.pallas_call(
+        body,
+        out_shape=out_shape,
+        in_specs=[pl.BlockSpec(memory_space=pltpu.SMEM)] + [vmem] * n_in,
+        out_specs=jax.tree.map(lambda _: vmem, out_shape),
+        scratch_shapes=list(scratch),
+        compiler_params=pltpu.CompilerParams(vmem_limit_bytes=VMEM_BYTES),
+        cost_estimate=pl.CostEstimate(flops=flops, bytes_accessed=bytes_accessed, transcendentals=0),
+    )
+
+
+def pair_rows(place_ref, routing_ref, dz, capacity, weighted):
+    me = place_ref[0]
+    toks = routing_ref.shape[2]
+    before = lax.broadcasted_iota(jnp.int32, (toks, toks), 0) <= lax.broadcasted_iota(
+        jnp.int32, (toks, toks), 1
+    )
+    rows = []
+    for expert in (me, me ^ CORE):
+        for block in (me ^ (NEAR * dz), me ^ (NEAR * dz + Y)):
+            rows.append(routing_ref[block, pl.ds(expert, 1), :])
+    weight = jnp.concatenate(rows, axis=0)
+    chosen = weight > 0
+    count = jnp.dot(
+        jnp.where(chosen, 1.0, 0.0).astype(BF16),
+        jnp.where(before, 1.0, 0.0).astype(BF16),
+        preferred_element_type=F32,
+    )
+    slot = jnp.where(chosen, count.astype(jnp.int32) - 1, -1)
+    tables = []
+    for expert in (0, 1):
+        first, second = slot[2 * expert : 2 * expert + 1], slot[2 * expert + 1 : 2 * expert + 2]
+        second = jnp.where(second >= 0, second + capacity, -1)
+        at = jnp.concatenate([first, second], axis=1)
+        value = jnp.concatenate(
+            [weight[2 * expert : 2 * expert + 1], weight[2 * expert + 1 : 2 * expert + 2]], axis=1
+        )
+        here = lax.broadcasted_iota(jnp.int32, (2 * capacity, 2 * toks), 0) == at
+        tables.append(jnp.where(here, value if weighted else 1.0, 0.0))
+    return jnp.concatenate(tables, axis=0).astype(BF16)
+
+
+def dispatch_kernel(capacity, dz_list, place_ref, routing_ref, *refs):
+    units, (own_ref, send_ref) = refs[:-2], refs[-2:]
+    rows, half = 2 * capacity, own_ref.shape[1] // 2
+    for p, dz in enumerate(dz_list):
+        table = pair_rows(place_ref, routing_ref, dz, capacity, False)
+        for dx in (0, 1):
+            first, second = units[4 * p + dx], units[4 * p + 2 + dx]
+            block = jnp.concatenate([first[...], second[...]], axis=0)
+            out = jnp.dot(table, block, preferred_element_type=F32).astype(BF16)
+            own_ref[p * rows : (p + 1) * rows, dx * half : (dx + 1) * half] = out[:rows]
+            send_ref[p * rows : (p + 1) * rows, dx * half : (dx + 1) * half] = out[rows:]
+
+
+def dispatch(place, routing, units, dz_list, capacity):
+    half = units[0].shape[1]
+    shape = jax.ShapeDtypeStruct((2 * capacity * len(dz_list), 2 * half), BF16)
+    flops = len(dz_list) * 2 * 4 * capacity * 256 * 2 * half
+    return kernel_call(
+        functools.partial(dispatch_kernel, capacity, dz_list),
+        (shape, shape),
+        1 + len(units),
+        flops,
+        len(units) * 256 * 1024 * 2,
+    )(place, routing, *units)
+
+
+def ffn_kernel(place_ref, own_ref, other_ref, gate_ref, up_ref, down_ref, own_out, other_out, rows_ref, hidden_ref):
+    x = place_ref[1]
+    n = own_ref.shape[0]
+    half = own_ref.shape[1] // 2
+    ff = gate_ref.shape[1]
+    rows_ref[:n] = own_ref[...]
+    rows_ref[n:] = other_ref[...]
+    mine = pl.ds(pl.multiple_of(x * half, half), half)
+    theirs = pl.ds(pl.multiple_of((1 - x) * half, half), half)
+    step = 256
+    nt = (((1,), (1,)), ((), ()))
+    for low in range(0, ff, step):
+        high = min(low + step, ff)
+
+        def project(ref):
+            return lax.dot_general(
+                rows_ref[:, :half], ref[0, low:high, mine], nt, preferred_element_type=F32
+            ) + lax.dot_general(
+                rows_ref[:, half:], ref[0, low:high, theirs], nt, preferred_element_type=F32
+            )
+
+        gate = project(gate_ref)
+        up = project(up_ref)
+        hidden_ref[:, low:high] = (gate / (1.0 + jnp.exp(-gate)) * up).astype(BF16)
+    for j, columns in enumerate((mine, theirs)):
+        out = jnp.dot(hidden_ref[...], down_ref[0, :, columns], preferred_element_type=F32).astype(BF16)
+        own_out[:, j * half : (j + 1) * half] = out[:n]
+        other_out[:, j * half : (j + 1) * half] = out[n:]
+
+
+def ffn(place, own, other, w_gate, w_up, w_down):
+    n, width = own.shape
+    ff = w_gate.shape[1]
+    shape = jax.ShapeDtypeStruct((n, width), BF16)
+    return kernel_call(
+        ffn_kernel,
+        (shape, shape),
+        5,
+        6 * 2 * n * width * ff,
+        6 * width * ff + 8 * n * width,
+        scratch=(pltpu.VMEM((2 * n, width), BF16), pltpu.VMEM((2 * n, ff), BF16)),
+    )(place, own, other, w_gate, w_up, w_down)
+
+
+def combine_kernel(capacity, dz_list, place_ref, routing_ref, own_ref, other_ref, *outs):
+    rows, half = 2 * capacity, own_ref.shape[1] // 2
+    toks = routing_ref.shape[2]
+    for p, dz in enumerate(dz_list):
+        table = pair_rows(place_ref, routing_ref, dz, capacity, True)
+        keep, send = outs[2 * p], outs[2 * p + 1]
+        for dx in (0, 1):
+            columns = slice(dx * half, (dx + 1) * half)
+            value = jnp.concatenate(
+                [own_ref[p * rows : (p + 1) * rows, columns], other_ref[p * rows : (p + 1) * rows, columns]],
+                axis=0,
+            )
+            out = lax.dot_general(
+                table, value, (((0,), (0,)), ((), ())), preferred_element_type=F32
+            ).astype(BF16)
+            for dy in (0, 1):
+                block = out[dy * toks : (dy + 1) * toks]
+                if p % 2 == 0:
+                    (send if dy else keep)[dx] = block
+                else:
+                    (send if dx else keep)[dy] = block
+
+
+def combine(place, routing, own, other, dz_list, capacity):
+    toks, half = routing.shape[2], own.shape[1] // 2
+    shape = jax.ShapeDtypeStruct((2, toks, half), BF16)
+    return kernel_call(
+        functools.partial(combine_kernel, capacity, dz_list),
+        (shape,) * (2 * len(dz_list)),
+        3,
+        len(dz_list) * 2 * 4 * capacity * 256 * 2 * half,
+        len(dz_list) * 8 * toks * half * 2,
+    )(place, routing, own, other)
+
+
+def local(tokens, expert_ids, route_weights, w_gate, w_up, w_down):
+    wide = lax.axis_size("wide")
+    tok_rows, top_count = expert_ids.shape
+    capacity = 7 * tok_rows * top_count // (6 * wide)
+    me, x = lax.axis_index("wide"), lax.axis_index("narrow")
+    place = jnp.stack([me, x]).astype(jnp.int32)
+
+    def hop(value, bit):
+        return lax.ppermute(value, "wide", [(i, i ^ bit) for i in range(wide)])
+
+    def hop_x(value):
+        return lax.ppermute(value, "narrow", [(0, 1), (1, 0)])
+
+    def add(a, b):
+        return (a.astype(F32) + b.astype(F32)).astype(BF16)
+
+    named = expert_ids.T[:, None, :] == jnp.arange(wide, dtype=jnp.int32)[None, :, None]
+    routing = jnp.sum(jnp.where(named, route_weights.astype(F32).T[:, None, :], 0.0), axis=0)
+    routing = lax.all_gather(routing, "wide", axis=0, tiled=False)
+
+    column = [tokens, hop(tokens, NEAR), hop(tokens, FAR), None]
+    column[3] = hop(column[2], NEAR)
+
+    def gather(dz):
+        unit = column[dz]
+        if dz % 2 == 0:
+            beside = hop_x(unit)
+            far = hop(jnp.stack([unit, beside]), Y)
+            return [unit, beside, far[0], far[1]]
+        beside = hop(unit, Y)
+        far = hop_x(jnp.stack([unit, beside]))
+        return [unit, far[0], beside, far[1]]
+
+    def chunk(dz_list):
+        units = [unit for dz in dz_list for unit in gather(dz)]
+        own, send = dispatch(place, routing, units, dz_list, capacity)
+        other = hop(send, CORE)
+        own, other = ffn(place, own, other, w_gate, w_up, w_down)
+        other = hop(other, CORE)
+        keep_a, send_a, keep_b, send_b = combine(place, routing, own, other, dz_list, capacity)
+        sum_a = add(keep_a, hop(send_a, Y))
+        sum_b = add(keep_b, hop_x(send_b))
+        return add(sum_a[0], hop_x(sum_a[1])), add(sum_b[0], hop(sum_b[1], Y))
+
+    mine, near = chunk((0, 1))
+    far, both = chunk((2, 3))
+    near = hop(near, NEAR)
+    far = add(far, hop(both, NEAR))
+    far = hop(far, FAR)
+    return (mine.astype(F32) + near.astype(F32) + far.astype(F32)).astype(BF16)
+
+
 def solution(mesh):
     in_specs = (
         P("wide", "narrow"),
@@ -58,4 +267,7 @@
         P("wide", "narrow", None),
     )
     out_specs = P("wide", "narrow")
-    return jax.shard_map(local, mesh=mesh, in_specs=in_specs, out_specs=out_specs, check_vma=False)
+    fits = mesh.shape["wide"] == 16 and mesh.shape["narrow"] == 2
+    return jax.shard_map(
+        local if fits else general, mesh=mesh, in_specs=in_specs, out_specs=out_specs, check_vma=False
+    )

time: 250 us -> 151 us (0.60); the launches traced: 245 us -> 151 us
  blocking collectives: 97.4 us -> 28.7 us
  starting transfers between devices: 5.66 us -> 28.9 us
  Pallas kernels: 0 us -> 22.2 us
  waiting for transfers between devices: 86.1 us -> 66.2 us
  matrix products: 16.9 us -> 0 us
  local copies, waits for them, and re-layouts: 15.1 us -> 0.22 us
  between operations: 13.5 us -> 0.27 us
  other arithmetic: 10.3 us -> 4.5 us
    all_to_all x1 -> x0, blocking collectives: 87.2 us -> none  [local(): lax.all_to_all(outgoing, 'wide', split_axis=0, concat_axis=0, tiled=True)]
    ppermute x0 -> x26, waiting for transfers between devices: none -> 66.2 us  [the longest x18 48.5 us: hop(): return lax.ppermute(value, 'wide', [(i, i ^ bit) for i in range(wide)])]
    reduce_scatter x1 -> x0, waiting for transfers between devices: 49.8 us -> none  [local(): lax.psum_scatter(partial_value, 'narrow', scatter_dimension=1, tiled=True)]
    all_to_all x1 -> x0, waiting for transfers between devices: 36.3 us -> none  [local(): lax.all_to_all(summed.astype(jnp.bfloat16), 'wide', split_axis=0, concat_...]
    ppermute x0 -> x26, starting transfers between devices: none -> 28.9 us  [the longest x18 18.4 us: hop(): return lax.ppermute(value, 'wide', [(i, i ^ bit) for i in range(wide)])]
    pallas_call x0 -> x6, Pallas kernels: none -> 22.2 us  [the longest x2 16.1 us: ffn(): kernel_call(ffn_kernel, (shape, shape), 5, 6 * 2 * n * width * ff, 6 * wi...]
    all_gather x1, blocking collectives: 10.2 us -> 28.7 us  [local(): routing = lax.all_gather(routing, 'wide', axis=0, tiled=False)]
    dot_general x3 -> x0, matrix products: 16.9 us -> none  [the longest x1 11.2 us: local(): jnp.einsum('secf,efd->secd', hidden, w_down, preferred_element_type=jnp.f...]
  transfers between devices with their start and end apart: 2 -> 26, of which waited for: 2 -> 11; matrix products, arithmetic and copies ran while one was open for 0% -> 3% of each run, Pallas kernels for 0% -> 15%
where the time goes in v1:
time: 151 us
  waiting for transfers between devices  66.2 us (44%)
  starting transfers between devices  28.9 us (19%)
  blocking collectives  28.7 us (19%)
  Pallas kernels  22.2 us (15%)
  other arithmetic  4.5 us (3%)
    ppermute x18, waiting for transfers between devices, hop(): return lax.ppermute(value, 'wide', [(i, i ^ bit) for i in range(wide)])  48.5 us
    all_gather x1, blocking collectives, local(): routing = lax.all_gather(routing, 'wide', axis=0, tiled=False)  28.7 us
    ppermute x18, starting transfers between devices, hop(): return lax.ppermute(value, 'wide', [(i, i ^ bit) for i in range(wide)])  18.4 us
    ppermute x8, waiting for transfers between devices, hop_x(): return lax.ppermute(value, 'narrow', [(0, 1), (1, 0)])  17.7 us
    pallas_call x2, Pallas kernels, ffn(): kernel_call(ffn_kernel, (shape, shape), 5, 6 * 2 * n * width * ff, 6 * wi...  16.1 us
    ppermute x8, starting transfers between devices, hop_x(): return lax.ppermute(value, 'narrow', [(0, 1), (1, 0)])  10.4 us
    pallas_call x2, Pallas kernels, combine(): kernel_call(functools.partial(combine_kernel, capacity, dz_list), (shape,...  3.21 us
  transfers between devices with their start and end apart: 26, of which 11 were waited for; matrix products, arithmetic and copies ran while one was open for 3% of the time, Pallas kernels for 15%

profile of v1, /device:TPU:0, one launch (start us, length us, event | category | flops | bytes accessed | tf_op | source)
XLA Modules:
  0.0 151.0 jit_solution(15581908325186913905)
XLA Ops:
  0.0 4.0 %collective-permute-start.12 = (bf16[128,1024]{1,0:T(8,128)(2,1)}, bf16[128,1024]{1,0:T(8,128)(2,1)S(1)}, u32[]{:S(2)}, u32[]{:S(2)}) collective-permute-start(bf16[128,1024]{1,0:T(8,128)(2,1)} %refs_0_.1), channel_id=1, source_target_pairs={{0,16},{2,18},{4,20},{6,22},{8,24},{10,26},{12,28},{14,30},{16,0},... | collective-permute-start | bytes 786440 | tf_op jit(solution)/shard_map/ppermute | solution.py:216
  4.0 1.6 %collective-permute-start.2 = (bf16[128,1024]{1,0:T(8,128)(2,1)}, bf16[128,1024]{1,0:T(8,128)(2,1)S(1)}, u32[]{:S(2)}, u32[]{:S(2)}) collective-permute-start(bf16[128,1024]{1,0:T(8,128)(2,1)} %refs_0_.1), channel_id=1, source_target_pairs={{0,8},{2,10},{4,12},{6,14},{8,0},{10,2},{12,4},{14,6},{16,24},{18,... | collective-permute-start | bytes 786440 | tf_op jit(solution)/shard_map/ppermute | solution.py:216
  5.6 1.5 collective-permute-start
  7.8 8.5 %collective-permute-done.12.refs_0_ = bf16[128,1024]{1,0:T(8,128)(2,1)S(1)} collective-permute-done((bf16[128,1024]{1,0:T(8,128)(2,1)}, bf16[128,1024]{1,0:T(8,128)(2,1)S(1)}, u32[]{:S(2)}, u32[]{:S(2)}) %collective-permute-start.12) | collective-permute-done | bytes 262176 | tf_op jit(solution)/shard_map/ppermute | solution.py:216
  17.0 1.5 %collective-permute-start.3 = (bf16[128,1024]{1,0:T(8,128)(2,1)S(1)}, bf16[128,1024]{1,0:T(8,128)(2,1)S(1)}, u32[]{:S(2)}, u32[]{:S(2)}) collective-permute-start(bf16[128,1024]{1,0:T(8,128)(2,1)S(1)} %collective-permute-done.2.refs_4_), channel_id=1, source_target_pairs={{0,4},{2,6},{4,0},{6,2},{8,12},{10,14},{12,8},{14,10},{16,20},{18,... | collective-permute-start | bytes 786440 | tf_op jit(solution)/shard_map/ppermute | solution.py:216
  19.2 1.0 pad_maximum_fusion
  20.8 1.5 collective-permute-start.13
  22.4 1.3 collective-permute-done.15.refs_4_
  23.7 1.3 collective-permute-start.16
  25.0 1.2 collective-permute-done.3.refs_6_
  26.3 1.6 %collective-permute-start.4 = (bf16[2,128,1024]{2,1,0:T(8,128)(2,1)S(1)}, bf16[2,128,1024]{2,1,0:T(8,128)(2,1)S(1)}, u32[]{:S(2)}, u32[]{:S(2)}) collective-permute-start(bf16[2,128,1024]{2,1,0:T(8,128)(2,1)S(1)} %pad_maximum_fusion.1), channel_id=1, source_target_pairs={{0,1},{1,0},{2,3},{3,2},{4,5},{5,4},{6,7},{7,6},{8,9},{9,8},{10,11... | collective-permute-start | bytes 1572872 | tf_op jit(solution)/shard_map/ppermute | solution.py:219
  27.8 28.7 %all-gather = f32[256,128]{1,0:T(8,128)S(1)} all-gather(f32[16,128]{1,0:T(8,128)S(1)} %select_reduce_fusion), channel_id=2, replica_groups=mesh['wide'=16,'narrow'=2] {'wide'}, dimensions={0}, use_global_device_ids=true | all-gather | bytes 139264 | tf_op jit(solution)/shard_map/all_gather | solution.py:226
  56.8 1.6 %collective-permute-start.17 = (bf16[2,128,1024]{2,1,0:T(8,128)(2,1)S(1)}, bf16[2,128,1024]{2,1,0:T(8,128)(2,1)S(1)}, u32[]{:S(2)}, u32[]{:S(2)}) collective-permute-start(bf16[2,128,1024]{2,1,0:T(8,128)(2,1)S(1)} %pad_maximum_fusion.3), channel_id=1, source_target_pairs={{0,1},{1,0},{2,3},{3,2},{4,5},{5,4},{6,7},{7,6},{8,9},{9,8},{10,11... | collective-permute-start | bytes 1572872 | tf_op jit(solution)/shard_map/ppermute | solution.py:219
  58.4 1.4 shard_map.64
  60.0 10.8 %collective-permute-done.14 = bf16[2,128,1024]{2,1,0:T(8,128)(2,1)S(1)} collective-permute-done((bf16[2,128,1024]{2,1,0:T(8,128)(2,1)S(1)}, bf16[2,128,1024]{2,1,0:T(8,128)(2,1)S(1)}, u32[]{:S(2)}, u32[]{:S(2)}) %collective-permute-start.14) | collective-permute-done | bytes 524320 | tf_op jit(solution)/shard_map/ppermute | solution.py:216
  71.0 1.5 shard_map.67
  72.6 8.0 %shard_map.65 = (bf16[224,2048]{1,0:T(8,128)(2,1)S(1)}, bf16[224,2048]{1,0:T(8,128)(2,1)S(1)}) custom-call(s32[2]{0:T(128)S(1)} %pad_add_fusion.place_ref, bf16[224,2048]{1,0:T(8,128)(2,1)S(1)} %get-tuple-element.21.own_ref, bf16[224,2048]{1,0:T(8,128)(2,1)S(1)} %collective-permute-done.5.other_ref, bf16[1,704,2048]{2,1,0:T(8,128)(2,1)} %gate_ref.3, ...), custom_call_target="tpu_custom_call" | custom-call | flops 3875536896 | bytes 12320768 | tf_op jit(solution)/shard_map/pallas_call | solution.py:163
  81.2 8.0 %shard_map.68 = (bf16[224,2048]{1,0:T(8,128)(2,1)S(1)}, bf16[224,2048]{1,0:T(8,128)(2,1)S(1)}) custom-call(s32[2]{0:T(128)S(1)} %pad_add_fusion.place_ref, bf16[224,2048]{1,0:T(8,128)(2,1)S(1)} %get-tuple-element.29.own_ref, bf16[224,2048]{1,0:T(8,128)(2,1)S(1)} %collective-permute-done.18.other_ref, bf16[1,704,2048]{2,1,0:T(8,128)(2,1)} %gate_ref.3, ...), custom_call_target="tpu_custom_call" | custom-call | flops 3875536896 | bytes 12320768 | tf_op jit(solution)/shard_map/pallas_call | solution.py:163
  89.3 1.6 %shard_map.66 = (bf16[2,128,1024]{2,1,0:T(8,128)(2,1)S(1)}, bf16[2,128,1024]{2,1,0:T(8,128)(2,1)S(1)}, bf16[2,128,1024]{2,1,0:T(8,128)(2,1)S(1)}, bf16[2,128,1024]{2,1,0:T(8,128)(2,1)S(1)}) custom-call(s32[2]{0:T(128)S(1)} %pad_add_fusion.place_ref, f32[16,16,128]{2,1,0:T(8,128)S(1)} %bitcast.60, bf16[224,2048]{1,0:T(8,128)(2,1)S(1)} %get-tuple-element.23.own_ref, ...), custom_call_target="tpu_custom_call" | custom-call | flops 469762048 | bytes 4194304 | tf_op jit(solution)/shard_map/pallas_call | solution.py:199
  90.9 1.6 %collective-permute-start.9 = (bf16[2,128,1024]{2,1,0:T(8,128)(2,1)S(1)}, bf16[2,128,1024]{2,1,0:T(8,128)(2,1)S(1)}, u32[]{:S(2)}, u32[]{:S(2)}) collective-permute-start(bf16[2,128,1024]{2,1,0:T(8,128)(2,1)S(1)} %get-tuple-element.28), channel_id=1, source_target_pairs={{0,1},{1,0},{2,3},{3,2},{4,5},{5,4},{6,7},{7,6},{8,9},{9,8},{10,11... | collective-permute-start | bytes 1572872 | tf_op jit(solution)/shard_map/ppermute | solution.py:219
  92.5 1.7 %collective-permute-start.7 = (bf16[2,128,1024]{2,1,0:T(8,128)(2,1)S(1)}, bf16[2,128,1024]{2,1,0:T(8,128)(2,1)S(1)}, u32[]{:S(2)}, u32[]{:S(2)}) collective-permute-start(bf16[2,128,1024]{2,1,0:T(8,128)(2,1)S(1)} %get-tuple-element.26), channel_id=1, source_target_pairs={{0,4},{2,6},{4,0},{6,2},{8,12},{10,14},{12,8},{14,10},{16,20},{18,... | collective-permute-start | bytes 1572872 | tf_op jit(solution)/shard_map/ppermute | solution.py:216
  94.2 1.6 %shard_map.69 = (bf16[2,128,1024]{2,1,0:T(8,128)(2,1)S(1)}, bf16[2,128,1024]{2,1,0:T(8,128)(2,1)S(1)}, bf16[2,128,1024]{2,1,0:T(8,128)(2,1)S(1)}, bf16[2,128,1024]{2,1,0:T(8,128)(2,1)S(1)}) custom-call(s32[2]{0:T(128)S(1)} %pad_add_fusion.place_ref, f32[16,16,128]{2,1,0:T(8,128)S(1)} %bitcast.61, bf16[224,2048]{1,0:T(8,128)(2,1)S(1)} %get-tuple-element.31.own_ref, ...), custom_call_target="tpu_custom_call" | custom-call | flops 469762048 | bytes 4194304 | tf_op jit(solution)/shard_map/pallas_call | solution.py:199
  96.7 9.0 %collective-permute-done.9 = bf16[2,128,1024]{2,1,0:T(8,128)(2,1)S(1)} collective-permute-done((bf16[2,128,1024]{2,1,0:T(8,128)(2,1)S(1)}, bf16[2,128,1024]{2,1,0:T(8,128)(2,1)S(1)}, u32[]{:S(2)}, u32[]{:S(2)}) %collective-permute-start.9) | collective-permute-done | bytes 524320 | tf_op jit(solution)/shard_map/ppermute | solution.py:219
  105.9 1.8 %collective-permute-start.10 = (bf16[128,1024]{1,0:T(8,128)(2,1)S(1)}, bf16[128,1024]{1,0:T(8,128)(2,1)S(1)}, u32[]{:S(2)}, u32[]{:S(2)}) collective-permute-start(bf16[128,1024]{1,0:T(8,128)(2,1)S(1)} %slice_bitcast_fusion.8), channel_id=1, source_target_pairs={{0,4},{2,6},{4,0},{6,2},{8,12},{10,14},{12,8},{14,10},{16,20},{18,... | collective-permute-start | bytes 786440 | tf_op jit(solution)/shard_map/ppermute | solution.py:216
  107.9 8.6 %collective-permute-done.22 = bf16[2,128,1024]{2,1,0:T(8,128)(2,1)S(1)} collective-permute-done((bf16[2,128,1024]{2,1,0:T(8,128)(2,1)S(1)}, bf16[2,128,1024]{2,1,0:T(8,128)(2,1)S(1)}, u32[]{:S(2)}, u32[]{:S(2)}) %collective-permute-start.22) | collective-permute-done | bytes 524320 | tf_op jit(solution)/shard_map/ppermute | solution.py:219
  116.7 1.8 %collective-permute-start.23 = (bf16[128,1024]{1,0:T(8,128)(2,1)S(1)}, bf16[128,1024]{1,0:T(8,128)(2,1)S(1)}, u32[]{:S(2)}, u32[]{:S(2)}) collective-permute-start(bf16[128,1024]{1,0:T(8,128)(2,1)S(1)} %slice_bitcast_fusion), channel_id=1, source_target_pairs={{0,4},{2,6},{4,0},{6,2},{8,12},{10,14},{12,8},{14,10},{16,20},{18,... | collective-permute-start | bytes 786440 | tf_op jit(solution)/shard_map/ppermute | solution.py:216
  118.8 1.6 %collective-permute-start.21 = (bf16[128,1024]{1,0:T(8,128)(2,1)S(1)}, bf16[128,1024]{1,0:T(8,128)(2,1)S(1)}, u32[]{:S(2)}, u32[]{:S(2)}) collective-permute-start(bf16[128,1024]{1,0:T(8,128)(2,1)S(1)} %slice_bitcast_fusion.2), channel_id=1, source_target_pairs={{0,1},{1,0},{2,3},{3,2},{4,5},{5,4},{6,7},{7,6},{8,9},{9,8},{10,11... | collective-permute-start | bytes 786440 | tf_op jit(solution)/shard_map/ppermute | solution.py:219
  120.3 8.6 %collective-permute-done.23 = bf16[128,1024]{1,0:T(8,128)(2,1)S(1)} collective-permute-done((bf16[128,1024]{1,0:T(8,128)(2,1)S(1)}, bf16[128,1024]{1,0:T(8,128)(2,1)S(1)}, u32[]{:S(2)}, u32[]{:S(2)}) %collective-permute-start.23) | collective-permute-done | bytes 262176 | tf_op jit(solution)/shard_map/ppermute | solution.py:216
  129.8 2.1 %collective-permute-start.11 = (bf16[128,1024]{1,0:T(8,128)(2,1)S(1)}, bf16[128,1024]{1,0:T(8,128)(2,1)S(1)}, u32[]{:S(2)}, u32[]{:S(2)}) collective-permute-start(bf16[128,1024]{1,0:T(8,128)(2,1)S(1)} %fusion.2), channel_id=1, source_target_pairs={{0,8},{2,10},{4,12},{6,14},{8,0},{10,2},{12,4},{14,6},{16,24},{18,... | collective-permute-start | bytes 786440 | tf_op jit(solution)/shard_map/ppermute | solution.py:216
  131.9 6.4 %collective-permute-done.24 = bf16[128,1024]{1,0:T(8,128)(2,1)S(1)} collective-permute-done((bf16[128,1024]{1,0:T(8,128)(2,1)S(1)}, bf16[128,1024]{1,0:T(8,128)(2,1)S(1)}, u32[]{:S(2)}, u32[]{:S(2)}) %collective-permute-start.24) | collective-permute-done | bytes 262176 | tf_op jit(solution)/shard_map/ppermute | solution.py:216
  138.6 6.1 %collective-permute-done.11 = bf16[128,1024]{1,0:T(8,128)(2,1)S(1)} collective-permute-done((bf16[128,1024]{1,0:T(8,128)(2,1)S(1)}, bf16[128,1024]{1,0:T(8,128)(2,1)S(1)}, u32[]{:S(2)}, u32[]{:S(2)}) %collective-permute-start.11) | collective-permute-done | bytes 262176 | tf_op jit(solution)/shard_map/ppermute | solution.py:216
  144.6 5.5 %collective-permute-done.25 = bf16[128,1024]{1,0:T(8,128)(2,1)S(1)} collective-permute-done((bf16[128,1024]{1,0:T(8,128)(2,1)S(1)}, bf16[128,1024]{1,0:T(8,128)(2,1)S(1)}, u32[]{:S(2)}, u32[]{:S(2)}) %collective-permute-start.25) | collective-permute-done | bytes 262176 | tf_op jit(solution)/shard_map/ppermute | solution.py:216
  (52 shorter events, 7.7 us)
Async XLA Ops:
  0.0 16.3 %collective-permute-start.12 = (bf16[128,1024]{1,0:T(8,128)(2,1)}, bf16[128,1024]{1,0:T(8,128)(2,1)S(1)}, u32[]{:S(2)}, u32[]{:S(2)}) collective-permute-start(bf16[128,1024]{1,0:T(8,128)(2,1)} %refs_0_.1), channel_id=1, source_target_pairs={{0,16},{2,18},{4,20},{6,22},{8,24},{10,26},{12,28},{14,30},{16,0},... | collective-permute-start | bytes 786440 | tf_op jit(solution)/shard_map/ppermute | solution.py:216
  4.0 13.0 %collective-permute-start.2 = (bf16[128,1024]{1,0:T(8,128)(2,1)}, bf16[128,1024]{1,0:T(8,128)(2,1)S(1)}, u32[]{:S(2)}, u32[]{:S(2)}) collective-permute-start(bf16[128,1024]{1,0:T(8,128)(2,1)} %refs_0_.1), channel_id=1, source_target_pairs={{0,8},{2,10},{4,12},{6,14},{8,0},{10,2},{12,4},{14,6},{16,24},{18,... | collective-permute-start | bytes 786440 | tf_op jit(solution)/shard_map/ppermute | solution.py:216
  5.6 13.6 %collective-permute-start = (bf16[128,1024]{1,0:T(8,128)(2,1)}, bf16[128,1024]{1,0:T(8,128)(2,1)S(1)}, u32[]{:S(2)}, u32[]{:S(2)}) collective-permute-start(bf16[128,1024]{1,0:T(8,128)(2,1)} %refs_0_.1), channel_id=1, source_target_pairs={{0,1},{1,0},{2,3},{3,2},{4,5},{5,4},{6,7},{7,6},{8,9},{9,8},{10,11... | collective-permute-start | bytes 786440 | tf_op jit(solution)/shard_map/ppermute | solution.py:219
  16.3 7.4 %collective-permute-start.15 = (bf16[128,1024]{1,0:T(8,128)(2,1)S(1)}, bf16[128,1024]{1,0:T(8,128)(2,1)S(1)}, u32[]{:S(2)}, u32[]{:S(2)}) collective-permute-start(bf16[128,1024]{1,0:T(8,128)(2,1)S(1)} %collective-permute-done.12.refs_0_), channel_id=1, source_target_pairs={{0,8},{2,10},{4,12},{6,14},{8,0},{10,2},{12,4},{14,6},{16,24},{18,... | collective-permute-start | bytes 786440 | tf_op jit(solution)/shard_map/ppermute | solution.py:216
  17.0 9.2 %collective-permute-start.3 = (bf16[128,1024]{1,0:T(8,128)(2,1)S(1)}, bf16[128,1024]{1,0:T(8,128)(2,1)S(1)}, u32[]{:S(2)}, u32[]{:S(2)}) collective-permute-start(bf16[128,1024]{1,0:T(8,128)(2,1)S(1)} %collective-permute-done.2.refs_4_), channel_id=1, source_target_pairs={{0,4},{2,6},{4,0},{6,2},{8,12},{10,14},{12,8},{14,10},{16,20},{18,... | collective-permute-start | bytes 786440 | tf_op jit(solution)/shard_map/ppermute | solution.py:216
  20.2 38.2 %copy-start = (bf16[128,1024]{1,0:T(8,128)(2,1)S(1)}, bf16[128,1024]{1,0:T(8,128)(2,1)}, u32[]{:S(2)}) copy-start(bf16[128,1024]{1,0:T(8,128)(2,1)} %refs_0_.1) | copy-start | bytes 786436
  20.3 38.1 %collective-permute-start.1 = (bf16[2,128,1024]{2,1,0:T(8,128)(2,1)S(1)}, bf16[2,128,1024]{2,1,0:T(8,128)(2,1)S(1)}, u32[]{:S(2)}, u32[]{:S(2)}) collective-permute-start(bf16[2,128,1024]{2,1,0:T(8,128)(2,1)S(1)} %pad_maximum_fusion), channel_id=1, source_target_pairs={{0,4},{2,6},{4,0},{6,2},{8,12},{10,14},{12,8},{14,10},{16,20},{18,... | collective-permute-start | bytes 1572872 | tf_op jit(solution)/shard_map/ppermute | solution.py:216
  20.8 35.7 %collective-permute-start.13 = (bf16[128,1024]{1,0:T(8,128)(2,1)S(1)}, bf16[128,1024]{1,0:T(8,128)(2,1)S(1)}, u32[]{:S(2)}, u32[]{:S(2)}) collective-permute-start(bf16[128,1024]{1,0:T(8,128)(2,1)S(1)} %collective-permute-done.12.refs_0_), channel_id=1, source_target_pairs={{0,1},{1,0},{2,3},{3,2},{4,5},{5,4},{6,7},{7,6},{8,9},{9,8},{10,11... | collective-permute-start | bytes 786440 | tf_op jit(solution)/shard_map/ppermute | solution.py:219
  23.7 33.0 %collective-permute-start.16 = (bf16[128,1024]{1,0:T(8,128)(2,1)S(1)}, bf16[128,1024]{1,0:T(8,128)(2,1)S(1)}, u32[]{:S(2)}, u32[]{:S(2)}) collective-permute-start(bf16[128,1024]{1,0:T(8,128)(2,1)S(1)} %collective-permute-done.15.refs_4_), channel_id=1, source_target_pairs={{0,4},{2,6},{4,0},{6,2},{8,12},{10,14},{12,8},{14,10},{16,20},{18,... | collective-permute-start | bytes 786440 | tf_op jit(solution)/shard_map/ppermute | solution.py:216
  26.3 32.1 %collective-permute-start.4 = (bf16[2,128,1024]{2,1,0:T(8,128)(2,1)S(1)}, bf16[2,128,1024]{2,1,0:T(8,128)(2,1)S(1)}, u32[]{:S(2)}, u32[]{:S(2)}) collective-permute-start(bf16[2,128,1024]{2,1,0:T(8,128)(2,1)S(1)} %pad_maximum_fusion.1), channel_id=1, source_target_pairs={{0,1},{1,0},{2,3},{3,2},{4,5},{5,4},{6,7},{7,6},{8,9},{9,8},{10,11... | collective-permute-start | bytes 1572872 | tf_op jit(solution)/shard_map/ppermute | solution.py:219
  56.6 14.2 %collective-permute-start.14 = (bf16[2,128,1024]{2,1,0:T(8,128)(2,1)S(1)}, bf16[2,128,1024]{2,1,0:T(8,128)(2,1)S(1)}, u32[]{:S(2)}, u32[]{:S(2)}) collective-permute-start(bf16[2,128,1024]{2,1,0:T(8,128)(2,1)S(1)} %pad_maximum_fusion.2), channel_id=1, source_target_pairs={{0,4},{2,6},{4,0},{6,2},{8,12},{10,14},{12,8},{14,10},{16,20},{18,... | collective-permute-start | bytes 1572872 | tf_op jit(solution)/shard_map/ppermute | solution.py:216
  56.8 14.2 %collective-permute-start.17 = (bf16[2,128,1024]{2,1,0:T(8,128)(2,1)S(1)}, bf16[2,128,1024]{2,1,0:T(8,128)(2,1)S(1)}, u32[]{:S(2)}, u32[]{:S(2)}) collective-permute-start(bf16[2,128,1024]{2,1,0:T(8,128)(2,1)S(1)} %pad_maximum_fusion.3), channel_id=1, source_target_pairs={{0,1},{1,0},{2,3},{3,2},{4,5},{5,4},{6,7},{7,6},{8,9},{9,8},{10,11... | collective-permute-start | bytes 1572872 | tf_op jit(solution)/shard_map/ppermute | solution.py:219
  59.9 12.7 %collective-permute-start.5 = (bf16[224,2048]{1,0:T(8,128)(2,1)S(1)}, bf16[224,2048]{1,0:T(8,128)(2,1)S(1)}, u32[]{:S(2)}, u32[]{:S(2)}) collective-permute-start(bf16[224,2048]{1,0:T(8,128)(2,1)S(1)} %get-tuple-element.22), channel_id=1, source_target_pairs={{0,2},{2,0},{4,6},{6,4},{8,10},{10,8},{12,14},{14,12},{16,18},{18,... | collective-permute-start | bytes 2752520 | tf_op jit(solution)/shard_map/ppermute | solution.py:216
  72.5 8.7 %collective-permute-start.18 = (bf16[224,2048]{1,0:T(8,128)(2,1)S(1)}, bf16[224,2048]{1,0:T(8,128)(2,1)S(1)}, u32[]{:S(2)}, u32[]{:S(2)}) collective-permute-start(bf16[224,2048]{1,0:T(8,128)(2,1)S(1)} %get-tuple-element.30), channel_id=1, source_target_pairs={{0,2},{2,0},{4,6},{6,4},{8,10},{10,8},{12,14},{14,12},{16,18},{18,... | collective-permute-start | bytes 2752520 | tf_op jit(solution)/shard_map/ppermute | solution.py:216
  80.6 8.7 %collective-permute-start.6 = (bf16[224,2048]{1,0:T(8,128)(2,1)S(1)}, bf16[224,2048]{1,0:T(8,128)(2,1)S(1)}, u32[]{:S(2)}, u32[]{:S(2)}) collective-permute-start(bf16[224,2048]{1,0:T(8,128)(2,1)S(1)} %get-tuple-element.24), channel_id=1, source_target_pairs={{0,2},{2,0},{4,6},{6,4},{8,10},{10,8},{12,14},{14,12},{16,18},{18,... | collective-permute-start | bytes 2752520 | tf_op jit(solution)/shard_map/ppermute | solution.py:216
  89.2 5.0 %collective-permute-start.19 = (bf16[224,2048]{1,0:T(8,128)(2,1)S(1)}, bf16[224,2048]{1,0:T(8,128)(2,1)S(1)}, u32[]{:S(2)}, u32[]{:S(2)}) collective-permute-start(bf16[224,2048]{1,0:T(8,128)(2,1)S(1)} %get-tuple-element.32), channel_id=1, source_target_pairs={{0,2},{2,0},{4,6},{6,4},{8,10},{10,8},{12,14},{14,12},{16,18},{18,... | collective-permute-start | bytes 2752520 | tf_op jit(solution)/shard_map/ppermute | solution.py:216
  90.9 14.8 %collective-permute-start.9 = (bf16[2,128,1024]{2,1,0:T(8,128)(2,1)S(1)}, bf16[2,128,1024]{2,1,0:T(8,128)(2,1)S(1)}, u32[]{:S(2)}, u32[]{:S(2)}) collective-permute-start(bf16[2,128,1024]{2,1,0:T(8,128)(2,1)S(1)} %get-tuple-element.28), channel_id=1, source_target_pairs={{0,1},{1,0},{2,3},{3,2},{4,5},{5,4},{6,7},{7,6},{8,9},{9,8},{10,11... | collective-permute-start | bytes 1572872 | tf_op jit(solution)/shard_map/ppermute | solution.py:219
  92.5 15.3 %collective-permute-start.7 = (bf16[2,128,1024]{2,1,0:T(8,128)(2,1)S(1)}, bf16[2,128,1024]{2,1,0:T(8,128)(2,1)S(1)}, u32[]{:S(2)}, u32[]{:S(2)}) collective-permute-start(bf16[2,128,1024]{2,1,0:T(8,128)(2,1)S(1)} %get-tuple-element.26), channel_id=1, source_target_pairs={{0,4},{2,6},{4,0},{6,2},{8,12},{10,14},{12,8},{14,10},{16,20},{18,... | collective-permute-start | bytes 1572872 | tf_op jit(solution)/shard_map/ppermute | solution.py:216
  95.8 20.7 %collective-permute-start.22 = (bf16[2,128,1024]{2,1,0:T(8,128)(2,1)S(1)}, bf16[2,128,1024]{2,1,0:T(8,128)(2,1)S(1)}, u32[]{:S(2)}, u32[]{:S(2)}) collective-permute-start(bf16[2,128,1024]{2,1,0:T(8,128)(2,1)S(1)} %get-tuple-element.36), channel_id=1, source_target_pairs={{0,1},{1,0},{2,3},{3,2},{4,5},{5,4},{6,7},{7,6},{8,9},{9,8},{10,11... | collective-permute-start | bytes 1572872 | tf_op jit(solution)/shard_map/ppermute | solution.py:219
  96.4 22.1 %collective-permute-start.20 = (bf16[2,128,1024]{2,1,0:T(8,128)(2,1)S(1)}, bf16[2,128,1024]{2,1,0:T(8,128)(2,1)S(1)}, u32[]{:S(2)}, u32[]{:S(2)}) collective-permute-start(bf16[2,128,1024]{2,1,0:T(8,128)(2,1)S(1)} %get-tuple-element.34), channel_id=1, source_target_pairs={{0,4},{2,6},{4,0},{6,2},{8,12},{10,14},{12,8},{14,10},{16,20},{18,... | collective-permute-start | bytes 1572872 | tf_op jit(solution)/shard_map/ppermute | solution.py:216
  105.9 23.8 %collective-permute-start.10 = (bf16[128,1024]{1,0:T(8,128)(2,1)S(1)}, bf16[128,1024]{1,0:T(8,128)(2,1)S(1)}, u32[]{:S(2)}, u32[]{:S(2)}) collective-permute-start(bf16[128,1024]{1,0:T(8,128)(2,1)S(1)} %slice_bitcast_fusion.8), channel_id=1, source_target_pairs={{0,4},{2,6},{4,0},{6,2},{8,12},{10,14},{12,8},{14,10},{16,20},{18,... | collective-permute-start | bytes 786440 | tf_op jit(solution)/shard_map/ppermute | solution.py:216
  116.7 12.2 %collective-permute-start.23 = (bf16[128,1024]{1,0:T(8,128)(2,1)S(1)}, bf16[128,1024]{1,0:T(8,128)(2,1)S(1)}, u32[]{:S(2)}, u32[]{:S(2)}) collective-permute-start(bf16[128,1024]{1,0:T(8,128)(2,1)S(1)} %slice_bitcast_fusion), channel_id=1, source_target_pairs={{0,4},{2,6},{4,0},{6,2},{8,12},{10,14},{12,8},{14,10},{16,20},{18,... | collective-permute-start | bytes 786440 | tf_op jit(solution)/shard_map/ppermute | solution.py:216
  118.8 13.1 %collective-permute-start.21 = (bf16[128,1024]{1,0:T(8,128)(2,1)S(1)}, bf16[128,1024]{1,0:T(8,128)(2,1)S(1)}, u32[]{:S(2)}, u32[]{:S(2)}) collective-permute-start(bf16[128,1024]{1,0:T(8,128)(2,1)S(1)} %slice_bitcast_fusion.2), channel_id=1, source_target_pairs={{0,1},{1,0},{2,3},{3,2},{4,5},{5,4},{6,7},{7,6},{8,9},{9,8},{10,11... | collective-permute-start | bytes 786440 | tf_op jit(solution)/shard_map/ppermute | solution.py:219
  129.0 9.3 %collective-permute-start.24 = (bf16[128,1024]{1,0:T(8,128)(2,1)S(1)}, bf16[128,1024]{1,0:T(8,128)(2,1)S(1)}, u32[]{:S(2)}, u32[]{:S(2)}) collective-permute-start(bf16[128,1024]{1,0:T(8,128)(2,1)S(1)} %fusion), channel_id=1, source_target_pairs={{0,8},{2,10},{4,12},{6,14},{8,0},{10,2},{12,4},{14,6},{16,24},{18,... | collective-permute-start | bytes 786440 | tf_op jit(solution)/shard_map/ppermute | solution.py:216
  129.1 9.4 %collective-permute-start.8 = (bf16[128,1024]{1,0:T(8,128)(2,1)S(1)}, bf16[128,1024]{1,0:T(8,128)(2,1)S(1)}, u32[]{:S(2)}, u32[]{:S(2)}) collective-permute-start(bf16[128,1024]{1,0:T(8,128)(2,1)S(1)} %slice_bitcast_fusion.10), channel_id=1, source_target_pairs={{0,1},{1,0},{2,3},{3,2},{4,5},{5,4},{6,7},{7,6},{8,9},{9,8},{10,11... | collective-permute-start | bytes 786440 | tf_op jit(solution)/shard_map/ppermute | solution.py:219
  129.8 14.8 %collective-permute-start.11 = (bf16[128,1024]{1,0:T(8,128)(2,1)S(1)}, bf16[128,1024]{1,0:T(8,128)(2,1)S(1)}, u32[]{:S(2)}, u32[]{:S(2)}) collective-permute-start(bf16[128,1024]{1,0:T(8,128)(2,1)S(1)} %fusion.2), channel_id=1, source_target_pairs={{0,8},{2,10},{4,12},{6,14},{8,0},{10,2},{12,4},{14,6},{16,24},{18,... | collective-permute-start | bytes 786440 | tf_op jit(solution)/shard_map/ppermute | solution.py:216
  138.5 11.6 %collective-permute-start.25 = (bf16[128,1024]{1,0:T(8,128)(2,1)S(1)}, bf16[128,1024]{1,0:T(8,128)(2,1)S(1)}, u32[]{:S(2)}, u32[]{:S(2)}) collective-permute-start(bf16[128,1024]{1,0:T(8,128)(2,1)S(1)} %add_convert_fusion.5), channel_id=1, source_target_pairs={{0,16},{2,18},{4,20},{6,22},{8,24},{10,26},{12,28},{14,30},{16,0},... | collective-permute-start | bytes 786440 | tf_op jit(solution)/shard_map/ppermute | solution.py:216

commit v2 on v1

--- a/solution.py
+++ b/solution.py
@@ -8,7 +8,7 @@
 from jax.sharding import PartitionSpec as P
 
 CORE, Y, NEAR, FAR = 1, 2, 4, 8
-VMEM_BYTES = 48 << 20
+VMEM_BYTES = 20 << 20
 F32, BF16 = jnp.float32, jnp.bfloat16
 
 
@@ -77,8 +77,8 @@
     )
     rows = []
     for expert in (me, me ^ CORE):
-        for block in (me ^ (NEAR * dz), me ^ (NEAR * dz + Y)):
-            rows.append(routing_ref[block, pl.ds(expert, 1), :])
+        for dy in (0, 1):
+            rows.append(routing_ref[2 * dz + dy, pl.ds(expert, 1), :])
     weight = jnp.concatenate(rows, axis=0)
     chosen = weight > 0
     count = jnp.dot(
@@ -223,7 +223,9 @@
 
     named = expert_ids.T[:, None, :] == jnp.arange(wide, dtype=jnp.int32)[None, :, None]
     routing = jnp.sum(jnp.where(named, route_weights.astype(F32).T[:, None, :], 0.0), axis=0)
-    routing = lax.all_gather(routing, "wide", axis=0, tiled=False)
+    routing = jnp.stack([routing, hop(routing, Y)])
+    routing = jnp.concatenate([routing, hop(routing, NEAR)])
+    routing = jnp.concatenate([routing, hop(routing, FAR)])
 
     column = [tokens, hop(tokens, NEAR), hop(tokens, FAR), None]
     column[3] = hop(column[2], NEAR)

time: 151 us -> 131 us (0.87)
  blocking collectives: 28.7 us -> 0 us
  starting transfers between devices: 28.9 us -> 36.7 us
  waiting for transfers between devices: 66.2 us -> 72.4 us
  Pallas kernels: 22.2 us -> 16.2 us
    all_gather x1 -> x0, blocking collectives: 28.7 us -> none  [local(): routing = lax.all_gather(routing, 'wide', axis=0, tiled=False)]
    ppermute x18 -> x21, starting transfers between devices: 18.4 us -> 27.3 us  [hop(): return lax.ppermute(value, 'wide', [(i, i ^ bit) for i in range(wide)])]
    pallas_call x2, Pallas kernels: 16.1 us -> 10.1 us  [ffn(): kernel_call(ffn_kernel, (shape, shape), 5, 6 * 2 * n * width * ff, 6 * wi...]
    ppermute x18 -> x21, waiting for transfers between devices: 48.5 us -> 53.3 us  [hop(): return lax.ppermute(value, 'wide', [(i, i ^ bit) for i in range(wide)])]
  transfers between devices with their start and end apart: 26 -> 29, of which waited for: 11 -> 13; matrix products, arithmetic and copies ran while one was open for 3% -> 3% of each run, Pallas kernels for 15% -> 12%
where the time goes in v2:
time: 131 us; the launch traced here: 130 us
  waiting for transfers between devices  72.4 us (55%)
  starting transfers between devices  36.7 us (28%)
  Pallas kernels  16.2 us (12%)
  other arithmetic  4.51 us (3%)
    ppermute x21, waiting for transfers between devices, hop(): return lax.ppermute(value, 'wide', [(i, i ^ bit) for i in range(wide)])  53.3 us
    ppermute x21, starting transfers between devices, hop(): return lax.ppermute(value, 'wide', [(i, i ^ bit) for i in range(wide)])  27.3 us
    ppermute x8, waiting for transfers between devices, hop_x(): return lax.ppermute(value, 'narrow', [(0, 1), (1, 0)])  19 us
    pallas_call x2, Pallas kernels, ffn(): kernel_call(ffn_kernel, (shape, shape), 5, 6 * 2 * n * width * ff, 6 * wi...  10.1 us
    ppermute x8, starting transfers between devices, hop_x(): return lax.ppermute(value, 'narrow', [(0, 1), (1, 0)])  9.4 us
    pallas_call x2, Pallas kernels, combine(): kernel_call(functools.partial(combine_kernel, capacity, dz_list), (shape,...  3.21 us
    pallas_call x2, Pallas kernels, dispatch(): kernel_call(functools.partial(dispatch_kernel, capacity, dz_list), (shape...  2.9 us
  transfers between devices with their start and end apart: 29, of which 13 were waited for; matrix products, arithmetic and copies ran while one was open for 3% of the time, Pallas kernels for 12%

profile of v2, /device:TPU:0, one launch (start us, length us, event | category | flops | bytes accessed | tf_op | source)
XLA Modules:
  0.0 130.3 jit_solution(8866062714076253442)
XLA Ops:
  0.0 4.0 %collective-permute-start.15 = (bf16[128,1024]{1,0:T(8,128)(2,1)}, bf16[128,1024]{1,0:T(8,128)(2,1)S(1)}, u32[]{:S(2)}, u32[]{:S(2)}) collective-permute-start(bf16[128,1024]{1,0:T(8,128)(2,1)} %refs_0_.1), channel_id=1, source_target_pairs={{0,16},{2,18},{4,20},{6,22},{8,24},{10,26},{12,28},{14,30},{16,0},... | collective-permute-start | bytes 786440 | tf_op jit(solution)/shard_map/ppermute | solution.py:216
  4.0 1.5 %collective-permute-start.3 = (bf16[128,1024]{1,0:T(8,128)(2,1)}, bf16[128,1024]{1,0:T(8,128)(2,1)S(1)}, u32[]{:S(2)}, u32[]{:S(2)}) collective-permute-start(bf16[128,1024]{1,0:T(8,128)(2,1)} %refs_0_.1), channel_id=1, source_target_pairs={{0,1},{1,0},{2,3},{3,2},{4,5},{5,4},{6,7},{7,6},{8,9},{9,8},{10,11... | collective-permute-start | bytes 786440 | tf_op jit(solution)/shard_map/ppermute | solution.py:219
  5.5 1.6 %collective-permute-start.5 = (bf16[128,1024]{1,0:T(8,128)(2,1)}, bf16[128,1024]{1,0:T(8,128)(2,1)S(1)}, u32[]{:S(2)}, u32[]{:S(2)}) collective-permute-start(bf16[128,1024]{1,0:T(8,128)(2,1)} %refs_0_.1), channel_id=1, source_target_pairs={{0,8},{2,10},{4,12},{6,14},{8,0},{10,2},{12,4},{14,6},{16,24},{18,... | collective-permute-start | bytes 786440 | tf_op jit(solution)/shard_map/ppermute | solution.py:216
  8.5 1.6 %collective-permute-start = (f32[16,128]{1,0:T(8,128)S(1)}, f32[16,128]{1,0:T(8,128)S(1)}, u32[]{:S(2)}, u32[]{:S(2)}) collective-permute-start(f32[16,128]{1,0:T(8,128)S(1)} %select_reduce_fusion), channel_id=1, source_target_pairs={{0,4},{2,6},{4,0},{6,2},{8,12},{10,14},{12,8},{14,10},{16,20},{18,... | collective-permute-start | bytes 24584 | tf_op jit(solution)/shard_map/ppermute | solution.py:216
  10.1 6.1 %collective-permute-done.15.refs_0_ = bf16[128,1024]{1,0:T(8,128)(2,1)S(1)} collective-permute-done((bf16[128,1024]{1,0:T(8,128)(2,1)}, bf16[128,1024]{1,0:T(8,128)(2,1)S(1)}, u32[]{:S(2)}, u32[]{:S(2)}) %collective-permute-start.15) | collective-permute-done | bytes 262176 | tf_op jit(solution)/shard_map/ppermute | solution.py:216
  17.7 1.6 %collective-permute-start.6 = (bf16[128,1024]{1,0:T(8,128)(2,1)S(1)}, bf16[128,1024]{1,0:T(8,128)(2,1)S(1)}, u32[]{:S(2)}, u32[]{:S(2)}) collective-permute-start(bf16[128,1024]{1,0:T(8,128)(2,1)S(1)} %collective-permute-done.5.refs_4_), channel_id=1, source_target_pairs={{0,4},{2,6},{4,0},{6,2},{8,12},{10,14},{12,8},{14,10},{16,20},{18,... | collective-permute-start | bytes 786440 | tf_op jit(solution)/shard_map/ppermute | solution.py:216
  21.4 1.5 %collective-permute-start.16 = (bf16[128,1024]{1,0:T(8,128)(2,1)S(1)}, bf16[128,1024]{1,0:T(8,128)(2,1)S(1)}, u32[]{:S(2)}, u32[]{:S(2)}) collective-permute-start(bf16[128,1024]{1,0:T(8,128)(2,1)S(1)} %collective-permute-done.15.refs_0_), channel_id=1, source_target_pairs={{0,1},{1,0},{2,3},{3,2},{4,5},{5,4},{6,7},{7,6},{8,9},{9,8},{10,11... | collective-permute-start | bytes 786440 | tf_op jit(solution)/shard_map/ppermute | solution.py:219
  24.1 3.1 %collective-permute-start.2 = (f32[4,16,128]{2,1,0:T(8,128)S(1)}, f32[4,16,128]{2,1,0:T(8,128)S(1)}, u32[]{:S(2)}, u32[]{:S(2)}) collective-permute-start(f32[4,16,128]{2,1,0:T(8,128)S(1)} %pad_maximum_fusion.5), channel_id=1, source_target_pairs={{0,16},{2,18},{4,20},{6,22},{8,24},{10,26},{12,28},{14,30},{16,0},... | collective-permute-start | bytes 98312 | tf_op jit(solution)/shard_map/ppermute | solution.py:216
  27.2 1.5 %collective-permute-start.19 = (bf16[128,1024]{1,0:T(8,128)(2,1)S(1)}, bf16[128,1024]{1,0:T(8,128)(2,1)S(1)}, u32[]{:S(2)}, u32[]{:S(2)}) collective-permute-start(bf16[128,1024]{1,0:T(8,128)(2,1)S(1)} %collective-permute-done.18.refs_4_), channel_id=1, source_target_pairs={{0,4},{2,6},{4,0},{6,2},{8,12},{10,14},{12,8},{14,10},{16,20},{18,... | collective-permute-start | bytes 786440 | tf_op jit(solution)/shard_map/ppermute | solution.py:216
  28.7 1.5 %collective-permute-start.7 = (bf16[2,128,1024]{2,1,0:T(8,128)(2,1)S(1)}, bf16[2,128,1024]{2,1,0:T(8,128)(2,1)S(1)}, u32[]{:S(2)}, u32[]{:S(2)}) collective-permute-start(bf16[2,128,1024]{2,1,0:T(8,128)(2,1)S(1)} %pad_maximum_fusion.1), channel_id=1, source_target_pairs={{0,1},{1,0},{2,3},{3,2},{4,5},{5,4},{6,7},{7,6},{8,9},{9,8},{10,11... | collective-permute-start | bytes 1572872 | tf_op jit(solution)/shard_map/ppermute | solution.py:219
  30.9 12.9 %collective-permute-done.19.refs_6_ = bf16[128,1024]{1,0:T(8,128)(2,1)S(1)} collective-permute-done((bf16[128,1024]{1,0:T(8,128)(2,1)S(1)}, bf16[128,1024]{1,0:T(8,128)(2,1)S(1)}, u32[]{:S(2)}, u32[]{:S(2)}) %collective-permute-start.19) | collective-permute-done | bytes 262176 | tf_op jit(solution)/shard_map/ppermute | solution.py:216
  44.8 1.4 %shard_map.64 = (bf16[224,2048]{1,0:T(8,128)(2,1)S(1)}, bf16[224,2048]{1,0:T(8,128)(2,1)S(1)}) custom-call(s32[2]{0:T(128)S(1)} %pad_add_fusion.place_ref, f32[8,16,128]{2,1,0:T(8,128)S(1)} %pad_maximum_fusion.4.routing_ref, bf16[128,1024]{1,0:T(8,128)(2,1)S(1)} %copy-done, bf16[128,1024]{1,0:T(8,128)(2,1)S(1)} %collective-permute-done.3.refs_1_, ...), custom_call_target="tpu_custom_call" | custom-call | flops 469762048 | bytes 4194304 | tf_op jit(solution)/shard_map/pallas_call | solution.py:120
  46.3 6.7 %collective-permute-done.17 = bf16[2,128,1024]{2,1,0:T(8,128)(2,1)S(1)} collective-permute-done((bf16[2,128,1024]{2,1,0:T(8,128)(2,1)S(1)}, bf16[2,128,1024]{2,1,0:T(8,128)(2,1)S(1)}, u32[]{:S(2)}, u32[]{:S(2)}) %collective-permute-start.17) | collective-permute-done | bytes 524320 | tf_op jit(solution)/shard_map/ppermute | solution.py:216
  53.1 1.2 collective-permute-done.20
  54.4 1.5 %shard_map.67 = (bf16[224,2048]{1,0:T(8,128)(2,1)S(1)}, bf16[224,2048]{1,0:T(8,128)(2,1)S(1)}) custom-call(s32[2]{0:T(128)S(1)} %pad_add_fusion.place_ref, f32[8,16,128]{2,1,0:T(8,128)S(1)} %pad_maximum_fusion.4.routing_ref, bf16[128,1024]{1,0:T(8,128)(2,1)S(1)} %collective-permute-done.15.refs_0_, bf16[128,1024]{1,0:T(8,128)(2,1)S(1)} %collective-permute-done.16.refs_1_, ...), custom_call_target="tpu_custom_call" | custom-call | flops 469762048 | bytes 4194304 | tf_op jit(solution)/shard_map/pallas_call | solution.py:120
  56.0 5.0 %shard_map.65 = (bf16[224,2048]{1,0:T(8,128)(2,1)S(1)}, bf16[224,2048]{1,0:T(8,128)(2,1)S(1)}) custom-call(s32[2]{0:T(128)S(1)} %pad_add_fusion.place_ref, bf16[224,2048]{1,0:T(8,128)(2,1)S(1)} %get-tuple-element.21.own_ref, bf16[224,2048]{1,0:T(8,128)(2,1)S(1)} %collective-permute-done.8.other_ref, bf16[1,704,2048]{2,1,0:T(8,128)(2,1)S(1)} %copy-done.1, ...), custom_call_target="tpu_custom_call" | custom-call | flops 3875536896 | bytes 12320768 | tf_op jit(solution)/shard_map/pallas_call | solution.py:163
  61.6 5.0 %shard_map.68 = (bf16[224,2048]{1,0:T(8,128)(2,1)S(1)}, bf16[224,2048]{1,0:T(8,128)(2,1)S(1)}) custom-call(s32[2]{0:T(128)S(1)} %pad_add_fusion.place_ref, bf16[224,2048]{1,0:T(8,128)(2,1)S(1)} %get-tuple-element.29.own_ref, bf16[224,2048]{1,0:T(8,128)(2,1)S(1)} %collective-permute-done.21.other_ref, bf16[1,704,2048]{2,1,0:T(8,128)(2,1)S(1)} %copy-done.1, ...), custom_call_target="tpu_custom_call" | custom-call | flops 3875536896 | bytes 12320768 | tf_op jit(solution)/shard_map/pallas_call | solution.py:163
  66.7 1.6 %shard_map.66 = (bf16[2,128,1024]{2,1,0:T(8,128)(2,1)S(1)}, bf16[2,128,1024]{2,1,0:T(8,128)(2,1)S(1)}, bf16[2,128,1024]{2,1,0:T(8,128)(2,1)S(1)}, bf16[2,128,1024]{2,1,0:T(8,128)(2,1)S(1)}) custom-call(s32[2]{0:T(128)S(1)} %pad_add_fusion.place_ref, f32[8,16,128]{2,1,0:T(8,128)S(1)} %pad_maximum_fusion.4.routing_ref, ...), custom_call_target="tpu_custom_call" | custom-call | flops 469762048 | bytes 4194304 | tf_op jit(solution)/shard_map/pallas_call | solution.py:199
  68.3 1.8 %collective-permute-start.12 = (bf16[2,128,1024]{2,1,0:T(8,128)(2,1)S(1)}, bf16[2,128,1024]{2,1,0:T(8,128)(2,1)S(1)}, u32[]{:S(2)}, u32[]{:S(2)}) collective-permute-start(bf16[2,128,1024]{2,1,0:T(8,128)(2,1)S(1)} %get-tuple-element.28), channel_id=1, source_target_pairs={{0,1},{1,0},{2,3},{3,2},{4,5},{5,4},{6,7},{7,6},{8,9},{9,8},{10,11... | collective-permute-start | bytes 1572872 | tf_op jit(solution)/shard_map/ppermute | solution.py:219
  70.1 1.5 %collective-permute-start.10 = (bf16[2,128,1024]{2,1,0:T(8,128)(2,1)S(1)}, bf16[2,128,1024]{2,1,0:T(8,128)(2,1)S(1)}, u32[]{:S(2)}, u32[]{:S(2)}) collective-permute-start(bf16[2,128,1024]{2,1,0:T(8,128)(2,1)S(1)} %get-tuple-element.26), channel_id=1, source_target_pairs={{0,4},{2,6},{4,0},{6,2},{8,12},{10,14},{12,8},{14,10},{16,20},{18,... | collective-permute-start | bytes 1572872 | tf_op jit(solution)/shard_map/ppermute | solution.py:216
  71.7 1.6 %shard_map.69 = (bf16[2,128,1024]{2,1,0:T(8,128)(2,1)S(1)}, bf16[2,128,1024]{2,1,0:T(8,128)(2,1)S(1)}, bf16[2,128,1024]{2,1,0:T(8,128)(2,1)S(1)}, bf16[2,128,1024]{2,1,0:T(8,128)(2,1)S(1)}) custom-call(s32[2]{0:T(128)S(1)} %pad_add_fusion.place_ref, f32[8,16,128]{2,1,0:T(8,128)S(1)} %pad_maximum_fusion.4.routing_ref, ...), custom_call_target="tpu_custom_call" | custom-call | flops 469762048 | bytes 4194304 | tf_op jit(solution)/shard_map/pallas_call | solution.py:199
  74.1 9.0 %collective-permute-done.12 = bf16[2,128,1024]{2,1,0:T(8,128)(2,1)S(1)} collective-permute-done((bf16[2,128,1024]{2,1,0:T(8,128)(2,1)S(1)}, bf16[2,128,1024]{2,1,0:T(8,128)(2,1)S(1)}, u32[]{:S(2)}, u32[]{:S(2)}) %collective-permute-start.12) | collective-permute-done | bytes 524320 | tf_op jit(solution)/shard_map/ppermute | solution.py:219
  83.3 1.6 %collective-permute-start.13 = (bf16[128,1024]{1,0:T(8,128)(2,1)S(1)}, bf16[128,1024]{1,0:T(8,128)(2,1)S(1)}, u32[]{:S(2)}, u32[]{:S(2)}) collective-permute-start(bf16[128,1024]{1,0:T(8,128)(2,1)S(1)} %slice_bitcast_fusion.8), channel_id=1, source_target_pairs={{0,4},{2,6},{4,0},{6,2},{8,12},{10,14},{12,8},{14,10},{16,20},{18,... | collective-permute-start | bytes 786440 | tf_op jit(solution)/shard_map/ppermute | solution.py:216
  85.1 8.8 %collective-permute-done.25 = bf16[2,128,1024]{2,1,0:T(8,128)(2,1)S(1)} collective-permute-done((bf16[2,128,1024]{2,1,0:T(8,128)(2,1)S(1)}, bf16[2,128,1024]{2,1,0:T(8,128)(2,1)S(1)}, u32[]{:S(2)}, u32[]{:S(2)}) %collective-permute-start.25) | collective-permute-done | bytes 524320 | tf_op jit(solution)/shard_map/ppermute | solution.py:219
  94.2 1.6 %collective-permute-start.26 = (bf16[128,1024]{1,0:T(8,128)(2,1)S(1)}, bf16[128,1024]{1,0:T(8,128)(2,1)S(1)}, u32[]{:S(2)}, u32[]{:S(2)}) collective-permute-start(bf16[128,1024]{1,0:T(8,128)(2,1)S(1)} %slice_bitcast_fusion), channel_id=1, source_target_pairs={{0,4},{2,6},{4,0},{6,2},{8,12},{10,14},{12,8},{14,10},{16,20},{18,... | collective-permute-start | bytes 786440 | tf_op jit(solution)/shard_map/ppermute | solution.py:216
  96.4 1.4 %collective-permute-start.24 = (bf16[128,1024]{1,0:T(8,128)(2,1)S(1)}, bf16[128,1024]{1,0:T(8,128)(2,1)S(1)}, u32[]{:S(2)}, u32[]{:S(2)}) collective-permute-start(bf16[128,1024]{1,0:T(8,128)(2,1)S(1)} %slice_bitcast_fusion.2), channel_id=1, source_target_pairs={{0,1},{1,0},{2,3},{3,2},{4,5},{5,4},{6,7},{7,6},{8,9},{9,8},{10,11... | collective-permute-start | bytes 786440 | tf_op jit(solution)/shard_map/ppermute | solution.py:219
  97.8 8.8 %collective-permute-done.26 = bf16[128,1024]{1,0:T(8,128)(2,1)S(1)} collective-permute-done((bf16[128,1024]{1,0:T(8,128)(2,1)S(1)}, bf16[128,1024]{1,0:T(8,128)(2,1)S(1)}, u32[]{:S(2)}, u32[]{:S(2)}) %collective-permute-start.26) | collective-permute-done | bytes 262176 | tf_op jit(solution)/shard_map/ppermute | solution.py:216
  107.3 2.1 %collective-permute-start.14 = (bf16[128,1024]{1,0:T(8,128)(2,1)S(1)}, bf16[128,1024]{1,0:T(8,128)(2,1)S(1)}, u32[]{:S(2)}, u32[]{:S(2)}) collective-permute-start(bf16[128,1024]{1,0:T(8,128)(2,1)S(1)} %fusion.2), channel_id=1, source_target_pairs={{0,8},{2,10},{4,12},{6,14},{8,0},{10,2},{12,4},{14,6},{16,24},{18,... | collective-permute-start | bytes 786440 | tf_op jit(solution)/shard_map/ppermute | solution.py:216
  109.4 6.6 %collective-permute-done.27 = bf16[128,1024]{1,0:T(8,128)(2,1)S(1)} collective-permute-done((bf16[128,1024]{1,0:T(8,128)(2,1)S(1)}, bf16[128,1024]{1,0:T(8,128)(2,1)S(1)}, u32[]{:S(2)}, u32[]{:S(2)}) %collective-permute-start.27) | collective-permute-done | bytes 262176 | tf_op jit(solution)/shard_map/ppermute | solution.py:216
  116.1 3.3 %collective-permute-start.28 = (bf16[128,1024]{1,0:T(8,128)(2,1)S(1)}, bf16[128,1024]{1,0:T(8,128)(2,1)S(1)}, u32[]{:S(2)}, u32[]{:S(2)}) collective-permute-start(bf16[128,1024]{1,0:T(8,128)(2,1)S(1)} %add_convert_fusion.5), channel_id=1, source_target_pairs={{0,16},{2,18},{4,20},{6,22},{8,24},{10,26},{12,28},{14,30},{16,0},... | collective-permute-start | bytes 786440 | tf_op jit(solution)/shard_map/ppermute | solution.py:216
  119.5 5.0 %collective-permute-done.14 = bf16[128,1024]{1,0:T(8,128)(2,1)S(1)} collective-permute-done((bf16[128,1024]{1,0:T(8,128)(2,1)S(1)}, bf16[128,1024]{1,0:T(8,128)(2,1)S(1)}, u32[]{:S(2)}, u32[]{:S(2)}) %collective-permute-start.14) | collective-permute-done | bytes 262176 | tf_op jit(solution)/shard_map/ppermute | solution.py:216
  124.5 5.0 %collective-permute-done.28 = bf16[128,1024]{1,0:T(8,128)(2,1)S(1)} collective-permute-done((bf16[128,1024]{1,0:T(8,128)(2,1)S(1)}, bf16[128,1024]{1,0:T(8,128)(2,1)S(1)}, u32[]{:S(2)}, u32[]{:S(2)}) %collective-permute-start.28) | collective-permute-done | bytes 262176 | tf_op jit(solution)/shard_map/ppermute | solution.py:216
  (66 shorter events, 12.4 us)
Async XLA Ops:
  0.0 16.3 %collective-permute-start.15 = (bf16[128,1024]{1,0:T(8,128)(2,1)}, bf16[128,1024]{1,0:T(8,128)(2,1)S(1)}, u32[]{:S(2)}, u32[]{:S(2)}) collective-permute-start(bf16[128,1024]{1,0:T(8,128)(2,1)} %refs_0_.1), channel_id=1, source_target_pairs={{0,16},{2,18},{4,20},{6,22},{8,24},{10,26},{12,28},{14,30},{16,0},... | collective-permute-start | bytes 786440 | tf_op jit(solution)/shard_map/ppermute | solution.py:216
  4.0 15.9 %collective-permute-start.3 = (bf16[128,1024]{1,0:T(8,128)(2,1)}, bf16[128,1024]{1,0:T(8,128)(2,1)S(1)}, u32[]{:S(2)}, u32[]{:S(2)}) collective-permute-start(bf16[128,1024]{1,0:T(8,128)(2,1)} %refs_0_.1), channel_id=1, source_target_pairs={{0,1},{1,0},{2,3},{3,2},{4,5},{5,4},{6,7},{7,6},{8,9},{9,8},{10,11... | collective-permute-start | bytes 786440 | tf_op jit(solution)/shard_map/ppermute | solution.py:219
  5.5 12.1 %collective-permute-start.5 = (bf16[128,1024]{1,0:T(8,128)(2,1)}, bf16[128,1024]{1,0:T(8,128)(2,1)S(1)}, u32[]{:S(2)}, u32[]{:S(2)}) collective-permute-start(bf16[128,1024]{1,0:T(8,128)(2,1)} %refs_0_.1), channel_id=1, source_target_pairs={{0,8},{2,10},{4,12},{6,14},{8,0},{10,2},{12,4},{14,6},{16,24},{18,... | collective-permute-start | bytes 786440 | tf_op jit(solution)/shard_map/ppermute | solution.py:216
  8.5 10.8 %collective-permute-start = (f32[16,128]{1,0:T(8,128)S(1)}, f32[16,128]{1,0:T(8,128)S(1)}, u32[]{:S(2)}, u32[]{:S(2)}) collective-permute-start(f32[16,128]{1,0:T(8,128)S(1)} %select_reduce_fusion), channel_id=1, source_target_pairs={{0,4},{2,6},{4,0},{6,2},{8,12},{10,14},{12,8},{14,10},{16,20},{18,... | collective-permute-start | bytes 24584 | tf_op jit(solution)/shard_map/ppermute | solution.py:216
  16.3 10.9 %collective-permute-start.18 = (bf16[128,1024]{1,0:T(8,128)(2,1)S(1)}, bf16[128,1024]{1,0:T(8,128)(2,1)S(1)}, u32[]{:S(2)}, u32[]{:S(2)}) collective-permute-start(bf16[128,1024]{1,0:T(8,128)(2,1)S(1)} %collective-permute-done.15.refs_0_), channel_id=1, source_target_pairs={{0,8},{2,10},{4,12},{6,14},{8,0},{10,2},{12,4},{14,6},{16,24},{18,... | collective-permute-start | bytes 786440 | tf_op jit(solution)/shard_map/ppermute | solution.py:216
  17.7 11.0 %collective-permute-start.6 = (bf16[128,1024]{1,0:T(8,128)(2,1)S(1)}, bf16[128,1024]{1,0:T(8,128)(2,1)S(1)}, u32[]{:S(2)}, u32[]{:S(2)}) collective-permute-start(bf16[128,1024]{1,0:T(8,128)(2,1)S(1)} %collective-permute-done.5.refs_4_), channel_id=1, source_target_pairs={{0,4},{2,6},{4,0},{6,2},{8,12},{10,14},{12,8},{14,10},{16,20},{18,... | collective-permute-start | bytes 786440 | tf_op jit(solution)/shard_map/ppermute | solution.py:216
  19.3 4.8 %collective-permute-start.1 = (f32[2,16,128]{2,1,0:T(8,128)S(1)}, f32[2,16,128]{2,1,0:T(8,128)S(1)}, u32[]{:S(2)}, u32[]{:S(2)}) collective-permute-start(f32[2,16,128]{2,1,0:T(8,128)S(1)} %pad_maximum_fusion.6), channel_id=1, source_target_pairs={{0,8},{2,10},{4,12},{6,14},{8,0},{10,2},{12,4},{14,6},{16,24},{18,... | collective-permute-start | bytes 49160 | tf_op jit(solution)/shard_map/ppermute | solution.py:216
  20.9 23.9 %copy-start = (bf16[128,1024]{1,0:T(8,128)(2,1)S(1)}, bf16[128,1024]{1,0:T(8,128)(2,1)}, u32[]{:S(2)}) copy-start(bf16[128,1024]{1,0:T(8,128)(2,1)} %refs_0_.1) | copy-start | bytes 786436
  20.9 23.8 %collective-permute-start.4 = (bf16[2,128,1024]{2,1,0:T(8,128)(2,1)S(1)}, bf16[2,128,1024]{2,1,0:T(8,128)(2,1)S(1)}, u32[]{:S(2)}, u32[]{:S(2)}) collective-permute-start(bf16[2,128,1024]{2,1,0:T(8,128)(2,1)S(1)} %pad_maximum_fusion), channel_id=1, source_target_pairs={{0,4},{2,6},{4,0},{6,2},{8,12},{10,14},{12,8},{14,10},{16,20},{18,... | collective-permute-start | bytes 1572872 | tf_op jit(solution)/shard_map/ppermute | solution.py:216
  21.4 8.8 %collective-permute-start.16 = (bf16[128,1024]{1,0:T(8,128)(2,1)S(1)}, bf16[128,1024]{1,0:T(8,128)(2,1)S(1)}, u32[]{:S(2)}, u32[]{:S(2)}) collective-permute-start(bf16[128,1024]{1,0:T(8,128)(2,1)S(1)} %collective-permute-done.15.refs_0_), channel_id=1, source_target_pairs={{0,1},{1,0},{2,3},{3,2},{4,5},{5,4},{6,7},{7,6},{8,9},{9,8},{10,11... | collective-permute-start | bytes 786440 | tf_op jit(solution)/shard_map/ppermute | solution.py:219
  24.1 6.2 %collective-permute-start.2 = (f32[4,16,128]{2,1,0:T(8,128)S(1)}, f32[4,16,128]{2,1,0:T(8,128)S(1)}, u32[]{:S(2)}, u32[]{:S(2)}) collective-permute-start(f32[4,16,128]{2,1,0:T(8,128)S(1)} %pad_maximum_fusion.5), channel_id=1, source_target_pairs={{0,16},{2,18},{4,20},{6,22},{8,24},{10,26},{12,28},{14,30},{16,0},... | collective-permute-start | bytes 98312 | tf_op jit(solution)/shard_map/ppermute | solution.py:216
  27.2 16.6 %collective-permute-start.19 = (bf16[128,1024]{1,0:T(8,128)(2,1)S(1)}, bf16[128,1024]{1,0:T(8,128)(2,1)S(1)}, u32[]{:S(2)}, u32[]{:S(2)}) collective-permute-start(bf16[128,1024]{1,0:T(8,128)(2,1)S(1)} %collective-permute-done.18.refs_4_), channel_id=1, source_target_pairs={{0,4},{2,6},{4,0},{6,2},{8,12},{10,14},{12,8},{14,10},{16,20},{18,... | collective-permute-start | bytes 786440 | tf_op jit(solution)/shard_map/ppermute | solution.py:216
  28.7 16.0 %collective-permute-start.7 = (bf16[2,128,1024]{2,1,0:T(8,128)(2,1)S(1)}, bf16[2,128,1024]{2,1,0:T(8,128)(2,1)S(1)}, u32[]{:S(2)}, u32[]{:S(2)}) collective-permute-start(bf16[2,128,1024]{2,1,0:T(8,128)(2,1)S(1)} %pad_maximum_fusion.1), channel_id=1, source_target_pairs={{0,1},{1,0},{2,3},{3,2},{4,5},{5,4},{6,7},{7,6},{8,9},{9,8},{10,11... | collective-permute-start | bytes 1572872 | tf_op jit(solution)/shard_map/ppermute | solution.py:219
  30.3 22.8 %collective-permute-start.17 = (bf16[2,128,1024]{2,1,0:T(8,128)(2,1)S(1)}, bf16[2,128,1024]{2,1,0:T(8,128)(2,1)S(1)}, u32[]{:S(2)}, u32[]{:S(2)}) collective-permute-start(bf16[2,128,1024]{2,1,0:T(8,128)(2,1)S(1)} %pad_maximum_fusion.2), channel_id=1, source_target_pairs={{0,4},{2,6},{4,0},{6,2},{8,12},{10,14},{12,8},{14,10},{16,20},{18,... | collective-permute-start | bytes 1572872 | tf_op jit(solution)/shard_map/ppermute | solution.py:216
  43.8 12.2 %copy-start.3 = (bf16[1,704,2048]{2,1,0:T(8,128)(2,1)S(1)}, bf16[1,704,2048]{2,1,0:T(8,128)(2,1)}, u32[]{:S(2)}) copy-start(bf16[1,704,2048]{2,1,0:T(8,128)(2,1)} %down_ref.3) | copy-start | bytes 8650756
  43.8 10.5 %collective-permute-start.20 = (bf16[2,128,1024]{2,1,0:T(8,128)(2,1)S(1)}, bf16[2,128,1024]{2,1,0:T(8,128)(2,1)S(1)}, u32[]{:S(2)}, u32[]{:S(2)}) collective-permute-start(bf16[2,128,1024]{2,1,0:T(8,128)(2,1)S(1)} %pad_maximum_fusion.3), channel_id=1, source_target_pairs={{0,1},{1,0},{2,3},{3,2},{4,5},{5,4},{6,7},{7,6},{8,9},{9,8},{10,11... | collective-permute-start | bytes 1572872 | tf_op jit(solution)/shard_map/ppermute | solution.py:219
  44.8 11.2 %copy-start.1 = (bf16[1,704,2048]{2,1,0:T(8,128)(2,1)S(1)}, bf16[1,704,2048]{2,1,0:T(8,128)(2,1)}, u32[]{:S(2)}) copy-start(bf16[1,704,2048]{2,1,0:T(8,128)(2,1)} %gate_ref.3) | copy-start | bytes 8650756
  46.3 9.7 %collective-permute-start.8 = (bf16[224,2048]{1,0:T(8,128)(2,1)S(1)}, bf16[224,2048]{1,0:T(8,128)(2,1)S(1)}, u32[]{:S(2)}, u32[]{:S(2)}) collective-permute-start(bf16[224,2048]{1,0:T(8,128)(2,1)S(1)} %get-tuple-element.22), channel_id=1, source_target_pairs={{0,2},{2,0},{4,6},{6,4},{8,10},{10,8},{12,14},{14,12},{16,18},{18,... | collective-permute-start | bytes 2752520 | tf_op jit(solution)/shard_map/ppermute | solution.py:216
  55.8 5.7 %collective-permute-start.21 = (bf16[224,2048]{1,0:T(8,128)(2,1)S(1)}, bf16[224,2048]{1,0:T(8,128)(2,1)S(1)}, u32[]{:S(2)}, u32[]{:S(2)}) collective-permute-start(bf16[224,2048]{1,0:T(8,128)(2,1)S(1)} %get-tuple-element.30), channel_id=1, source_target_pairs={{0,2},{2,0},{4,6},{6,4},{8,10},{10,8},{12,14},{14,12},{16,18},{18,... | collective-permute-start | bytes 2752520 | tf_op jit(solution)/shard_map/ppermute | solution.py:216
  61.0 5.7 %collective-permute-start.9 = (bf16[224,2048]{1,0:T(8,128)(2,1)S(1)}, bf16[224,2048]{1,0:T(8,128)(2,1)S(1)}, u32[]{:S(2)}, u32[]{:S(2)}) collective-permute-start(bf16[224,2048]{1,0:T(8,128)(2,1)S(1)} %get-tuple-element.24), channel_id=1, source_target_pairs={{0,2},{2,0},{4,6},{6,4},{8,10},{10,8},{12,14},{14,12},{16,18},{18,... | collective-permute-start | bytes 2752520 | tf_op jit(solution)/shard_map/ppermute | solution.py:216
  66.6 5.0 %collective-permute-start.22 = (bf16[224,2048]{1,0:T(8,128)(2,1)S(1)}, bf16[224,2048]{1,0:T(8,128)(2,1)S(1)}, u32[]{:S(2)}, u32[]{:S(2)}) collective-permute-start(bf16[224,2048]{1,0:T(8,128)(2,1)S(1)} %get-tuple-element.32), channel_id=1, source_target_pairs={{0,2},{2,0},{4,6},{6,4},{8,10},{10,8},{12,14},{14,12},{16,18},{18,... | collective-permute-start | bytes 2752520 | tf_op jit(solution)/shard_map/ppermute | solution.py:216
  68.3 14.8 %collective-permute-start.12 = (bf16[2,128,1024]{2,1,0:T(8,128)(2,1)S(1)}, bf16[2,128,1024]{2,1,0:T(8,128)(2,1)S(1)}, u32[]{:S(2)}, u32[]{:S(2)}) collective-permute-start(bf16[2,128,1024]{2,1,0:T(8,128)(2,1)S(1)} %get-tuple-element.28), channel_id=1, source_target_pairs={{0,1},{1,0},{2,3},{3,2},{4,5},{5,4},{6,7},{7,6},{8,9},{9,8},{10,11... | collective-permute-start | bytes 1572872 | tf_op jit(solution)/shard_map/ppermute | solution.py:219
  70.1 14.8 %collective-permute-start.10 = (bf16[2,128,1024]{2,1,0:T(8,128)(2,1)S(1)}, bf16[2,128,1024]{2,1,0:T(8,128)(2,1)S(1)}, u32[]{:S(2)}, u32[]{:S(2)}) collective-permute-start(bf16[2,128,1024]{2,1,0:T(8,128)(2,1)S(1)} %get-tuple-element.26), channel_id=1, source_target_pairs={{0,4},{2,6},{4,0},{6,2},{8,12},{10,14},{12,8},{14,10},{16,20},{18,... | collective-permute-start | bytes 1572872 | tf_op jit(solution)/shard_map/ppermute | solution.py:216
  73.3 20.7 %collective-permute-start.25 = (bf16[2,128,1024]{2,1,0:T(8,128)(2,1)S(1)}, bf16[2,128,1024]{2,1,0:T(8,128)(2,1)S(1)}, u32[]{:S(2)}, u32[]{:S(2)}) collective-permute-start(bf16[2,128,1024]{2,1,0:T(8,128)(2,1)S(1)} %get-tuple-element.36), channel_id=1, source_target_pairs={{0,1},{1,0},{2,3},{3,2},{4,5},{5,4},{6,7},{7,6},{8,9},{9,8},{10,11... | collective-permute-start | bytes 1572872 | tf_op jit(solution)/shard_map/ppermute | solution.py:219
  73.6 22.5 %collective-permute-start.23 = (bf16[2,128,1024]{2,1,0:T(8,128)(2,1)S(1)}, bf16[2,128,1024]{2,1,0:T(8,128)(2,1)S(1)}, u32[]{:S(2)}, u32[]{:S(2)}) collective-permute-start(bf16[2,128,1024]{2,1,0:T(8,128)(2,1)S(1)} %get-tuple-element.34), channel_id=1, source_target_pairs={{0,4},{2,6},{4,0},{6,2},{8,12},{10,14},{12,8},{14,10},{16,20},{18,... | collective-permute-start | bytes 1572872 | tf_op jit(solution)/shard_map/ppermute | solution.py:216
  83.3 23.9 %collective-permute-start.13 = (bf16[128,1024]{1,0:T(8,128)(2,1)S(1)}, bf16[128,1024]{1,0:T(8,128)(2,1)S(1)}, u32[]{:S(2)}, u32[]{:S(2)}) collective-permute-start(bf16[128,1024]{1,0:T(8,128)(2,1)S(1)} %slice_bitcast_fusion.8), channel_id=1, source_target_pairs={{0,4},{2,6},{4,0},{6,2},{8,12},{10,14},{12,8},{14,10},{16,20},{18,... | collective-permute-start | bytes 786440 | tf_op jit(solution)/shard_map/ppermute | solution.py:216
  94.2 12.5 %collective-permute-start.26 = (bf16[128,1024]{1,0:T(8,128)(2,1)S(1)}, bf16[128,1024]{1,0:T(8,128)(2,1)S(1)}, u32[]{:S(2)}, u32[]{:S(2)}) collective-permute-start(bf16[128,1024]{1,0:T(8,128)(2,1)S(1)} %slice_bitcast_fusion), channel_id=1, source_target_pairs={{0,4},{2,6},{4,0},{6,2},{8,12},{10,14},{12,8},{14,10},{16,20},{18,... | collective-permute-start | bytes 786440 | tf_op jit(solution)/shard_map/ppermute | solution.py:216
  96.4 13.0 %collective-permute-start.24 = (bf16[128,1024]{1,0:T(8,128)(2,1)S(1)}, bf16[128,1024]{1,0:T(8,128)(2,1)S(1)}, u32[]{:S(2)}, u32[]{:S(2)}) collective-permute-start(bf16[128,1024]{1,0:T(8,128)(2,1)S(1)} %slice_bitcast_fusion.2), channel_id=1, source_target_pairs={{0,1},{1,0},{2,3},{3,2},{4,5},{5,4},{6,7},{7,6},{8,9},{9,8},{10,11... | collective-permute-start | bytes 786440 | tf_op jit(solution)/shard_map/ppermute | solution.py:219
  106.7 9.3 %collective-permute-start.27 = (bf16[128,1024]{1,0:T(8,128)(2,1)S(1)}, bf16[128,1024]{1,0:T(8,128)(2,1)S(1)}, u32[]{:S(2)}, u32[]{:S(2)}) collective-permute-start(bf16[128,1024]{1,0:T(8,128)(2,1)S(1)} %fusion), channel_id=1, source_target_pairs={{0,8},{2,10},{4,12},{6,14},{8,0},{10,2},{12,4},{14,6},{16,24},{18,... | collective-permute-start | bytes 786440 | tf_op jit(solution)/shard_map/ppermute | solution.py:216
  106.8 12.7 %collective-permute-start.11 = (bf16[128,1024]{1,0:T(8,128)(2,1)S(1)}, bf16[128,1024]{1,0:T(8,128)(2,1)S(1)}, u32[]{:S(2)}, u32[]{:S(2)}) collective-permute-start(bf16[128,1024]{1,0:T(8,128)(2,1)S(1)} %slice_bitcast_fusion.10), channel_id=1, source_target_pairs={{0,1},{1,0},{2,3},{3,2},{4,5},{5,4},{6,7},{7,6},{8,9},{9,8},{10,11... | collective-permute-start | bytes 786440 | tf_op jit(solution)/shard_map/ppermute | solution.py:219
  107.3 17.1 %collective-permute-start.14 = (bf16[128,1024]{1,0:T(8,128)(2,1)S(1)}, bf16[128,1024]{1,0:T(8,128)(2,1)S(1)}, u32[]{:S(2)}, u32[]{:S(2)}) collective-permute-start(bf16[128,1024]{1,0:T(8,128)(2,1)S(1)} %fusion.2), channel_id=1, source_target_pairs={{0,8},{2,10},{4,12},{6,14},{8,0},{10,2},{12,4},{14,6},{16,24},{18,... | collective-permute-start | bytes 786440 | tf_op jit(solution)/shard_map/ppermute | solution.py:216
  116.1 13.3 %collective-permute-start.28 = (bf16[128,1024]{1,0:T(8,128)(2,1)S(1)}, bf16[128,1024]{1,0:T(8,128)(2,1)S(1)}, u32[]{:S(2)}, u32[]{:S(2)}) collective-permute-start(bf16[128,1024]{1,0:T(8,128)(2,1)S(1)} %add_convert_fusion.5), channel_id=1, source_target_pairs={{0,16},{2,18},{4,20},{6,22},{8,24},{10,26},{12,28},{14,30},{16,0},... | collective-permute-start | bytes 786440 | tf_op jit(solution)/shard_map/ppermute | solution.py:216
  (1 other events, 11.2 us)

commit v3 on v0

--- a/solution.py
+++ b/solution.py
@@ -1,10 +1,23 @@
+import functools
+
 import jax
 import jax.numpy as jnp
 from jax import lax
+from jax.experimental import pallas as pl
+from jax.experimental.pallas import tpu as pltpu
 from jax.sharding import PartitionSpec as P
 
-
-def local(tokens, expert_ids, route_weights, w_gate, w_up, w_down):
+CORE, Y, NEAR, FAR = 1, 2, 4, 8
+VMEM_BYTES = 20 << 20
+ROUTE_FLOPS = 40_000_000_000
+PACK_FLOPS = 10_000_000_000
+MIX_FLOPS = 0
+FIRST_X = ("0",)
+ORDER = ["u1p", "gather2", "pack0", "gather2b", "gather1", "expert0", "u3p", "u3_xy", "gather3", "pack2", "u1_x", "gather1b", "mix0", "expert2", "mix2", "u3_yx", "u1_ys", "pack3", "pack1", "sum0", "expert31", "sum2", "mix31", "out2", "end2", "sum31", "out0", "out31"]
+F32, BF16 = jnp.float32, jnp.bfloat16
+
+
+def general(tokens, expert_ids, route_weights, w_gate, w_up, w_down):
     tok_rows = expert_ids.shape[0]
     top_count = expert_ids.shape[1]
     local_experts = w_gate.shape[0]
@@ -48,6 +61,385 @@
     return mixed.astype(jnp.bfloat16)
 
 
+def kernel_call(body, out_shape, n_in, flops, bytes_accessed, scratch=()):
+    vmem = pl.BlockSpec(memory_space=pltpu.VMEM)
+    return pl.pallas_call(
+        body,
+        out_shape=out_shape,
+        in_specs=[pl.BlockSpec(memory_space=pltpu.SMEM)] + [vmem] * n_in,
+        out_specs=jax.tree.map(lambda _: vmem, out_shape),
+        scratch_shapes=list(scratch),
+        compiler_params=pltpu.CompilerParams(vmem_limit_bytes=VMEM_BYTES),
+        cost_estimate=pl.CostEstimate(flops=flops, bytes_accessed=bytes_accessed, transcendentals=0),
+    )
+
+
+def route_kernel(ids_ref, weights_ref, tokens_ref, out_ref):
+    toks = tokens_ref.shape[0]
+    experts = out_ref.shape[0] - toks
+    total = jnp.zeros((experts, toks), F32)
+    number = lax.broadcasted_iota(jnp.int32, (experts, toks), 0)
+    weights = weights_ref[...].astype(F32)
+    for k in range(ids_ref.shape[0]):
+        total += jnp.where(number == ids_ref[k : k + 1, :], weights[k : k + 1, :], 0.0)
+    out_ref[:toks] = tokens_ref[...]
+    out_ref[toks:] = jnp.zeros((experts, out_ref.shape[1]), BF16)
+    out_ref[toks:, :toks] = total.astype(BF16)
+
+
+def route(ids, weights, tokens, experts):
+    vmem = pl.BlockSpec(memory_space=pltpu.VMEM)
+    return pl.pallas_call(
+        route_kernel,
+        out_shape=jax.ShapeDtypeStruct((tokens.shape[0] + experts, tokens.shape[1]), BF16),
+        in_specs=[vmem] * 3,
+        out_specs=vmem,
+        cost_estimate=pl.CostEstimate(flops=ROUTE_FLOPS, bytes_accessed=1 << 16, transcendentals=0),
+    )(ids, weights, tokens)
+
+
+def routing_table(routes, toks, capacity, weighted):
+    me = lax.axis_index("wide")
+    before = lax.broadcasted_iota(jnp.int32, (toks, toks), 0) <= lax.broadcasted_iota(
+        jnp.int32, (toks, toks), 1
+    )
+    number = lax.broadcasted_iota(jnp.int32, routes[0].shape, 0)
+    weight = jnp.concatenate(
+        [
+            jnp.sum(jnp.where(number == expert, block, 0.0), axis=0, keepdims=True)
+            for expert in (me, me ^ CORE)
+            for block in routes
+        ],
+        axis=0,
+    )
+    chosen = weight > 0
+    count = jnp.dot(
+        jnp.where(chosen, 1.0, 0.0).astype(BF16),
+        jnp.where(before, 1.0, 0.0).astype(BF16),
+        preferred_element_type=F32,
+    )
+    slot = jnp.where(chosen, count.astype(jnp.int32) - 1, -1)
+    tables = []
+    for expert in (0, 1):
+        first, second = slot[2 * expert : 2 * expert + 1], slot[2 * expert + 1 : 2 * expert + 2]
+        second = jnp.where(second >= 0, second + capacity, -1)
+        at = jnp.concatenate([first, second], axis=1)
+        value = jnp.concatenate(
+            [weight[2 * expert : 2 * expert + 1], weight[2 * expert + 1 : 2 * expert + 2]], axis=1
+        )
+        here = lax.broadcasted_iota(jnp.int32, (2 * capacity, 2 * toks), 0) == at
+        tables.append(jnp.where(here, value if weighted else 1.0, 0.0))
+    return jnp.concatenate(tables, axis=0).astype(BF16)
+
+
+def dispatch_kernel(capacity, toks, layout, routes, place_ref, *refs):
+    units, (own_ref, send_ref, routes_ref) = refs[:-3], refs[-3:]
+    rows, half = 2 * capacity, own_ref.shape[1] // 2
+    experts = routes_ref.shape[1]
+    blocks = [units[number][row : row + experts, :toks].astype(F32) for number, row in routes]
+    for i, block in enumerate(blocks):
+        routes_ref[i] = block
+    table = routing_table(blocks, toks, capacity, False)
+    for dx in (0, 1):
+        parts = []
+        for number, at, count, column, dy, row in sorted(layout, key=lambda part: part[4:]):
+            if column == dx:
+                parts.append(units[number][at : at + count])
+        out = jnp.dot(table, jnp.concatenate(parts, axis=0), preferred_element_type=F32).astype(BF16)
+        own_ref[:, dx * half : (dx + 1) * half] = out[:rows]
+        send_ref[:, dx * half : (dx + 1) * half] = out[rows:]
+
+
+def dispatch(place, units, layout, routes, capacity, toks, experts):
+    half = units[0].shape[-1]
+    shape = jax.ShapeDtypeStruct((2 * capacity, 2 * half), BF16)
+    return kernel_call(
+        functools.partial(dispatch_kernel, capacity, toks, layout, routes),
+        (shape, shape, jax.ShapeDtypeStruct((2, experts, toks), F32)),
+        len(units),
+        PACK_FLOPS if len(units) == 4 else 0,
+        0,
+    )(place, *units)
+
+
+def ffn_kernel(count, place_ref, *refs):
+    inputs, (gate_ref, up_ref, down_ref) = refs[:count], refs[count : count + 3]
+    outputs, (rows_ref, hidden_ref) = refs[count + 3 : -2], refs[-2:]
+    x = place_ref[1]
+    n, half = inputs[0].shape[0], inputs[0].shape[1] // 2
+    ff = gate_ref.shape[1]
+    for i, ref in enumerate(inputs):
+        rows_ref[i * n : (i + 1) * n] = ref[...]
+    mine = pl.ds(pl.multiple_of(x * half, half), half)
+    theirs = pl.ds(pl.multiple_of((1 - x) * half, half), half)
+    step = 256
+    nt = (((1,), (1,)), ((), ()))
+    for low in range(0, ff, step):
+        high = min(low + step, ff)
+
+        def project(ref):
+            return lax.dot_general(
+                rows_ref[:, :half], ref[0, low:high, mine], nt, preferred_element_type=F32
+            ) + lax.dot_general(
+                rows_ref[:, half:], ref[0, low:high, theirs], nt, preferred_element_type=F32
+            )
+
+        gate = project(gate_ref)
+        up = project(up_ref)
+        hidden_ref[:, low:high] = (gate / (1.0 + jnp.exp(-gate)) * up).astype(BF16)
+    for j, columns in enumerate((mine, theirs)):
+        out = jnp.dot(hidden_ref[...], down_ref[0, :, columns], preferred_element_type=F32).astype(BF16)
+        for i, ref in enumerate(outputs):
+            ref[:, j * half : (j + 1) * half] = out[i * n : (i + 1) * n]
+
+
+def ffn(place, inputs, w_gate, w_up, w_down):
+    count = len(inputs)
+    n, width = inputs[0].shape
+    ff = w_gate.shape[1]
+    return kernel_call(
+        functools.partial(ffn_kernel, count),
+        (jax.ShapeDtypeStruct((n, width), BF16),) * count,
+        count + 3,
+        count * n * width * ff,
+        0,
+        scratch=(pltpu.VMEM((count * n, width), BF16), pltpu.VMEM((count * n, ff), BF16)),
+    )(place, *inputs, w_gate, w_up, w_down)
+
+
+def combine_kernel(capacity, layouts, place_ref, *refs):
+    count = len(layouts)
+    inputs, outs = refs[: 3 * count], refs[3 * count :]
+    half = inputs[1].shape[1] // 2
+    toks = inputs[0].shape[2]
+    for p, layout in enumerate(layouts):
+        routes_ref, own_ref, other_ref = inputs[3 * p : 3 * p + 3]
+        table = routing_table([routes_ref[0], routes_ref[1]], toks, capacity, True)
+        for dx in (0, 1):
+            columns = slice(dx * half, (dx + 1) * half)
+            value = jnp.concatenate([own_ref[:, columns], other_ref[:, columns]], axis=0)
+            out = lax.dot_general(
+                table, value, (((0,), (0,)), ((), ())), preferred_element_type=F32
+            ).astype(BF16)
+            for number, at, count, column, dy, row in layout:
+                if column == dx:
+                    low = dy * toks + row
+                    outs[number][at : at + count] = out[low : low + count]
+
+
+def combine(place, pairs, layouts, capacity):
+    toks, half = pairs[0][0].shape[2], pairs[0][1].shape[1] // 2
+    parts = [part for layout in layouts for part in layout]
+    rows = [0] * (1 + max(part[0] for part in parts))
+    for part in parts:
+        rows[part[0]] += part[2]
+    return kernel_call(
+        functools.partial(combine_kernel, capacity, layouts),
+        tuple(jax.ShapeDtypeStruct((count, half), BF16) for count in rows),
+        3 * len(pairs),
+        MIX_FLOPS,
+        0,
+    )(place, *[array for pair in pairs for array in pair])
+
+
+def local(tokens, expert_ids, route_weights, w_gate, w_up, w_down):
+    wide = lax.axis_size("wide")
+    tok_rows, top_count = expert_ids.shape
+    capacity = 7 * tok_rows * top_count // (6 * wide)
+    cut, full = tok_rows // 2, tok_rows
+    me, x = lax.axis_index("wide"), lax.axis_index("narrow")
+    place = jnp.stack([me, x]).astype(jnp.int32)
+
+    def hop(value, bit):
+        return lax.ppermute(value, "wide", [(i, i ^ bit) for i in range(wide)])
+
+    def hop_x(value):
+        return lax.ppermute(value, "narrow", [(0, 1), (1, 0)])
+
+    def hop_xy(value):
+        pairs = [(2 * i + j, 2 * (i ^ Y) + 1 - j) for i in range(wide) for j in (0, 1)]
+        return lax.ppermute(value, ("wide", "narrow"), pairs)
+
+    def add(a, b):
+        return (a.astype(F32) + b.astype(F32)).astype(BF16)
+
+    def rows(*parts):
+        return jnp.concatenate(parts, axis=0)
+
+    held, last = {}, []
+
+    def take(*names):
+        values = [held[name] for name in names]
+        tied = lax.optimization_barrier(tuple(values + last))
+        for name, value in zip(names, tied):
+            held[name] = value
+        last[:] = [tied[0]]
+        return tied[0] if len(names) == 1 else tied[: len(names)]
+
+    def put(**values):
+        held.update(values)
+        last[:] = [next(iter(values.values()))]
+
+    halves = (
+        (0, 0, full, 0, 0, 0),
+        (1, 0, cut, 1, 0, 0),
+        (2, 0, cut, 0, 1, cut),
+        (3, 0, cut, 0, 1, 0),
+        (3, cut, cut, 1, 1, 0),
+        (4, 0, cut, 1, 0, cut),
+        (4, cut, cut, 1, 1, cut),
+    )
+    by_dy = ((0, 0, full, 0, 0, 0), (0, full, full, 1, 0, 0), (1, 0, full, 0, 1, 0), (1, full, full, 1, 1, 0))
+    by_dx = ((0, 0, full, 0, 0, 0), (0, full, full, 0, 1, 0), (1, 0, full, 1, 0, 0), (1, full, full, 1, 1, 0))
+    by_half = (
+        (0, 0, cut, 0, 0, 0),
+        (0, cut, cut, 1, 0, 0),
+        (1, 0, cut, 0, 1, 0),
+        (1, cut, cut, 1, 1, 0),
+        (2, 0, cut, 0, 0, cut),
+        (2, cut, cut, 0, 1, cut),
+        (3, 0, cut, 1, 0, cut),
+        (3, cut, cut, 1, 1, cut),
+    )
+
+    def pack(key, units, layout, routes):
+        own, send, table = dispatch(place, take(*units), layout, routes, capacity, tok_rows, wide)
+        put(**{"own" + key: own, "table" + key: table})
+        held["other" + key] = hop(send, CORE)
+
+    def expert(key):
+        mine, theirs = ffn(place, take("own" + key, "other" + key), w_gate, w_up, w_down)
+        put(**{"own" + key: mine})
+        held["back" + key] = hop(theirs, CORE)
+
+    def mix(key, layout):
+        return combine(place, [take("table" + key, "own" + key, "back" + key)], [layout], capacity)
+
+    u0p = route(expert_ids.T, route_weights.T, tokens, wide)
+    held.update(u0p=u0p, u2p=hop(u0p, FAR), u1p=hop(u0p, NEAR), u0p_y=hop(u0p, Y))
+    held.update(u0_x=hop_x(tokens), u0_yx=hop_xy(tokens))
+
+    def gather2():
+        u2p = take("u2p")
+        held.update(top2_x=hop_x(u2p[:cut]), low2_y=hop(u2p[cut:], Y), u3p=hop(u2p, NEAR))
+
+    def gather2b():
+        top_x, low_y, u2p = take("top2_x", "low2_y", "u2p")
+        held.update(tops2=hop(rows(u2p[:cut], top_x), Y), lows2=hop_x(rows(u2p[cut:full], low_y[:cut])))
+        held.update(u3_xy=hop(rows(top_x, low_y), NEAR))
+
+    def gather1():
+        held.update(u1_x=hop_x(take("u1p")[:full]))
+
+    def gather1b():
+        held.update(u1_ys=hop(rows(*take("u1p", "u1_x")), Y))
+
+    def gather3():
+        held.update(u3_yx=hop(rows(*take("tops2", "lows2")), NEAR))
+
+    def pack0():
+        layout = ((0, 0, full, 0, 0, 0), (1, 0, full, 1, 0, 0), (2, 0, full, 0, 1, 0), (3, 0, full, 1, 1, 0))
+        pack("0", ("u0p", "u0_x", "u0p_y", "u0_yx"), layout, ((0, full), (2, full)))
+
+    def pack2():
+        pack("2", ("u2p", "top2_x", "low2_y", "tops2", "lows2"), halves, ((0, full), (2, cut)))
+
+    def pack3():
+        layout = (
+            (0, 0, full, 0, 0, 0),
+            (1, 0, cut, 1, 0, 0),
+            (1, cut, cut, 0, 1, cut),
+            (2, 0, cut, 0, 1, 0),
+            (2, cut, cut, 1, 1, 0),
+            (2, 2 * cut, cut, 1, 0, cut),
+            (2, 3 * cut, cut, 1, 1, cut),
+        )
+        pack("3", ("u3p", "u3_xy", "u3_yx"), layout, ((0, full), (1, 2 * cut)))
+
+    def pack1():
+        layout = (
+            (0, 0, full, 0, 0, 0),
+            (1, 0, full, 1, 0, 0),
+            (2, 0, full, 0, 1, 0),
+            (2, full + wide, full, 1, 1, 0),
+        )
+        pack("1", ("u1p", "u1_x", "u1_ys"), layout, ((0, full), (2, full)))
+
+    def mix_whole(key):
+        def step():
+            first_x = key in FIRST_X
+            keep, send = mix(key, by_dx if first_x else by_dy)
+            put(**{"keep" + key: keep})
+            held["got" + key] = hop_x(send) if first_x else hop(send, Y)
+
+        return step
+
+    def sum_whole(key):
+        def step():
+            keep, got = take("keep" + key, "got" + key)
+            both = add(keep, got)
+            put(**{"keep" + key: both[:full]})
+            held["got" + key] = hop(both[full:], Y) if key in FIRST_X else hop_x(both[full:])
+
+        return step
+
+    def end_whole(key):
+        def step():
+            end = add(*take("keep" + key, "got" + key))
+            put(**{"end" + key: end if key == "0" else hop(end, FAR)})
+            last[:] = [end]
+
+        return step
+
+    def expert31():
+        names = ("own3", "own1", "other3", "other1")
+        own3, own1, back3, back1 = ffn(place, take(*names), w_gate, w_up, w_down)
+        put(own3=own3, own1=own1)
+        held.update(back3=hop(back3, CORE), back1=hop(back1, CORE))
+
+    def mix31():
+        layouts = [
+            tuple((number, at + p * full, count, dx, dy, row) for number, at, count, dx, dy, row in by_half)
+            for p in (0, 1)
+        ]
+        names = ("table3", "own3", "back3", "table1", "own1", "back1")
+        values = take(*names)
+        keep_top, send_top, keep_low, send_low = combine(
+            place, [values[:3], values[3:]], layouts, capacity
+        )
+        put(top=keep_top, low=keep_low)
+        held.update(got_low=hop_x(send_low), got_top=hop(send_top, Y))
+
+    def sum31():
+        top, low, got_top, got_low = take("top", "low", "got_top", "got_low")
+        top, low = add(top, got_top), add(low, got_low)
+        put(top=rows(top[:cut], top[full : full + cut]), low=rows(low[:cut], low[full : full + cut]))
+        held.update(got_top=hop_x(rows(top[cut:full], top[full + cut :])))
+        held.update(got_low=hop(rows(low[cut:full], low[full + cut :]), Y))
+
+    def out31():
+        top, low, got_top, got_low = take("top", "low", "got_top", "got_low")
+        top, low = add(top, got_top), add(low, got_low)
+        put(end3=hop(rows(top[:cut], low[:cut]), NEAR | FAR), end1=hop(rows(top[cut:], low[cut:]), NEAR))
+        last[:] = [top]
+
+    steps = dict(
+        gather2=gather2, gather2b=gather2b, gather1=gather1, gather1b=gather1b, gather3=gather3,
+        pack0=pack0, pack1=pack1, pack2=pack2, pack3=pack3,
+        expert0=lambda: expert("0"), expert2=lambda: expert("2"), expert31=expert31,
+        mix0=mix_whole("0"), mix2=mix_whole("2"), mix31=mix31,
+        sum0=sum_whole("0"), sum2=sum_whole("2"), sum31=sum31,
+        out0=end_whole("0"), out2=end_whole("2"), out31=out31,
+    )
+    for step in ORDER:
+        if step in steps:
+            steps[step]()
+        else:
+            take(*step.split())
+    total = sum(held["end" + key].astype(F32) for key in "0123")
+    return total.astype(BF16)
+
+
 def solution(mesh):
     in_specs = (
         P("wide", "narrow"),
@@ -58,4 +450,7 @@
         P("wide", "narrow", None),
     )
     out_specs = P("wide", "narrow")
-    return jax.shard_map(local, mesh=mesh, in_specs=in_specs, out_specs=out_specs, check_vma=False)
+    fits = mesh.shape["wide"] == 16 and mesh.shape["narrow"] == 2
+    return jax.shard_map(
+        local if fits else general, mesh=mesh, in_specs=in_specs, out_specs=out_specs, check_vma=False
+    )

time: 250 us -> 117 us (0.47); the launches traced: 245 us -> 116 us
  blocking collectives: 97.4 us -> 0 us
  waiting for transfers between devices: 86.1 us -> 58.3 us
  starting transfers between devices: 5.66 us -> 32.9 us
  Pallas kernels: 0 us -> 21.3 us
  matrix products: 16.9 us -> 0 us
  local copies, waits for them, and re-layouts: 15.1 us -> 1.23 us
  between operations: 13.5 us -> 0.38 us
  other arithmetic: 10.3 us -> 2.25 us
    all_to_all x1 -> x0, blocking collectives: 87.2 us -> none  [local(): lax.all_to_all(outgoing, 'wide', split_axis=0, concat_axis=0, tiled=True)]
    ppermute x0 -> x33, waiting for transfers between devices: none -> 58.3 us  [the longest x24 47.8 us: hop(): return lax.ppermute(value, 'wide', [(i, i ^ bit) for i in range(wide)])]
    reduce_scatter x1 -> x0, waiting for transfers between devices: 49.8 us -> none  [local(): lax.psum_scatter(partial_value, 'narrow', scatter_dimension=1, tiled=True)]
    all_to_all x1 -> x0, waiting for transfers between devices: 36.3 us -> none  [local(): lax.all_to_all(summed.astype(jnp.bfloat16), 'wide', split_axis=0, concat_...]
    ppermute x0 -> x33, starting transfers between devices: none -> 32.9 us  [the longest x24 25 us: hop(): return lax.ppermute(value, 'wide', [(i, i ^ bit) for i in range(wide)])]
    pallas_call x0 -> x11, Pallas kernels: none -> 21.3 us  [the longest x3 11.4 us: ffn(): kernel_call(functools.partial(ffn_kernel, count), (jax.ShapeDtypeStruct((...]
    dot_general x3 -> x0, matrix products: 16.9 us -> none  [the longest x1 11.2 us: local(): jnp.einsum('secf,efd->secd', hidden, w_down, preferred_element_type=jnp.f...]
    all_gather x1 -> x0, blocking collectives: 10.2 us -> none  [local(): whole = lax.all_gather(tokens, 'narrow', axis=1, tiled=True)]
  transfers between devices with their start and end apart: 2 -> 33, of which waited for: 2 -> 17; matrix products, arithmetic and copies ran while one was open for 0% -> 1% of each run, Pallas kernels for 0% -> 17%
where the time goes in v3:
time: 117 us; the launch traced here: 116 us
  waiting for transfers between devices  58.3 us (50%)
  starting transfers between devices  32.9 us (28%)
  Pallas kernels  21.3 us (18%)
  other arithmetic  2.25 us (2%)
  local copies, waits for them, and re-layouts  1.23 us (1%)
    ppermute x24, waiting for transfers between devices, hop(): return lax.ppermute(value, 'wide', [(i, i ^ bit) for i in range(wide)])  47.8 us
    ppermute x24, starting transfers between devices, hop(): return lax.ppermute(value, 'wide', [(i, i ^ bit) for i in range(wide)])  25 us
    pallas_call x3, Pallas kernels, ffn(): kernel_call(functools.partial(ffn_kernel, count), (jax.ShapeDtypeStruct((...  11.4 us
    ppermute x8, waiting for transfers between devices, hop_x(): return lax.ppermute(value, 'narrow', [(0, 1), (1, 0)])  10.4 us
    ppermute x8, starting transfers between devices, hop_x(): return lax.ppermute(value, 'narrow', [(0, 1), (1, 0)])  6.49 us
    pallas_call x4, Pallas kernels, dispatch(): kernel_call(functools.partial(dispatch_kernel, capacity, toks, layout, ro...  4.26 us
    pallas_call x3, Pallas kernels, combine(): kernel_call(functools.partial(combine_kernel, capacity, layouts), tuple((...  3.88 us
  transfers between devices with their start and end apart: 33, of which 17 were waited for; matrix products, arithmetic and copies ran while one was open for 1% of the time, Pallas kernels for 17%

profile of v3, /device:TPU:0, one launch (start us, length us, event | category | flops | bytes accessed | tf_op | source)
XLA Modules:
  0.0 116.4 jit_solution(8833021558880613809)
XLA Ops:
  0.0 1.8 %shard_map.64.refs_0_ = bf16[144,1024]{1,0:T(8,128)(2,1)} custom-call(s32[6,128]{1,0:T(8,128)} %bitcast.4, bf16[6,128]{1,0:T(8,128)(2,1)} %bitcast.5, bf16[128,1024]{1,0:T(8,128)(2,1)} %tokens_ref.1), custom_call_target="tpu_custom_call" | custom-call | flops 40000000000 | bytes 65536 | tf_op jit(solution)/shard_map/pallas_call | solution.py:92
  1.8 3.0 %collective-permute-start.4 = (bf16[144,1024]{1,0:T(8,128)(2,1)}, bf16[144,1024]{1,0:T(8,128)(2,1)S(1)}, u32[]{:S(2)}, u32[]{:S(2)}) collective-permute-start(bf16[144,1024]{1,0:T(8,128)(2,1)} %shard_map.64.refs_0_), channel_id=1, source_target_pairs={{0,8},{2,10},{4,12},{6,14},{8,0},{10,2},{12,4},{14,6},{16,24},{18,... | collective-permute-start | bytes 884744 | tf_op jit(solution)/shard_map/ppermute | solution.py:254
  4.8 2.6 %collective-permute-start.3 = (bf16[144,1024]{1,0:T(8,128)(2,1)}, bf16[144,1024]{1,0:T(8,128)(2,1)S(1)}, u32[]{:S(2)}, u32[]{:S(2)}) collective-permute-start(bf16[144,1024]{1,0:T(8,128)(2,1)} %shard_map.64.refs_0_), channel_id=1, source_target_pairs={{0,16},{2,18},{4,20},{6,22},{8,24},{10,26},{12,28},{14,30},{16,0},... | collective-permute-start | bytes 884744 | tf_op jit(solution)/shard_map/ppermute | solution.py:254
  7.4 1.5 %collective-permute-start.1 = (bf16[144,1024]{1,0:T(8,128)(2,1)}, bf16[144,1024]{1,0:T(8,128)(2,1)S(1)}, u32[]{:S(2)}, u32[]{:S(2)}) collective-permute-start(bf16[144,1024]{1,0:T(8,128)(2,1)} %shard_map.64.refs_0_), channel_id=1, source_target_pairs={{0,4},{2,6},{4,0},{6,2},{8,12},{10,14},{12,8},{14,10},{16,20},{18,... | collective-permute-start | bytes 884744 | tf_op jit(solution)/shard_map/ppermute | solution.py:254
  8.9 1.4 %collective-permute-start.2 = (bf16[128,1024]{1,0:T(8,128)(2,1)S(1)}, bf16[128,1024]{1,0:T(8,128)(2,1)S(1)}, u32[]{:S(2)}, u32[]{:S(2)}) collective-permute-start(bf16[128,1024]{1,0:T(8,128)(2,1)S(1)} %copy-done.4), channel_id=1, source_target_pairs={{0,5},{1,4},{2,7},{3,6},{4,1},{5,0},{6,3},{7,2},{8,13},{9,12},{10,... | collective-permute-start | bytes 786440 | tf_op jit(solution)/shard_map/ppermute | solution.py:261
  10.9 7.2 %collective-permute-done.4.refs_0_ = bf16[144,1024]{1,0:T(8,128)(2,1)S(1)} collective-permute-done((bf16[144,1024]{1,0:T(8,128)(2,1)}, bf16[144,1024]{1,0:T(8,128)(2,1)S(1)}, u32[]{:S(2)}, u32[]{:S(2)}) %collective-permute-start.4) | collective-permute-done | bytes 294944 | tf_op jit(solution)/shard_map/ppermute | solution.py:254
  18.2 2.6 %collective-permute-done.3.refs_0_ = bf16[144,1024]{1,0:T(8,128)(2,1)S(1)} collective-permute-done((bf16[144,1024]{1,0:T(8,128)(2,1)}, bf16[144,1024]{1,0:T(8,128)(2,1)S(1)}, u32[]{:S(2)}, u32[]{:S(2)}) %collective-permute-start.3) | collective-permute-done | bytes 294944 | tf_op jit(solution)/shard_map/ppermute | solution.py:254
  21.3 1.5 %collective-permute-start.6 = (bf16[64,1024]{1,0:T(8,128)(2,1)S(1)}, bf16[64,1024]{1,0:T(8,128)(2,1)S(1)}, u32[]{:S(2)}, u32[]{:S(2)}) collective-permute-start(bf16[64,1024]{1,0:T(8,128)(2,1)S(1)} %slice.66), channel_id=1, source_target_pairs={{0,1},{1,0},{2,3},{3,2},{4,5},{5,4},{6,7},{7,6},{8,9},{9,8},{10,11... | collective-permute-start | bytes 393224 | tf_op jit(solution)/shard_map/ppermute | solution.py:257
  22.8 1.5 %collective-permute-start.7 = (bf16[80,1024]{1,0:T(8,128)(2,1)S(1)}, bf16[80,1024]{1,0:T(8,128)(2,1)S(1)}, u32[]{:S(2)}, u32[]{:S(2)}) collective-permute-start(bf16[80,1024]{1,0:T(8,128)(2,1)S(1)} %slice.67), channel_id=1, source_target_pairs={{0,4},{2,6},{4,0},{6,2},{8,12},{10,14},{12,8},{14,10},{16,20},{18,... | collective-permute-start | bytes 491528 | tf_op jit(solution)/shard_map/ppermute | solution.py:254
  26.4 1.7 %collective-permute-done.7.refs_2_ = bf16[80,1024]{1,0:T(8,128)(2,1)S(1)} collective-permute-done((bf16[80,1024]{1,0:T(8,128)(2,1)S(1)}, bf16[80,1024]{1,0:T(8,128)(2,1)S(1)}, u32[]{:S(2)}, u32[]{:S(2)}) %collective-permute-start.7) | collective-permute-done | bytes 163872 | tf_op jit(solution)/shard_map/ppermute | solution.py:254
  28.2 1.6 %collective-permute-start.10 = (bf16[128,1024]{1,0:T(8,128)(2,1)S(1)}, bf16[128,1024]{1,0:T(8,128)(2,1)S(1)}, u32[]{:S(2)}, u32[]{:S(2)}) collective-permute-start(bf16[128,1024]{1,0:T(8,128)(2,1)S(1)} %pad_maximum_fusion.3), channel_id=1, source_target_pairs={{0,4},{2,6},{4,0},{6,2},{8,12},{10,14},{12,8},{14,10},{16,20},{18,... | collective-permute-start | bytes 786440 | tf_op jit(solution)/shard_map/ppermute | solution.py:254
  29.8 1.7 %collective-permute-start.12 = (bf16[144,1024]{1,0:T(8,128)(2,1)S(1)}, bf16[144,1024]{1,0:T(8,128)(2,1)S(1)}, u32[]{:S(2)}, u32[]{:S(2)}) collective-permute-start(bf16[144,1024]{1,0:T(8,128)(2,1)S(1)} %pad_maximum_fusion.2), channel_id=1, source_target_pairs={{0,8},{2,10},{4,12},{6,14},{8,0},{10,2},{12,4},{14,6},{16,24},{18,... | collective-permute-start | bytes 884744 | tf_op jit(solution)/shard_map/ppermute | solution.py:254
  32.1 1.6 %collective-permute-start.9 = (bf16[128,1024]{1,0:T(8,128)(2,1)S(1)}, bf16[128,1024]{1,0:T(8,128)(2,1)S(1)}, u32[]{:S(2)}, u32[]{:S(2)}) collective-permute-start(bf16[128,1024]{1,0:T(8,128)(2,1)S(1)} %slice.68), channel_id=1, source_target_pairs={{0,1},{1,0},{2,3},{3,2},{4,5},{5,4},{6,7},{7,6},{8,9},{9,8},{10,11... | collective-permute-start | bytes 786440 | tf_op jit(solution)/shard_map/ppermute | solution.py:257
  33.6 3.2 %shard_map.66 = (bf16[112,2048]{1,0:T(8,128)(2,1)S(1)}, bf16[112,2048]{1,0:T(8,128)(2,1)S(1)}) custom-call(s32[2]{0:T(128)S(1)} %pad_add_fusion.place_ref, bf16[112,2048]{1,0:T(8,128)(2,1)S(1)} %get-tuple-element.109.refs_0_, bf16[112,2048]{1,0:T(8,128)(2,1)S(1)} %collective-permute-done.5.refs_1_, bf16[1,704,2048]{2,1,0:T(8,128)(2,1)S(1)} %copy-done, ...), custom_call_target="tpu_custom_call" | custom-call | flops 322961408 | tf_op jit(solution)/shard_map/pallas_call | solution.py:200
  36.9 2.8 %collective-permute-done.11.refs_4_ = bf16[128,1024]{1,0:T(8,128)(2,1)S(1)} collective-permute-done((bf16[128,1024]{1,0:T(8,128)(2,1)S(1)}, bf16[128,1024]{1,0:T(8,128)(2,1)S(1)}, u32[]{:S(2)}, u32[]{:S(2)}) %collective-permute-start.11) | collective-permute-done | bytes 262176 | tf_op jit(solution)/shard_map/ppermute | solution.py:257
  40.9 1.7 %collective-permute-done.9.refs_1_ = bf16[128,1024]{1,0:T(8,128)(2,1)S(1)} collective-permute-done((bf16[128,1024]{1,0:T(8,128)(2,1)S(1)}, bf16[128,1024]{1,0:T(8,128)(2,1)S(1)}, u32[]{:S(2)}, u32[]{:S(2)}) %collective-permute-start.9) | collective-permute-done | bytes 262176 | tf_op jit(solution)/shard_map/ppermute | solution.py:257
  42.6 1.6 %collective-permute-start.15 = (bf16[272,1024]{1,0:T(8,128)(2,1)S(1)}, bf16[272,1024]{1,0:T(8,128)(2,1)S(1)}, u32[]{:S(2)}, u32[]{:S(2)}) collective-permute-start(bf16[272,1024]{1,0:T(8,128)(2,1)S(1)} %pad_maximum_fusion), channel_id=1, source_target_pairs={{0,4},{2,6},{4,0},{6,2},{8,12},{10,14},{12,8},{14,10},{16,20},{18,... | collective-permute-start | bytes 1671176 | tf_op jit(solution)/shard_map/ppermute | solution.py:254
  46.5 3.2 %shard_map.69 = (bf16[112,2048]{1,0:T(8,128)(2,1)S(1)}, bf16[112,2048]{1,0:T(8,128)(2,1)S(1)}) custom-call(s32[2]{0:T(128)S(1)} %pad_add_fusion.place_ref, bf16[112,2048]{1,0:T(8,128)(2,1)S(1)} %get-tuple-element.135.refs_0_, bf16[112,2048]{1,0:T(8,128)(2,1)S(1)} %collective-permute-done.17.refs_1_, bf16[1,704,2048]{2,1,0:T(8,128)(2,1)S(1)} %copy-done, ...), custom_call_target="tpu_custom_call" | custom-call | flops 322961408 | tf_op jit(solution)/shard_map/pallas_call | solution.py:200
  49.8 1.8 %collective-permute-done.18.refs_2_ = bf16[112,2048]{1,0:T(8,128)(2,1)S(1)} collective-permute-done((bf16[112,2048]{1,0:T(8,128)(2,1)S(1)}, bf16[112,2048]{1,0:T(8,128)(2,1)S(1)}, u32[]{:S(2)}, u32[]{:S(2)}) %collective-permute-start.18) | collective-permute-done | bytes 458784 | tf_op jit(solution)/shard_map/ppermute | solution.py:254
  52.7 3.9 %collective-permute-done.16.refs_2_ = bf16[256,1024]{1,0:T(8,128)(2,1)S(1)} collective-permute-done((bf16[256,1024]{1,0:T(8,128)(2,1)S(1)}, bf16[256,1024]{1,0:T(8,128)(2,1)S(1)}, u32[]{:S(2)}, u32[]{:S(2)}) %collective-permute-start.16) | collective-permute-done | bytes 524320 | tf_op jit(solution)/shard_map/ppermute | solution.py:254
  61.9 5.0 %shard_map.73 = (bf16[112,2048]{1,0:T(8,128)(2,1)S(1)}, bf16[112,2048]{1,0:T(8,128)(2,1)S(1)}, bf16[112,2048]{1,0:T(8,128)(2,1)S(1)}, bf16[112,2048]{1,0:T(8,128)(2,1)S(1)}) custom-call(s32[2]{0:T(128)S(1)} %pad_add_fusion.place_ref, bf16[112,2048]{1,0:T(8,128)(2,1)S(1)} %get-tuple-element.158.refs_0_, bf16[112,2048]{1,0:T(8,128)(2,1)S(1)} %get-tuple-element.159.refs_1_, ...), custom_call_target="tpu_custom_call" | custom-call | flops 645922816 | tf_op jit(solution)/shard_map/pallas_call | solution.py:200
  69.5 1.6 %shard_map.74 = (bf16[256,1024]{1,0:T(8,128)(2,1)S(1)}, bf16[256,1024]{1,0:T(8,128)(2,1)S(1)}, bf16[256,1024]{1,0:T(8,128)(2,1)S(1)}, bf16[256,1024]{1,0:T(8,128)(2,1)S(1)}) custom-call(s32[2]{0:T(128)S(1)} %pad_add_fusion.place_ref, f32[2,16,128]{2,1,0:T(8,128)S(1)} %get-tuple-element.170.refs_0_, bf16[112,2048]{1,0:T(8,128)(2,1)S(1)} %get-tuple-element.171.refs_1_, ...), custom_call_target="tpu_custom_call" | custom-call | tf_op jit(solution)/shard_map/pallas_call | solution.py:236
  71.1 1.5 %collective-permute-start.25 = (bf16[256,1024]{1,0:T(8,128)(2,1)S(1)}, bf16[256,1024]{1,0:T(8,128)(2,1)S(1)}, u32[]{:S(2)}, u32[]{:S(2)}) collective-permute-start(bf16[256,1024]{1,0:T(8,128)(2,1)S(1)} %get-tuple-element.178), channel_id=1, source_target_pairs={{0,4},{2,6},{4,0},{6,2},{8,12},{10,14},{12,8},{14,10},{16,20},{18,... | collective-permute-start | bytes 1572872 | tf_op jit(solution)/shard_map/ppermute | solution.py:254
  73.2 4.3 %collective-permute-done.27 = bf16[128,1024]{1,0:T(8,128)(2,1)S(1)} collective-permute-done((bf16[128,1024]{1,0:T(8,128)(2,1)S(1)}, bf16[128,1024]{1,0:T(8,128)(2,1)S(1)}, u32[]{:S(2)}, u32[]{:S(2)}) %collective-permute-start.27) | collective-permute-done | bytes 262176 | tf_op jit(solution)/shard_map/ppermute | solution.py:257
  77.6 1.4 %collective-permute-start.28 = (bf16[128,1024]{1,0:T(8,128)(2,1)S(1)}, bf16[128,1024]{1,0:T(8,128)(2,1)S(1)}, u32[]{:S(2)}, u32[]{:S(2)}) collective-permute-start(bf16[128,1024]{1,0:T(8,128)(2,1)S(1)} %add_convert_fusion.8), channel_id=1, source_target_pairs={{0,16},{2,18},{4,20},{6,22},{8,24},{10,26},{12,28},{14,30},{16,0},... | collective-permute-start | bytes 786440 | tf_op jit(solution)/shard_map/ppermute | solution.py:254
  80.0 9.9 %collective-permute-done.28 = bf16[128,1024]{1,0:T(8,128)(2,1)S(1)} collective-permute-done((bf16[128,1024]{1,0:T(8,128)(2,1)S(1)}, bf16[128,1024]{1,0:T(8,128)(2,1)S(1)}, u32[]{:S(2)}, u32[]{:S(2)}) %collective-permute-start.28) | collective-permute-done | bytes 262176 | tf_op jit(solution)/shard_map/ppermute | solution.py:254
  90.4 2.2 %collective-permute-start.30 = (bf16[128,1024]{1,0:T(8,128)(2,1)S(1)}, bf16[128,1024]{1,0:T(8,128)(2,1)S(1)}, u32[]{:S(2)}, u32[]{:S(2)}) collective-permute-start(bf16[128,1024]{1,0:T(8,128)(2,1)S(1)} %pad_maximum_fusion.8), channel_id=1, source_target_pairs={{0,4},{2,6},{4,0},{6,2},{8,12},{10,14},{12,8},{14,10},{16,20},{18,... | collective-permute-start | bytes 786440 | tf_op jit(solution)/shard_map/ppermute | solution.py:254
  93.3 5.7 %collective-permute-done.30 = bf16[128,1024]{1,0:T(8,128)(2,1)S(1)} collective-permute-done((bf16[128,1024]{1,0:T(8,128)(2,1)S(1)}, bf16[128,1024]{1,0:T(8,128)(2,1)S(1)}, u32[]{:S(2)}, u32[]{:S(2)}) %collective-permute-start.30) | collective-permute-done | bytes 262176 | tf_op jit(solution)/shard_map/ppermute | solution.py:254
  99.0 1.6 %collective-permute-done.29 = bf16[128,1024]{1,0:T(8,128)(2,1)S(1)} collective-permute-done((bf16[128,1024]{1,0:T(8,128)(2,1)S(1)}, bf16[128,1024]{1,0:T(8,128)(2,1)S(1)}, u32[]{:S(2)}, u32[]{:S(2)}) %collective-permute-start.29) | collective-permute-done | bytes 262176 | tf_op jit(solution)/shard_map/ppermute | solution.py:257
  100.9 2.4 %collective-permute-start.32 = (bf16[128,1024]{1,0:T(8,128)(2,1)S(1)}, bf16[128,1024]{1,0:T(8,128)(2,1)S(1)}, u32[]{:S(2)}, u32[]{:S(2)}) collective-permute-start(bf16[128,1024]{1,0:T(8,128)(2,1)S(1)} %pad_maximum_fusion.10), channel_id=1, source_target_pairs={{0,24},{2,26},{4,28},{6,30},{8,16},{10,18},{12,20},{14,22},{16,8},... | collective-permute-start | bytes 786440 | tf_op jit(solution)/shard_map/ppermute | solution.py:254
  103.4 8.6 %collective-permute-done.32 = bf16[128,1024]{1,0:T(8,128)(2,1)S(1)} collective-permute-done((bf16[128,1024]{1,0:T(8,128)(2,1)S(1)}, bf16[128,1024]{1,0:T(8,128)(2,1)S(1)}, u32[]{:S(2)}, u32[]{:S(2)}) %collective-permute-start.32) | collective-permute-done | bytes 262176 | tf_op jit(solution)/shard_map/ppermute | solution.py:254
  112.0 3.5 %collective-permute-done.31 = bf16[128,1024]{1,0:T(8,128)(2,1)S(1)} collective-permute-done((bf16[128,1024]{1,0:T(8,128)(2,1)S(1)}, bf16[128,1024]{1,0:T(8,128)(2,1)S(1)}, u32[]{:S(2)}, u32[]{:S(2)}) %collective-permute-start.31) | collective-permute-done | bytes 262176 | tf_op jit(solution)/shard_map/ppermute | solution.py:254
  (86 shorter events, 20.3 us)
Async XLA Ops:
  1.8 16.4 %collective-permute-start.4 = (bf16[144,1024]{1,0:T(8,128)(2,1)}, bf16[144,1024]{1,0:T(8,128)(2,1)S(1)}, u32[]{:S(2)}, u32[]{:S(2)}) collective-permute-start(bf16[144,1024]{1,0:T(8,128)(2,1)} %shard_map.64.refs_0_), channel_id=1, source_target_pairs={{0,8},{2,10},{4,12},{6,14},{8,0},{10,2},{12,4},{14,6},{16,24},{18,... | collective-permute-start | bytes 884744 | tf_op jit(solution)/shard_map/ppermute | solution.py:254
  4.8 16.0 %collective-permute-start.3 = (bf16[144,1024]{1,0:T(8,128)(2,1)}, bf16[144,1024]{1,0:T(8,128)(2,1)S(1)}, u32[]{:S(2)}, u32[]{:S(2)}) collective-permute-start(bf16[144,1024]{1,0:T(8,128)(2,1)} %shard_map.64.refs_0_), channel_id=1, source_target_pairs={{0,16},{2,18},{4,20},{6,22},{8,24},{10,26},{12,28},{14,30},{16,0},... | collective-permute-start | bytes 884744 | tf_op jit(solution)/shard_map/ppermute | solution.py:254
  7.4 16.9 %collective-permute-start.1 = (bf16[144,1024]{1,0:T(8,128)(2,1)}, bf16[144,1024]{1,0:T(8,128)(2,1)S(1)}, u32[]{:S(2)}, u32[]{:S(2)}) collective-permute-start(bf16[144,1024]{1,0:T(8,128)(2,1)} %shard_map.64.refs_0_), channel_id=1, source_target_pairs={{0,4},{2,6},{4,0},{6,2},{8,12},{10,14},{12,8},{14,10},{16,20},{18,... | collective-permute-start | bytes 884744 | tf_op jit(solution)/shard_map/ppermute | solution.py:254
  8.9 13.9 %collective-permute-start.2 = (bf16[128,1024]{1,0:T(8,128)(2,1)S(1)}, bf16[128,1024]{1,0:T(8,128)(2,1)S(1)}, u32[]{:S(2)}, u32[]{:S(2)}) collective-permute-start(bf16[128,1024]{1,0:T(8,128)(2,1)S(1)} %copy-done.4), channel_id=1, source_target_pairs={{0,5},{1,4},{2,7},{3,6},{4,1},{5,0},{6,3},{7,2},{8,13},{9,12},{10,... | collective-permute-start | bytes 786440 | tf_op jit(solution)/shard_map/ppermute | solution.py:261
  10.3 14.0 %collective-permute-start = (bf16[128,1024]{1,0:T(8,128)(2,1)S(1)}, bf16[128,1024]{1,0:T(8,128)(2,1)S(1)}, u32[]{:S(2)}, u32[]{:S(2)}) collective-permute-start(bf16[128,1024]{1,0:T(8,128)(2,1)S(1)} %copy-done.4), channel_id=1, source_target_pairs={{0,1},{1,0},{2,3},{3,2},{4,5},{5,4},{6,7},{7,6},{8,9},{9,8},{10,11... | collective-permute-start | bytes 786440 | tf_op jit(solution)/shard_map/ppermute | solution.py:257
  20.8 16.1 %collective-permute-start.13 = (bf16[144,1024]{1,0:T(8,128)(2,1)S(1)}, bf16[144,1024]{1,0:T(8,128)(2,1)S(1)}, u32[]{:S(2)}, u32[]{:S(2)}) collective-permute-start(bf16[144,1024]{1,0:T(8,128)(2,1)S(1)} %collective-permute-done.3.refs_0_), channel_id=1, source_target_pairs={{0,8},{2,10},{4,12},{6,14},{8,0},{10,2},{12,4},{14,6},{16,24},{18,... | collective-permute-start | bytes 884744 | tf_op jit(solution)/shard_map/ppermute | solution.py:254
  21.3 5.2 %collective-permute-start.6 = (bf16[64,1024]{1,0:T(8,128)(2,1)S(1)}, bf16[64,1024]{1,0:T(8,128)(2,1)S(1)}, u32[]{:S(2)}, u32[]{:S(2)}) collective-permute-start(bf16[64,1024]{1,0:T(8,128)(2,1)S(1)} %slice.66), channel_id=1, source_target_pairs={{0,1},{1,0},{2,3},{3,2},{4,5},{5,4},{6,7},{7,6},{8,9},{9,8},{10,11... | collective-permute-start | bytes 393224 | tf_op jit(solution)/shard_map/ppermute | solution.py:257
  22.8 5.3 %collective-permute-start.7 = (bf16[80,1024]{1,0:T(8,128)(2,1)S(1)}, bf16[80,1024]{1,0:T(8,128)(2,1)S(1)}, u32[]{:S(2)}, u32[]{:S(2)}) collective-permute-start(bf16[80,1024]{1,0:T(8,128)(2,1)S(1)} %slice.67), channel_id=1, source_target_pairs={{0,4},{2,6},{4,0},{6,2},{8,12},{10,14},{12,8},{14,10},{16,20},{18,... | collective-permute-start | bytes 491528 | tf_op jit(solution)/shard_map/ppermute | solution.py:254
  26.3 5.7 %collective-permute-start.5 = (bf16[112,2048]{1,0:T(8,128)(2,1)S(1)}, bf16[112,2048]{1,0:T(8,128)(2,1)S(1)}, u32[]{:S(2)}, u32[]{:S(2)}) collective-permute-start(bf16[112,2048]{1,0:T(8,128)(2,1)S(1)} %get-tuple-element.106), channel_id=1, source_target_pairs={{0,2},{2,0},{4,6},{6,4},{8,10},{10,8},{12,14},{14,12},{16,18},{18,... | collective-permute-start | bytes 1376264 | tf_op jit(solution)/shard_map/ppermute | solution.py:254
  28.2 8.8 %collective-permute-start.10 = (bf16[128,1024]{1,0:T(8,128)(2,1)S(1)}, bf16[128,1024]{1,0:T(8,128)(2,1)S(1)}, u32[]{:S(2)}, u32[]{:S(2)}) collective-permute-start(bf16[128,1024]{1,0:T(8,128)(2,1)S(1)} %pad_maximum_fusion.3), channel_id=1, source_target_pairs={{0,4},{2,6},{4,0},{6,2},{8,12},{10,14},{12,8},{14,10},{16,20},{18,... | collective-permute-start | bytes 786440 | tf_op jit(solution)/shard_map/ppermute | solution.py:254
  29.8 7.2 %collective-permute-start.12 = (bf16[144,1024]{1,0:T(8,128)(2,1)S(1)}, bf16[144,1024]{1,0:T(8,128)(2,1)S(1)}, u32[]{:S(2)}, u32[]{:S(2)}) collective-permute-start(bf16[144,1024]{1,0:T(8,128)(2,1)S(1)} %pad_maximum_fusion.2), channel_id=1, source_target_pairs={{0,8},{2,10},{4,12},{6,14},{8,0},{10,2},{12,4},{14,6},{16,24},{18,... | collective-permute-start | bytes 884744 | tf_op jit(solution)/shard_map/ppermute | solution.py:254
  31.4 8.3 %collective-permute-start.11 = (bf16[128,1024]{1,0:T(8,128)(2,1)S(1)}, bf16[128,1024]{1,0:T(8,128)(2,1)S(1)}, u32[]{:S(2)}, u32[]{:S(2)}) collective-permute-start(bf16[128,1024]{1,0:T(8,128)(2,1)S(1)} %pad_maximum_fusion.4), channel_id=1, source_target_pairs={{0,1},{1,0},{2,3},{3,2},{4,5},{5,4},{6,7},{7,6},{8,9},{9,8},{10,11... | collective-permute-start | bytes 786440 | tf_op jit(solution)/shard_map/ppermute | solution.py:257
  32.1 10.5 %collective-permute-start.9 = (bf16[128,1024]{1,0:T(8,128)(2,1)S(1)}, bf16[128,1024]{1,0:T(8,128)(2,1)S(1)}, u32[]{:S(2)}, u32[]{:S(2)}) collective-permute-start(bf16[128,1024]{1,0:T(8,128)(2,1)S(1)} %slice.68), channel_id=1, source_target_pairs={{0,1},{1,0},{2,3},{3,2},{4,5},{5,4},{6,7},{7,6},{8,9},{9,8},{10,11... | collective-permute-start | bytes 786440 | tf_op jit(solution)/shard_map/ppermute | solution.py:257
  36.8 7.9 %collective-permute-start.8 = (bf16[112,2048]{1,0:T(8,128)(2,1)S(1)}, bf16[112,2048]{1,0:T(8,128)(2,1)S(1)}, u32[]{:S(2)}, u32[]{:S(2)}) collective-permute-start(bf16[112,2048]{1,0:T(8,128)(2,1)S(1)} %get-tuple-element.112), channel_id=1, source_target_pairs={{0,2},{2,0},{4,6},{6,4},{8,10},{10,8},{12,14},{14,12},{16,18},{18,... | collective-permute-start | bytes 1376264 | tf_op jit(solution)/shard_map/ppermute | solution.py:254
  40.9 5.7 %collective-permute-start.17 = (bf16[112,2048]{1,0:T(8,128)(2,1)S(1)}, bf16[112,2048]{1,0:T(8,128)(2,1)S(1)}, u32[]{:S(2)}, u32[]{:S(2)}) collective-permute-start(bf16[112,2048]{1,0:T(8,128)(2,1)S(1)} %get-tuple-element.134), channel_id=1, source_target_pairs={{0,2},{2,0},{4,6},{6,4},{8,10},{10,8},{12,14},{14,12},{16,18},{18,... | collective-permute-start | bytes 1376264 | tf_op jit(solution)/shard_map/ppermute | solution.py:254
  42.6 14.6 %collective-permute-start.15 = (bf16[272,1024]{1,0:T(8,128)(2,1)S(1)}, bf16[272,1024]{1,0:T(8,128)(2,1)S(1)}, u32[]{:S(2)}, u32[]{:S(2)}) collective-permute-start(bf16[272,1024]{1,0:T(8,128)(2,1)S(1)} %pad_maximum_fusion), channel_id=1, source_target_pairs={{0,4},{2,6},{4,0},{6,2},{8,12},{10,14},{12,8},{14,10},{16,20},{18,... | collective-permute-start | bytes 1671176 | tf_op jit(solution)/shard_map/ppermute | solution.py:254
  44.3 12.4 %collective-permute-start.16 = (bf16[256,1024]{1,0:T(8,128)(2,1)S(1)}, bf16[256,1024]{1,0:T(8,128)(2,1)S(1)}, u32[]{:S(2)}, u32[]{:S(2)}) collective-permute-start(bf16[256,1024]{1,0:T(8,128)(2,1)S(1)} %pad_maximum_fusion.1), channel_id=1, source_target_pairs={{0,8},{2,10},{4,12},{6,14},{8,0},{10,2},{12,4},{14,6},{16,24},{18,... | collective-permute-start | bytes 1572872 | tf_op jit(solution)/shard_map/ppermute | solution.py:254
  45.9 14.0 %collective-permute-start.14 = (bf16[256,1024]{1,0:T(8,128)(2,1)S(1)}, bf16[256,1024]{1,0:T(8,128)(2,1)S(1)}, u32[]{:S(2)}, u32[]{:S(2)}) collective-permute-start(bf16[256,1024]{1,0:T(8,128)(2,1)S(1)} %get-tuple-element.131), channel_id=1, source_target_pairs={{0,1},{1,0},{2,3},{3,2},{4,5},{5,4},{6,7},{7,6},{8,9},{9,8},{10,11... | collective-permute-start | bytes 1572872 | tf_op jit(solution)/shard_map/ppermute | solution.py:257
  49.7 1.9 %collective-permute-start.18 = (bf16[112,2048]{1,0:T(8,128)(2,1)S(1)}, bf16[112,2048]{1,0:T(8,128)(2,1)S(1)}, u32[]{:S(2)}, u32[]{:S(2)}) collective-permute-start(bf16[112,2048]{1,0:T(8,128)(2,1)S(1)} %get-tuple-element.138), channel_id=1, source_target_pairs={{0,2},{2,0},{4,6},{6,4},{8,10},{10,8},{12,14},{14,12},{16,18},{18,... | collective-permute-start | bytes 1376264 | tf_op jit(solution)/shard_map/ppermute | solution.py:254
  56.7 11.4 %collective-permute-start.24 = (bf16[256,1024]{1,0:T(8,128)(2,1)S(1)}, bf16[256,1024]{1,0:T(8,128)(2,1)S(1)}, u32[]{:S(2)}, u32[]{:S(2)}) collective-permute-start(bf16[256,1024]{1,0:T(8,128)(2,1)S(1)} %get-tuple-element.167), channel_id=1, source_target_pairs={{0,4},{2,6},{4,0},{6,2},{8,12},{10,14},{12,8},{14,10},{16,20},{18,... | collective-permute-start | bytes 1572872 | tf_op jit(solution)/shard_map/ppermute | solution.py:254
  59.5 2.5 %collective-permute-start.20 = (bf16[112,2048]{1,0:T(8,128)(2,1)S(1)}, bf16[112,2048]{1,0:T(8,128)(2,1)S(1)}, u32[]{:S(2)}, u32[]{:S(2)}) collective-permute-start(bf16[112,2048]{1,0:T(8,128)(2,1)S(1)} %get-tuple-element.156), channel_id=1, source_target_pairs={{0,2},{2,0},{4,6},{6,4},{8,10},{10,8},{12,14},{14,12},{16,18},{18,... | collective-permute-start | bytes 1376264 | tf_op jit(solution)/shard_map/ppermute | solution.py:254
  67.0 2.0 %collective-permute-start.22 = (bf16[112,2048]{1,0:T(8,128)(2,1)S(1)}, bf16[112,2048]{1,0:T(8,128)(2,1)S(1)}, u32[]{:S(2)}, u32[]{:S(2)}) collective-permute-start(bf16[112,2048]{1,0:T(8,128)(2,1)S(1)} %get-tuple-element.163), channel_id=1, source_target_pairs={{0,2},{2,0},{4,6},{6,4},{8,10},{10,8},{12,14},{14,12},{16,18},{18,... | collective-permute-start | bytes 1376264 | tf_op jit(solution)/shard_map/ppermute | solution.py:254
  67.2 2.3 %collective-permute-start.23 = (bf16[112,2048]{1,0:T(8,128)(2,1)S(1)}, bf16[112,2048]{1,0:T(8,128)(2,1)S(1)}, u32[]{:S(2)}, u32[]{:S(2)}) collective-permute-start(bf16[112,2048]{1,0:T(8,128)(2,1)S(1)} %get-tuple-element.166), channel_id=1, source_target_pairs={{0,2},{2,0},{4,6},{6,4},{8,10},{10,8},{12,14},{14,12},{16,18},{18,... | collective-permute-start | bytes 1376264 | tf_op jit(solution)/shard_map/ppermute | solution.py:254
  68.3 9.2 %collective-permute-start.27 = (bf16[128,1024]{1,0:T(8,128)(2,1)S(1)}, bf16[128,1024]{1,0:T(8,128)(2,1)S(1)}, u32[]{:S(2)}, u32[]{:S(2)}) collective-permute-start(bf16[128,1024]{1,0:T(8,128)(2,1)S(1)} %get-tuple-element.203), channel_id=1, source_target_pairs={{0,1},{1,0},{2,3},{3,2},{4,5},{5,4},{6,7},{7,6},{8,9},{9,8},{10,11... | collective-permute-start | bytes 786440 | tf_op jit(solution)/shard_map/ppermute | solution.py:257
  71.1 18.8 %collective-permute-start.25 = (bf16[256,1024]{1,0:T(8,128)(2,1)S(1)}, bf16[256,1024]{1,0:T(8,128)(2,1)S(1)}, u32[]{:S(2)}, u32[]{:S(2)}) collective-permute-start(bf16[256,1024]{1,0:T(8,128)(2,1)S(1)} %get-tuple-element.178), channel_id=1, source_target_pairs={{0,4},{2,6},{4,0},{6,2},{8,12},{10,14},{12,8},{14,10},{16,20},{18,... | collective-permute-start | bytes 1572872 | tf_op jit(solution)/shard_map/ppermute | solution.py:254
  72.7 17.3 %collective-permute-start.26 = (bf16[256,1024]{1,0:T(8,128)(2,1)S(1)}, bf16[256,1024]{1,0:T(8,128)(2,1)S(1)}, u32[]{:S(2)}, u32[]{:S(2)}) collective-permute-start(bf16[256,1024]{1,0:T(8,128)(2,1)S(1)} %get-tuple-element.179), channel_id=1, source_target_pairs={{0,1},{1,0},{2,3},{3,2},{4,5},{5,4},{6,7},{7,6},{8,9},{9,8},{10,11... | collective-permute-start | bytes 1572872 | tf_op jit(solution)/shard_map/ppermute | solution.py:257
  77.6 12.3 %collective-permute-start.28 = (bf16[128,1024]{1,0:T(8,128)(2,1)S(1)}, bf16[128,1024]{1,0:T(8,128)(2,1)S(1)}, u32[]{:S(2)}, u32[]{:S(2)}) collective-permute-start(bf16[128,1024]{1,0:T(8,128)(2,1)S(1)} %add_convert_fusion.8), channel_id=1, source_target_pairs={{0,16},{2,18},{4,20},{6,22},{8,24},{10,26},{12,28},{14,30},{16,0},... | collective-permute-start | bytes 786440 | tf_op jit(solution)/shard_map/ppermute | solution.py:254
  79.0 14.3 %collective-permute-start.19 = (bf16[128,1024]{1,0:T(8,128)(2,1)S(1)}, bf16[128,1024]{1,0:T(8,128)(2,1)S(1)}, u32[]{:S(2)}, u32[]{:S(2)}) collective-permute-start(bf16[128,1024]{1,0:T(8,128)(2,1)S(1)} %get-tuple-element.193), channel_id=1, source_target_pairs={{0,4},{2,6},{4,0},{6,2},{8,12},{10,14},{12,8},{14,10},{16,20},{18,... | collective-permute-start | bytes 786440 | tf_op jit(solution)/shard_map/ppermute | solution.py:254
  90.4 8.6 %collective-permute-start.30 = (bf16[128,1024]{1,0:T(8,128)(2,1)S(1)}, bf16[128,1024]{1,0:T(8,128)(2,1)S(1)}, u32[]{:S(2)}, u32[]{:S(2)}) collective-permute-start(bf16[128,1024]{1,0:T(8,128)(2,1)S(1)} %pad_maximum_fusion.8), channel_id=1, source_target_pairs={{0,4},{2,6},{4,0},{6,2},{8,12},{10,14},{12,8},{14,10},{16,20},{18,... | collective-permute-start | bytes 786440 | tf_op jit(solution)/shard_map/ppermute | solution.py:254
  92.6 8.0 %collective-permute-start.29 = (bf16[128,1024]{1,0:T(8,128)(2,1)S(1)}, bf16[128,1024]{1,0:T(8,128)(2,1)S(1)}, u32[]{:S(2)}, u32[]{:S(2)}) collective-permute-start(bf16[128,1024]{1,0:T(8,128)(2,1)S(1)} %pad_maximum_fusion.7), channel_id=1, source_target_pairs={{0,1},{1,0},{2,3},{3,2},{4,5},{5,4},{6,7},{7,6},{8,9},{9,8},{10,11... | collective-permute-start | bytes 786440 | tf_op jit(solution)/shard_map/ppermute | solution.py:257
  100.9 11.1 %collective-permute-start.32 = (bf16[128,1024]{1,0:T(8,128)(2,1)S(1)}, bf16[128,1024]{1,0:T(8,128)(2,1)S(1)}, u32[]{:S(2)}, u32[]{:S(2)}) collective-permute-start(bf16[128,1024]{1,0:T(8,128)(2,1)S(1)} %pad_maximum_fusion.10), channel_id=1, source_target_pairs={{0,24},{2,26},{4,28},{6,30},{8,16},{10,18},{12,20},{14,22},{16,8},... | collective-permute-start | bytes 786440 | tf_op jit(solution)/shard_map/ppermute | solution.py:254
  103.3 12.2 %collective-permute-start.31 = (bf16[128,1024]{1,0:T(8,128)(2,1)S(1)}, bf16[128,1024]{1,0:T(8,128)(2,1)S(1)}, u32[]{:S(2)}, u32[]{:S(2)}) collective-permute-start(bf16[128,1024]{1,0:T(8,128)(2,1)S(1)} %pad_maximum_fusion.9), channel_id=1, source_target_pairs={{0,8},{2,10},{4,12},{6,14},{8,0},{10,2},{12,4},{14,6},{16,24},{18,... | collective-permute-start | bytes 786440 | tf_op jit(solution)/shard_map/ppermute | solution.py:254
  (6 other events, 35.8 us)

commit v4 on v3

--- a/solution.py
+++ b/solution.py
@@ -12,8 +12,8 @@
 ROUTE_FLOPS = 40_000_000_000
 PACK_FLOPS = 10_000_000_000
 MIX_FLOPS = 0
-FIRST_X = ("0",)
-ORDER = ["u1p", "gather2", "pack0", "gather2b", "gather1", "expert0", "u3p", "u3_xy", "gather3", "pack2", "u1_x", "gather1b", "mix0", "expert2", "mix2", "u3_yx", "u1_ys", "pack3", "pack1", "sum0", "expert31", "sum2", "mix31", "out2", "end2", "sum31", "out0", "out31"]
+FIRST_X = ("2",)
+ORDER = ["u1p", "gather12", "pack0", "gather2", "gather1", "expert0", "pack2", "gather3", "expert2", "mix0", "mix2", "pack1", "pack3", "expert31", "sum0", "mix3", "mix1", "sum2", "sum3", "out2", "sum1", "out3", "end2", "out1", "out0"]
 F32, BF16 = jnp.float32, jnp.bfloat16
 
 
@@ -150,14 +150,14 @@
         send_ref[:, dx * half : (dx + 1) * half] = out[rows:]
 
 
-def dispatch(place, units, layout, routes, capacity, toks, experts):
+def dispatch(place, units, layout, routes, capacity, toks, experts, flops):
     half = units[0].shape[-1]
     shape = jax.ShapeDtypeStruct((2 * capacity, 2 * half), BF16)
     return kernel_call(
         functools.partial(dispatch_kernel, capacity, toks, layout, routes),
         (shape, shape, jax.ShapeDtypeStruct((2, experts, toks), F32)),
         len(units),
-        PACK_FLOPS if len(units) == 4 else 0,
+        flops,
         0,
     )(place, *units)
 
@@ -303,7 +303,7 @@
     )
 
     def pack(key, units, layout, routes):
-        own, send, table = dispatch(place, take(*units), layout, routes, capacity, tok_rows, wide)
+        own, send, table = dispatch(place, take(*units), layout, routes, capacity, tok_rows, wide, PACK_FLOPS if key == "0" else 0)
         put(**{"own" + key: own, "table" + key: table})
         held["other" + key] = hop(send, CORE)
 
@@ -319,30 +319,37 @@
     held.update(u0p=u0p, u2p=hop(u0p, FAR), u1p=hop(u0p, NEAR), u0p_y=hop(u0p, Y))
     held.update(u0_x=hop_x(tokens), u0_yx=hop_xy(tokens))
 
+    def gather12():
+        u2p, u1p = take("u2p", "u1p")
+        held.update(top_x=hop_x(rows(u2p[:cut], u1p[:cut])), low_y=hop(rows(u2p[cut:], u1p[cut:]), Y))
+        held.update(u3p=hop(u2p, NEAR))
+
     def gather2():
-        u2p = take("u2p")
-        held.update(top2_x=hop_x(u2p[:cut]), low2_y=hop(u2p[cut:], Y), u3p=hop(u2p, NEAR))
-
-    def gather2b():
-        top_x, low_y, u2p = take("top2_x", "low2_y", "u2p")
-        held.update(tops2=hop(rows(u2p[:cut], top_x), Y), lows2=hop_x(rows(u2p[cut:full], low_y[:cut])))
-        held.update(u3_xy=hop(rows(top_x, low_y), NEAR))
+        top_x, low_y, u2p = take("top_x", "low_y", "u2p")
+        held.update(tops2=hop(rows(u2p[:cut], top_x[:cut]), Y))
+        held.update(lows2=hop_x(rows(u2p[cut:full], low_y[:cut])))
+        held.update(u3_xy=hop(rows(top_x[:cut], low_y[: cut + wide]), NEAR))
 
     def gather1():
-        held.update(u1_x=hop_x(take("u1p")[:full]))
-
-    def gather1b():
-        held.update(u1_ys=hop(rows(*take("u1p", "u1_x")), Y))
+        top_x, low_y, u1p = take("top_x", "low_y", "u1p")
+        held.update(tops1=hop(rows(u1p[:cut], top_x[cut:]), Y))
+        held.update(lows1=hop_x(rows(u1p[cut:full], low_y[cut + wide : full + wide])))
 
     def gather3():
-        held.update(u3_yx=hop(rows(*take("tops2", "lows2")), NEAR))
+        u3p, u3_xy = take("u3p", "u3_xy")
+        held.update(tops3=hop(rows(u3p[:cut], u3_xy[:cut]), Y))
+        held.update(lows3=hop_x(rows(u3p[cut:full], u3_xy[cut:full])))
 
     def pack0():
         layout = ((0, 0, full, 0, 0, 0), (1, 0, full, 1, 0, 0), (2, 0, full, 0, 1, 0), (3, 0, full, 1, 1, 0))
         pack("0", ("u0p", "u0_x", "u0p_y", "u0_yx"), layout, ((0, full), (2, full)))
 
     def pack2():
-        pack("2", ("u2p", "top2_x", "low2_y", "tops2", "lows2"), halves, ((0, full), (2, cut)))
+        pack("2", ("u2p", "top_x", "low_y", "tops2", "lows2"), halves, ((0, full), (2, cut)))
+
+    def pack1():
+        layout = ((0, 0, full, 0, 0, 0), (1, cut, cut, 1, 0, 0), (2, cut + wide, cut, 0, 1, cut)) + halves[3:]
+        pack("1", ("u1p", "top_x", "low_y", "tops1", "lows1"), layout, ((0, full), (2, full + wide)))
 
     def pack3():
         layout = (
@@ -351,19 +358,10 @@
             (1, cut, cut, 0, 1, cut),
             (2, 0, cut, 0, 1, 0),
             (2, cut, cut, 1, 1, 0),
-            (2, 2 * cut, cut, 1, 0, cut),
-            (2, 3 * cut, cut, 1, 1, cut),
+            (3, 0, cut, 1, 0, cut),
+            (3, cut, cut, 1, 1, cut),
         )
-        pack("3", ("u3p", "u3_xy", "u3_yx"), layout, ((0, full), (1, 2 * cut)))
-
-    def pack1():
-        layout = (
-            (0, 0, full, 0, 0, 0),
-            (1, 0, full, 1, 0, 0),
-            (2, 0, full, 0, 1, 0),
-            (2, full + wide, full, 1, 1, 0),
-        )
-        pack("1", ("u1p", "u1_x", "u1_ys"), layout, ((0, full), (2, full)))
+        pack("3", ("u3p", "u3_xy", "tops3", "lows3"), layout, ((0, full), (1, full)))
 
     def mix_whole(key):
         def step():
@@ -391,45 +389,49 @@
 
         return step
 
-    def expert31():
-        names = ("own3", "own1", "other3", "other1")
-        own3, own1, back3, back1 = ffn(place, take(*names), w_gate, w_up, w_down)
-        put(own3=own3, own1=own1)
-        held.update(back3=hop(back3, CORE), back1=hop(back1, CORE))
-
-    def mix31():
-        layouts = [
-            tuple((number, at + p * full, count, dx, dy, row) for number, at, count, dx, dy, row in by_half)
-            for p in (0, 1)
-        ]
-        names = ("table3", "own3", "back3", "table1", "own1", "back1")
-        values = take(*names)
-        keep_top, send_top, keep_low, send_low = combine(
-            place, [values[:3], values[3:]], layouts, capacity
-        )
-        put(top=keep_top, low=keep_low)
-        held.update(got_low=hop_x(send_low), got_top=hop(send_top, Y))
-
-    def sum31():
-        top, low, got_top, got_low = take("top", "low", "got_top", "got_low")
-        top, low = add(top, got_top), add(low, got_low)
-        put(top=rows(top[:cut], top[full : full + cut]), low=rows(low[:cut], low[full : full + cut]))
-        held.update(got_top=hop_x(rows(top[cut:full], top[full + cut :])))
-        held.update(got_low=hop(rows(low[cut:full], low[full + cut :]), Y))
-
-    def out31():
-        top, low, got_top, got_low = take("top", "low", "got_top", "got_low")
-        top, low = add(top, got_top), add(low, got_low)
-        put(end3=hop(rows(top[:cut], low[:cut]), NEAR | FAR), end1=hop(rows(top[cut:], low[cut:]), NEAR))
-        last[:] = [top]
+    def mix_halves(key):
+        def step():
+            keep_top, send_top, keep_low, send_low = mix(key, by_half)
+            put(**{"top" + key: keep_top, "low" + key: keep_low})
+            held.update({"got_low" + key: hop_x(send_low), "got_top" + key: hop(send_top, Y)})
+
+        return step
+
+    def sum_halves(key):
+        def step():
+            top, low, got_top, got_low = take("top" + key, "low" + key, "got_top" + key, "got_low" + key)
+            top, low = add(top, got_top), add(low, got_low)
+            put(**{"top" + key: top[:cut], "low" + key: low[:cut]})
+            held.update({"got_top" + key: hop_x(top[cut:]), "got_low" + key: hop(low[cut:], Y)})
+
+        return step
+
+    def end_halves(key):
+        def step():
+            top, low, got_top, got_low = take("top" + key, "low" + key, "got_top" + key, "got_low" + key)
+            end = rows(add(top, got_top), add(low, got_low))
+            put(**{"end" + key: hop(end, NEAR | FAR if key == "3" else NEAR)})
+            last[:] = [end]
+
+        return step
+
+    def expert_pair(a, b):
+        def step():
+            names = ("own" + a, "own" + b, "other" + a, "other" + b)
+            own_a, own_b, back_a, back_b = ffn(place, take(*names), w_gate, w_up, w_down)
+            put(**{"own" + a: own_a, "own" + b: own_b})
+            held.update({"back" + a: hop(back_a, CORE), "back" + b: hop(back_b, CORE)})
+
+        return step
 
     steps = dict(
-        gather2=gather2, gather2b=gather2b, gather1=gather1, gather1b=gather1b, gather3=gather3,
+        gather12=gather12, gather2=gather2, gather1=gather1, gather3=gather3,
         pack0=pack0, pack1=pack1, pack2=pack2, pack3=pack3,
-        expert0=lambda: expert("0"), expert2=lambda: expert("2"), expert31=expert31,
-        mix0=mix_whole("0"), mix2=mix_whole("2"), mix31=mix31,
-        sum0=sum_whole("0"), sum2=sum_whole("2"), sum31=sum31,
-        out0=end_whole("0"), out2=end_whole("2"), out31=out31,
+        expert0=lambda: expert("0"), expert1=lambda: expert("1"), expert2=lambda: expert("2"),
+        expert3=lambda: expert("3"), expert31=expert_pair("3", "1"), expert21=expert_pair("2", "1"),
+        mix0=mix_whole("0"), mix2=mix_whole("2"), mix1=mix_halves("1"), mix3=mix_halves("3"),
+        sum0=sum_whole("0"), sum2=sum_whole("2"), sum1=sum_halves("1"), sum3=sum_halves("3"),
+        out0=end_whole("0"), out2=end_whole("2"), out1=end_halves("1"), out3=end_halves("3"),
     )
     for step in ORDER:
         if step in steps:

time: 117 us -> 112 us (0.957)
  waiting for transfers between devices: 58.3 us -> 43.6 us
  starting transfers between devices: 32.9 us -> 42.3 us
    ppermute x24 -> x26, waiting for transfers between devices: 47.8 us -> 35.5 us  [hop(): return lax.ppermute(value, 'wide', [(i, i ^ bit) for i in range(wide)])]
    ppermute x8 -> x11, starting transfers between devices: 6.49 us -> 11.4 us  [hop_x(): return lax.ppermute(value, 'narrow', [(0, 1), (1, 0)])]
    ppermute x24 -> x26, starting transfers between devices: 25 us -> 29.5 us  [hop(): return lax.ppermute(value, 'wide', [(i, i ^ bit) for i in range(wide)])]
    ppermute x8 -> x11, waiting for transfers between devices: 10.4 us -> 8.08 us  [hop_x(): return lax.ppermute(value, 'narrow', [(0, 1), (1, 0)])]
    pallas_call x3 -> x4, Pallas kernels: 3.88 us -> 4.56 us  [combine(): kernel_call(functools.partial(combine_kernel, capacity, layouts), tuple((...]
  transfers between devices with their start and end apart: 33 -> 38, of which waited for: 17 -> 19; matrix products, arithmetic and copies ran while one was open for 1% -> 1% of each run, Pallas kernels for 17% -> 18%
where the time goes in v4:
time: 112 us
  waiting for transfers between devices  43.6 us (39%)
  starting transfers between devices  42.3 us (38%)
  Pallas kernels  22 us (20%)
  other arithmetic  2.06 us (2%)
  local copies, waits for them, and re-layouts  1.3 us (1%)
    ppermute x26, waiting for transfers between devices, hop(): return lax.ppermute(value, 'wide', [(i, i ^ bit) for i in range(wide)])  35.5 us
    ppermute x26, starting transfers between devices, hop(): return lax.ppermute(value, 'wide', [(i, i ^ bit) for i in range(wide)])  29.5 us
    ppermute x11, starting transfers between devices, hop_x(): return lax.ppermute(value, 'narrow', [(0, 1), (1, 0)])  11.4 us
    pallas_call x3, Pallas kernels, ffn(): kernel_call(functools.partial(ffn_kernel, count), (jax.ShapeDtypeStruct((...  11.4 us
    ppermute x11, waiting for transfers between devices, hop_x(): return lax.ppermute(value, 'narrow', [(0, 1), (1, 0)])  8.08 us
    pallas_call x4, Pallas kernels, combine(): kernel_call(functools.partial(combine_kernel, capacity, layouts), tuple((...  4.56 us
    pallas_call x4, Pallas kernels, dispatch(): kernel_call(functools.partial(dispatch_kernel, capacity, toks, layout, ro...  4.26 us
  transfers between devices with their start and end apart: 38, of which 19 were waited for; matrix products, arithmetic and copies ran while one was open for 1% of the time, Pallas kernels for 18%

profile of v4, /device:TPU:0, one launch (start us, length us, event | category | flops | bytes accessed | tf_op | source)
XLA Modules:
  0.0 111.7 jit_solution(18070839272525205876)
XLA Ops:
  0.0 1.8 %shard_map.64.refs_0_ = bf16[144,1024]{1,0:T(8,128)(2,1)} custom-call(s32[6,128]{1,0:T(8,128)} %bitcast.4, bf16[6,128]{1,0:T(8,128)(2,1)} %bitcast.5, bf16[128,1024]{1,0:T(8,128)(2,1)} %tokens_ref.1), custom_call_target="tpu_custom_call" | custom-call | flops 40000000000 | bytes 65536 | tf_op jit(solution)/shard_map/pallas_call | solution.py:92
  1.8 3.0 %collective-permute-start.4 = (bf16[144,1024]{1,0:T(8,128)(2,1)}, bf16[144,1024]{1,0:T(8,128)(2,1)S(1)}, u32[]{:S(2)}, u32[]{:S(2)}) collective-permute-start(bf16[144,1024]{1,0:T(8,128)(2,1)} %shard_map.64.refs_0_), channel_id=1, source_target_pairs={{0,8},{2,10},{4,12},{6,14},{8,0},{10,2},{12,4},{14,6},{16,24},{18,... | collective-permute-start | bytes 884744 | tf_op jit(solution)/shard_map/ppermute | solution.py:254
  4.8 2.6 %collective-permute-start.3 = (bf16[144,1024]{1,0:T(8,128)(2,1)}, bf16[144,1024]{1,0:T(8,128)(2,1)S(1)}, u32[]{:S(2)}, u32[]{:S(2)}) collective-permute-start(bf16[144,1024]{1,0:T(8,128)(2,1)} %shard_map.64.refs_0_), channel_id=1, source_target_pairs={{0,16},{2,18},{4,20},{6,22},{8,24},{10,26},{12,28},{14,30},{16,0},... | collective-permute-start | bytes 884744 | tf_op jit(solution)/shard_map/ppermute | solution.py:254
  7.4 1.5 %collective-permute-start.1 = (bf16[144,1024]{1,0:T(8,128)(2,1)}, bf16[144,1024]{1,0:T(8,128)(2,1)S(1)}, u32[]{:S(2)}, u32[]{:S(2)}) collective-permute-start(bf16[144,1024]{1,0:T(8,128)(2,1)} %shard_map.64.refs_0_), channel_id=1, source_target_pairs={{0,4},{2,6},{4,0},{6,2},{8,12},{10,14},{12,8},{14,10},{16,20},{18,... | collective-permute-start | bytes 884744 | tf_op jit(solution)/shard_map/ppermute | solution.py:254
  8.9 1.4 %collective-permute-start.2 = (bf16[128,1024]{1,0:T(8,128)(2,1)S(1)}, bf16[128,1024]{1,0:T(8,128)(2,1)S(1)}, u32[]{:S(2)}, u32[]{:S(2)}) collective-permute-start(bf16[128,1024]{1,0:T(8,128)(2,1)S(1)} %copy-done.4), channel_id=1, source_target_pairs={{0,5},{1,4},{2,7},{3,6},{4,1},{5,0},{6,3},{7,2},{8,13},{9,12},{10,... | collective-permute-start | bytes 786440 | tf_op jit(solution)/shard_map/ppermute | solution.py:261
  11.0 7.2 %collective-permute-done.4.refs_0_ = bf16[144,1024]{1,0:T(8,128)(2,1)S(1)} collective-permute-done((bf16[144,1024]{1,0:T(8,128)(2,1)}, bf16[144,1024]{1,0:T(8,128)(2,1)S(1)}, u32[]{:S(2)}, u32[]{:S(2)}) %collective-permute-start.4) | collective-permute-done | bytes 294944 | tf_op jit(solution)/shard_map/ppermute | solution.py:254
  18.2 2.6 %collective-permute-done.3.refs_0_ = bf16[144,1024]{1,0:T(8,128)(2,1)S(1)} collective-permute-done((bf16[144,1024]{1,0:T(8,128)(2,1)}, bf16[144,1024]{1,0:T(8,128)(2,1)S(1)}, u32[]{:S(2)}, u32[]{:S(2)}) %collective-permute-start.3) | collective-permute-done | bytes 294944 | tf_op jit(solution)/shard_map/ppermute | solution.py:254
  21.4 1.6 %collective-permute-start.6 = (bf16[128,1024]{1,0:T(8,128)(2,1)S(1)}, bf16[128,1024]{1,0:T(8,128)(2,1)S(1)}, u32[]{:S(2)}, u32[]{:S(2)}) collective-permute-start(bf16[128,1024]{1,0:T(8,128)(2,1)S(1)} %pad_maximum_fusion.2), channel_id=1, source_target_pairs={{0,1},{1,0},{2,3},{3,2},{4,5},{5,4},{6,7},{7,6},{8,9},{9,8},{10,11... | collective-permute-start | bytes 786440 | tf_op jit(solution)/shard_map/ppermute | solution.py:257
  23.0 1.6 %collective-permute-start.7 = (bf16[160,1024]{1,0:T(8,128)(2,1)S(1)}, bf16[160,1024]{1,0:T(8,128)(2,1)S(1)}, u32[]{:S(2)}, u32[]{:S(2)}) collective-permute-start(bf16[160,1024]{1,0:T(8,128)(2,1)S(1)} %pad_maximum_fusion), channel_id=1, source_target_pairs={{0,4},{2,6},{4,0},{6,2},{8,12},{10,14},{12,8},{14,10},{16,20},{18,... | collective-permute-start | bytes 983048 | tf_op jit(solution)/shard_map/ppermute | solution.py:254
  26.7 1.6 %collective-permute-done.6.refs_1_ = bf16[128,1024]{1,0:T(8,128)(2,1)S(1)} collective-permute-done((bf16[128,1024]{1,0:T(8,128)(2,1)S(1)}, bf16[128,1024]{1,0:T(8,128)(2,1)S(1)}, u32[]{:S(2)}, u32[]{:S(2)}) %collective-permute-start.6) | collective-permute-done | bytes 262176 | tf_op jit(solution)/shard_map/ppermute | solution.py:257
  28.3 2.7 %collective-permute-done.7.refs_2_ = bf16[160,1024]{1,0:T(8,128)(2,1)S(1)} collective-permute-done((bf16[160,1024]{1,0:T(8,128)(2,1)S(1)}, bf16[160,1024]{1,0:T(8,128)(2,1)S(1)}, u32[]{:S(2)}, u32[]{:S(2)}) %collective-permute-start.7) | collective-permute-done | bytes 327712 | tf_op jit(solution)/shard_map/ppermute | solution.py:254
  31.1 1.6 %collective-permute-start.9 = (bf16[128,1024]{1,0:T(8,128)(2,1)S(1)}, bf16[128,1024]{1,0:T(8,128)(2,1)S(1)}, u32[]{:S(2)}, u32[]{:S(2)}) collective-permute-start(bf16[128,1024]{1,0:T(8,128)(2,1)S(1)} %pad_maximum_fusion.3), channel_id=1, source_target_pairs={{0,4},{2,6},{4,0},{6,2},{8,12},{10,14},{12,8},{14,10},{16,20},{18,... | collective-permute-start | bytes 786440 | tf_op jit(solution)/shard_map/ppermute | solution.py:254
  34.9 3.2 %shard_map.66 = (bf16[112,2048]{1,0:T(8,128)(2,1)S(1)}, bf16[112,2048]{1,0:T(8,128)(2,1)S(1)}) custom-call(s32[2]{0:T(128)S(1)} %pad_add_fusion.place_ref, bf16[112,2048]{1,0:T(8,128)(2,1)S(1)} %get-tuple-element.122.refs_0_, bf16[112,2048]{1,0:T(8,128)(2,1)S(1)} %collective-permute-done.5.refs_1_, bf16[1,704,2048]{2,1,0:T(8,128)(2,1)S(1)} %copy-done, ...), custom_call_target="tpu_custom_call" | custom-call | flops 322961408 | tf_op jit(solution)/shard_map/pallas_call | solution.py:200
  42.1 3.2 %shard_map.68 = (bf16[112,2048]{1,0:T(8,128)(2,1)S(1)}, bf16[112,2048]{1,0:T(8,128)(2,1)S(1)}) custom-call(s32[2]{0:T(128)S(1)} %pad_add_fusion.place_ref, bf16[112,2048]{1,0:T(8,128)(2,1)S(1)} %get-tuple-element.136.refs_0_, bf16[112,2048]{1,0:T(8,128)(2,1)S(1)} %collective-permute-done.11.refs_1_, bf16[1,704,2048]{2,1,0:T(8,128)(2,1)S(1)} %copy-done, ...), custom_call_target="tpu_custom_call" | custom-call | flops 322961408 | tf_op jit(solution)/shard_map/pallas_call | solution.py:200
  45.5 1.6 %collective-permute-start.15 = (bf16[128,1024]{1,0:T(8,128)(2,1)S(1)}, bf16[128,1024]{1,0:T(8,128)(2,1)S(1)}, u32[]{:S(2)}, u32[]{:S(2)}) collective-permute-start(bf16[128,1024]{1,0:T(8,128)(2,1)S(1)} %pad_maximum_fusion.5), channel_id=1, source_target_pairs={{0,4},{2,6},{4,0},{6,2},{8,12},{10,14},{12,8},{14,10},{16,20},{18,... | collective-permute-start | bytes 786440 | tf_op jit(solution)/shard_map/ppermute | solution.py:254
  47.2 1.4 %collective-permute-start.16 = (bf16[128,1024]{1,0:T(8,128)(2,1)S(1)}, bf16[128,1024]{1,0:T(8,128)(2,1)S(1)}, u32[]{:S(2)}, u32[]{:S(2)}) collective-permute-start(bf16[128,1024]{1,0:T(8,128)(2,1)S(1)} %pad_maximum_fusion.6), channel_id=1, source_target_pairs={{0,1},{1,0},{2,3},{3,2},{4,5},{5,4},{6,7},{7,6},{8,9},{9,8},{10,11... | collective-permute-start | bytes 786440 | tf_op jit(solution)/shard_map/ppermute | solution.py:257
  52.6 2.5 %collective-permute-done.15.refs_2_ = bf16[128,1024]{1,0:T(8,128)(2,1)S(1)} collective-permute-done((bf16[128,1024]{1,0:T(8,128)(2,1)S(1)}, bf16[128,1024]{1,0:T(8,128)(2,1)S(1)}, u32[]{:S(2)}, u32[]{:S(2)}) %collective-permute-start.15) | collective-permute-done | bytes 262176 | tf_op jit(solution)/shard_map/ppermute | solution.py:254
  56.3 1.4 %collective-permute-start.27 = (bf16[256,1024]{1,0:T(8,128)(2,1)S(1)}, bf16[256,1024]{1,0:T(8,128)(2,1)S(1)}, u32[]{:S(2)}, u32[]{:S(2)}) collective-permute-start(bf16[256,1024]{1,0:T(8,128)(2,1)S(1)} %get-tuple-element.188), channel_id=1, source_target_pairs={{0,1},{1,0},{2,3},{3,2},{4,5},{5,4},{6,7},{7,6},{8,9},{9,8},{10,11... | collective-permute-start | bytes 1572872 | tf_op jit(solution)/shard_map/ppermute | solution.py:257
  58.1 5.0 %shard_map.73 = (bf16[112,2048]{1,0:T(8,128)(2,1)S(1)}, bf16[112,2048]{1,0:T(8,128)(2,1)S(1)}, bf16[112,2048]{1,0:T(8,128)(2,1)S(1)}, bf16[112,2048]{1,0:T(8,128)(2,1)S(1)}) custom-call(s32[2]{0:T(128)S(1)} %pad_add_fusion.place_ref, bf16[112,2048]{1,0:T(8,128)(2,1)S(1)} %get-tuple-element.165.refs_0_, bf16[112,2048]{1,0:T(8,128)(2,1)S(1)} %get-tuple-element.166.refs_1_, ...), custom_call_target="tpu_custom_call" | custom-call | flops 645922816 | tf_op jit(solution)/shard_map/pallas_call | solution.py:200
  63.8 2.2 %collective-permute-done.14 = bf16[256,1024]{1,0:T(8,128)(2,1)S(1)} collective-permute-done((bf16[256,1024]{1,0:T(8,128)(2,1)S(1)}, bf16[256,1024]{1,0:T(8,128)(2,1)S(1)}, u32[]{:S(2)}, u32[]{:S(2)}) %collective-permute-start.14) | collective-permute-done | bytes 524320 | tf_op jit(solution)/shard_map/ppermute | solution.py:254
  69.3 1.8 %collective-permute-done.27 = bf16[256,1024]{1,0:T(8,128)(2,1)S(1)} collective-permute-done((bf16[256,1024]{1,0:T(8,128)(2,1)S(1)}, bf16[256,1024]{1,0:T(8,128)(2,1)S(1)}, u32[]{:S(2)}, u32[]{:S(2)}) %collective-permute-start.27) | collective-permute-done | bytes 524320 | tf_op jit(solution)/shard_map/ppermute | solution.py:257
  71.1 1.4 %collective-permute-start.29 = (bf16[128,1024]{1,0:T(8,128)(2,1)S(1)}, bf16[128,1024]{1,0:T(8,128)(2,1)S(1)}, u32[]{:S(2)}, u32[]{:S(2)}) collective-permute-start(bf16[128,1024]{1,0:T(8,128)(2,1)S(1)} %get-tuple-element.192), channel_id=1, source_target_pairs={{0,4},{2,6},{4,0},{6,2},{8,12},{10,14},{12,8},{14,10},{16,20},{18,... | collective-permute-start | bytes 786440 | tf_op jit(solution)/shard_map/ppermute | solution.py:254
  75.9 4.5 %collective-permute-done.29 = bf16[128,1024]{1,0:T(8,128)(2,1)S(1)} collective-permute-done((bf16[128,1024]{1,0:T(8,128)(2,1)S(1)}, bf16[128,1024]{1,0:T(8,128)(2,1)S(1)}, u32[]{:S(2)}, u32[]{:S(2)}) %collective-permute-start.29) | collective-permute-done | bytes 262176 | tf_op jit(solution)/shard_map/ppermute | solution.py:254
  82.4 3.5 %collective-permute-done.28 = bf16[128,1024]{1,0:T(8,128)(2,1)S(1)} collective-permute-done((bf16[128,1024]{1,0:T(8,128)(2,1)S(1)}, bf16[128,1024]{1,0:T(8,128)(2,1)S(1)}, u32[]{:S(2)}, u32[]{:S(2)}) %collective-permute-start.28) | collective-permute-done | bytes 262176 | tf_op jit(solution)/shard_map/ppermute | solution.py:254
  86.0 2.9 %collective-permute-start.33 = (bf16[128,1024]{1,0:T(8,128)(2,1)S(1)}, bf16[128,1024]{1,0:T(8,128)(2,1)S(1)}, u32[]{:S(2)}, u32[]{:S(2)}) collective-permute-start(bf16[128,1024]{1,0:T(8,128)(2,1)S(1)} %add_convert_fusion.7), channel_id=1, source_target_pairs={{0,16},{2,18},{4,20},{6,22},{8,24},{10,26},{12,28},{14,30},{16,0},... | collective-permute-start | bytes 786440 | tf_op jit(solution)/shard_map/ppermute | solution.py:254
  89.9 1.4 %collective-permute-start.31 = (bf16[64,1024]{1,0:T(8,128)(2,1)S(1)}, bf16[64,1024]{1,0:T(8,128)(2,1)S(1)}, u32[]{:S(2)}, u32[]{:S(2)}) collective-permute-start(bf16[64,1024]{1,0:T(8,128)(2,1)S(1)} %get-tuple-element.229), channel_id=1, source_target_pairs={{0,1},{1,0},{2,3},{3,2},{4,5},{5,4},{6,7},{7,6},{8,9},{9,8},{10,11... | collective-permute-start | bytes 393224 | tf_op jit(solution)/shard_map/ppermute | solution.py:257
  92.1 1.4 %collective-permute-start.35 = (bf16[64,1024]{1,0:T(8,128)(2,1)S(1)}, bf16[64,1024]{1,0:T(8,128)(2,1)S(1)}, u32[]{:S(2)}, u32[]{:S(2)}) collective-permute-start(bf16[64,1024]{1,0:T(8,128)(2,1)S(1)} %get-tuple-element.231), channel_id=1, source_target_pairs={{0,4},{2,6},{4,0},{6,2},{8,12},{10,14},{12,8},{14,10},{16,20},{18,... | collective-permute-start | bytes 393224 | tf_op jit(solution)/shard_map/ppermute | solution.py:254
  93.6 2.8 %collective-permute-done.34 = bf16[64,1024]{1,0:T(8,128)(2,1)S(1)} collective-permute-done((bf16[64,1024]{1,0:T(8,128)(2,1)S(1)}, bf16[64,1024]{1,0:T(8,128)(2,1)S(1)}, u32[]{:S(2)}, u32[]{:S(2)}) %collective-permute-start.34) | collective-permute-done | bytes 131104 | tf_op jit(solution)/shard_map/ppermute | solution.py:257
  97.9 2.7 %collective-permute-start.37 = (bf16[128,1024]{1,0:T(8,128)(2,1)S(1)}, bf16[128,1024]{1,0:T(8,128)(2,1)S(1)}, u32[]{:S(2)}, u32[]{:S(2)}) collective-permute-start(bf16[128,1024]{1,0:T(8,128)(2,1)S(1)} %pad_maximum_fusion.9), channel_id=1, source_target_pairs={{0,24},{2,26},{4,28},{6,30},{8,16},{10,18},{12,20},{14,22},{16,8},... | collective-permute-start | bytes 786440 | tf_op jit(solution)/shard_map/ppermute | solution.py:254
  101.5 1.7 %collective-permute-start.36 = (bf16[128,1024]{1,0:T(8,128)(2,1)S(1)}, bf16[128,1024]{1,0:T(8,128)(2,1)S(1)}, u32[]{:S(2)}, u32[]{:S(2)}) collective-permute-start(bf16[128,1024]{1,0:T(8,128)(2,1)S(1)} %pad_maximum_fusion.10), channel_id=1, source_target_pairs={{0,8},{2,10},{4,12},{6,14},{8,0},{10,2},{12,4},{14,6},{16,24},{18,... | collective-permute-start | bytes 786440 | tf_op jit(solution)/shard_map/ppermute | solution.py:254
  103.2 5.8 %collective-permute-done.37 = bf16[128,1024]{1,0:T(8,128)(2,1)S(1)} collective-permute-done((bf16[128,1024]{1,0:T(8,128)(2,1)S(1)}, bf16[128,1024]{1,0:T(8,128)(2,1)S(1)}, u32[]{:S(2)}, u32[]{:S(2)}) %collective-permute-start.37) | collective-permute-done | bytes 262176 | tf_op jit(solution)/shard_map/ppermute | solution.py:254
  109.0 1.7 %collective-permute-done.36 = bf16[128,1024]{1,0:T(8,128)(2,1)S(1)} collective-permute-done((bf16[128,1024]{1,0:T(8,128)(2,1)S(1)}, bf16[128,1024]{1,0:T(8,128)(2,1)S(1)}, u32[]{:S(2)}, u32[]{:S(2)}) %collective-permute-start.36) | collective-permute-done | bytes 262176 | tf_op jit(solution)/shard_map/ppermute | solution.py:254
  (108 shorter events, 29.9 us)
Async XLA Ops:
  1.8 16.4 %collective-permute-start.4 = (bf16[144,1024]{1,0:T(8,128)(2,1)}, bf16[144,1024]{1,0:T(8,128)(2,1)S(1)}, u32[]{:S(2)}, u32[]{:S(2)}) collective-permute-start(bf16[144,1024]{1,0:T(8,128)(2,1)} %shard_map.64.refs_0_), channel_id=1, source_target_pairs={{0,8},{2,10},{4,12},{6,14},{8,0},{10,2},{12,4},{14,6},{16,24},{18,... | collective-permute-start | bytes 884744 | tf_op jit(solution)/shard_map/ppermute | solution.py:254
  4.8 16.0 %collective-permute-start.3 = (bf16[144,1024]{1,0:T(8,128)(2,1)}, bf16[144,1024]{1,0:T(8,128)(2,1)S(1)}, u32[]{:S(2)}, u32[]{:S(2)}) collective-permute-start(bf16[144,1024]{1,0:T(8,128)(2,1)} %shard_map.64.refs_0_), channel_id=1, source_target_pairs={{0,16},{2,18},{4,20},{6,22},{8,24},{10,26},{12,28},{14,30},{16,0},... | collective-permute-start | bytes 884744 | tf_op jit(solution)/shard_map/ppermute | solution.py:254
  7.4 15.5 %collective-permute-start.1 = (bf16[144,1024]{1,0:T(8,128)(2,1)}, bf16[144,1024]{1,0:T(8,128)(2,1)S(1)}, u32[]{:S(2)}, u32[]{:S(2)}) collective-permute-start(bf16[144,1024]{1,0:T(8,128)(2,1)} %shard_map.64.refs_0_), channel_id=1, source_target_pairs={{0,4},{2,6},{4,0},{6,2},{8,12},{10,14},{12,8},{14,10},{16,20},{18,... | collective-permute-start | bytes 884744 | tf_op jit(solution)/shard_map/ppermute | solution.py:254
  8.9 14.0 %collective-permute-start.2 = (bf16[128,1024]{1,0:T(8,128)(2,1)S(1)}, bf16[128,1024]{1,0:T(8,128)(2,1)S(1)}, u32[]{:S(2)}, u32[]{:S(2)}) collective-permute-start(bf16[128,1024]{1,0:T(8,128)(2,1)S(1)} %copy-done.4), channel_id=1, source_target_pairs={{0,5},{1,4},{2,7},{3,6},{4,1},{5,0},{6,3},{7,2},{8,13},{9,12},{10,... | collective-permute-start | bytes 786440 | tf_op jit(solution)/shard_map/ppermute | solution.py:261
  10.3 12.6 %collective-permute-start = (bf16[128,1024]{1,0:T(8,128)(2,1)S(1)}, bf16[128,1024]{1,0:T(8,128)(2,1)S(1)}, u32[]{:S(2)}, u32[]{:S(2)}) collective-permute-start(bf16[128,1024]{1,0:T(8,128)(2,1)S(1)} %copy-done.4), channel_id=1, source_target_pairs={{0,1},{1,0},{2,3},{3,2},{4,5},{5,4},{6,7},{7,6},{8,9},{9,8},{10,11... | collective-permute-start | bytes 786440 | tf_op jit(solution)/shard_map/ppermute | solution.py:257
  20.8 20.7 %collective-permute-start.12 = (bf16[144,1024]{1,0:T(8,128)(2,1)S(1)}, bf16[144,1024]{1,0:T(8,128)(2,1)S(1)}, u32[]{:S(2)}, u32[]{:S(2)}) collective-permute-start(bf16[144,1024]{1,0:T(8,128)(2,1)S(1)} %collective-permute-done.3.refs_0_), channel_id=1, source_target_pairs={{0,8},{2,10},{4,12},{6,14},{8,0},{10,2},{12,4},{14,6},{16,24},{18,... | collective-permute-start | bytes 884744 | tf_op jit(solution)/shard_map/ppermute | solution.py:254
  21.4 6.9 %collective-permute-start.6 = (bf16[128,1024]{1,0:T(8,128)(2,1)S(1)}, bf16[128,1024]{1,0:T(8,128)(2,1)S(1)}, u32[]{:S(2)}, u32[]{:S(2)}) collective-permute-start(bf16[128,1024]{1,0:T(8,128)(2,1)S(1)} %pad_maximum_fusion.2), channel_id=1, source_target_pairs={{0,1},{1,0},{2,3},{3,2},{4,5},{5,4},{6,7},{7,6},{8,9},{9,8},{10,11... | collective-permute-start | bytes 786440 | tf_op jit(solution)/shard_map/ppermute | solution.py:257
  23.0 8.0 %collective-permute-start.7 = (bf16[160,1024]{1,0:T(8,128)(2,1)S(1)}, bf16[160,1024]{1,0:T(8,128)(2,1)S(1)}, u32[]{:S(2)}, u32[]{:S(2)}) collective-permute-start(bf16[160,1024]{1,0:T(8,128)(2,1)S(1)} %pad_maximum_fusion), channel_id=1, source_target_pairs={{0,4},{2,6},{4,0},{6,2},{8,12},{10,14},{12,8},{14,10},{16,20},{18,... | collective-permute-start | bytes 983048 | tf_op jit(solution)/shard_map/ppermute | solution.py:254
  26.6 8.3 %collective-permute-start.5 = (bf16[112,2048]{1,0:T(8,128)(2,1)S(1)}, bf16[112,2048]{1,0:T(8,128)(2,1)S(1)}, u32[]{:S(2)}, u32[]{:S(2)}) collective-permute-start(bf16[112,2048]{1,0:T(8,128)(2,1)S(1)} %get-tuple-element.117), channel_id=1, source_target_pairs={{0,2},{2,0},{4,6},{6,4},{8,10},{10,8},{12,14},{14,12},{16,18},{18,... | collective-permute-start | bytes 1376264 | tf_op jit(solution)/shard_map/ppermute | solution.py:254
  31.1 7.0 %collective-permute-start.9 = (bf16[128,1024]{1,0:T(8,128)(2,1)S(1)}, bf16[128,1024]{1,0:T(8,128)(2,1)S(1)}, u32[]{:S(2)}, u32[]{:S(2)}) collective-permute-start(bf16[128,1024]{1,0:T(8,128)(2,1)S(1)} %pad_maximum_fusion.3), channel_id=1, source_target_pairs={{0,4},{2,6},{4,0},{6,2},{8,12},{10,14},{12,8},{14,10},{16,20},{18,... | collective-permute-start | bytes 786440 | tf_op jit(solution)/shard_map/ppermute | solution.py:254
  32.7 6.4 %collective-permute-start.10 = (bf16[128,1024]{1,0:T(8,128)(2,1)S(1)}, bf16[128,1024]{1,0:T(8,128)(2,1)S(1)}, u32[]{:S(2)}, u32[]{:S(2)}) collective-permute-start(bf16[128,1024]{1,0:T(8,128)(2,1)S(1)} %pad_maximum_fusion.4), channel_id=1, source_target_pairs={{0,1},{1,0},{2,3},{3,2},{4,5},{5,4},{6,7},{7,6},{8,9},{9,8},{10,11... | collective-permute-start | bytes 786440 | tf_op jit(solution)/shard_map/ppermute | solution.py:257
  33.4 8.1 %collective-permute-start.13 = (bf16[144,1024]{1,0:T(8,128)(2,1)S(1)}, bf16[144,1024]{1,0:T(8,128)(2,1)S(1)}, u32[]{:S(2)}, u32[]{:S(2)}) collective-permute-start(bf16[144,1024]{1,0:T(8,128)(2,1)S(1)} %pad_maximum_fusion.1), channel_id=1, source_target_pairs={{0,8},{2,10},{4,12},{6,14},{8,0},{10,2},{12,4},{14,6},{16,24},{18,... | collective-permute-start | bytes 884744 | tf_op jit(solution)/shard_map/ppermute | solution.py:254
  40.3 11.1 %collective-permute-start.17 = (bf16[128,1024]{1,0:T(8,128)(2,1)S(1)}, bf16[128,1024]{1,0:T(8,128)(2,1)S(1)}, u32[]{:S(2)}, u32[]{:S(2)}) collective-permute-start(bf16[128,1024]{1,0:T(8,128)(2,1)S(1)} %pad_maximum_fusion.7), channel_id=1, source_target_pairs={{0,4},{2,6},{4,0},{6,2},{8,12},{10,14},{12,8},{14,10},{16,20},{18,... | collective-permute-start | bytes 786440 | tf_op jit(solution)/shard_map/ppermute | solution.py:254
  40.9 10.5 %collective-permute-start.18 = (bf16[128,1024]{1,0:T(8,128)(2,1)S(1)}, bf16[128,1024]{1,0:T(8,128)(2,1)S(1)}, u32[]{:S(2)}, u32[]{:S(2)}) collective-permute-start(bf16[128,1024]{1,0:T(8,128)(2,1)S(1)} %pad_maximum_fusion.8), channel_id=1, source_target_pairs={{0,1},{1,0},{2,3},{3,2},{4,5},{5,4},{6,7},{7,6},{8,9},{9,8},{10,11... | collective-permute-start | bytes 786440 | tf_op jit(solution)/shard_map/ppermute | solution.py:257
  41.5 5.6 %collective-permute-start.8 = (bf16[112,2048]{1,0:T(8,128)(2,1)S(1)}, bf16[112,2048]{1,0:T(8,128)(2,1)S(1)}, u32[]{:S(2)}, u32[]{:S(2)}) collective-permute-start(bf16[112,2048]{1,0:T(8,128)(2,1)S(1)} %get-tuple-element.125), channel_id=1, source_target_pairs={{0,2},{2,0},{4,6},{6,4},{8,10},{10,8},{12,14},{14,12},{16,18},{18,... | collective-permute-start | bytes 1376264 | tf_op jit(solution)/shard_map/ppermute | solution.py:254
  45.5 9.6 %collective-permute-start.15 = (bf16[128,1024]{1,0:T(8,128)(2,1)S(1)}, bf16[128,1024]{1,0:T(8,128)(2,1)S(1)}, u32[]{:S(2)}, u32[]{:S(2)}) collective-permute-start(bf16[128,1024]{1,0:T(8,128)(2,1)S(1)} %pad_maximum_fusion.5), channel_id=1, source_target_pairs={{0,4},{2,6},{4,0},{6,2},{8,12},{10,14},{12,8},{14,10},{16,20},{18,... | collective-permute-start | bytes 786440 | tf_op jit(solution)/shard_map/ppermute | solution.py:254
  47.2 8.0 %collective-permute-start.16 = (bf16[128,1024]{1,0:T(8,128)(2,1)S(1)}, bf16[128,1024]{1,0:T(8,128)(2,1)S(1)}, u32[]{:S(2)}, u32[]{:S(2)}) collective-permute-start(bf16[128,1024]{1,0:T(8,128)(2,1)S(1)} %pad_maximum_fusion.6), channel_id=1, source_target_pairs={{0,1},{1,0},{2,3},{3,2},{4,5},{5,4},{6,7},{7,6},{8,9},{9,8},{10,11... | collective-permute-start | bytes 786440 | tf_op jit(solution)/shard_map/ppermute | solution.py:257
  49.7 16.3 %collective-permute-start.14 = (bf16[256,1024]{1,0:T(8,128)(2,1)S(1)}, bf16[256,1024]{1,0:T(8,128)(2,1)S(1)}, u32[]{:S(2)}, u32[]{:S(2)}) collective-permute-start(bf16[256,1024]{1,0:T(8,128)(2,1)S(1)} %get-tuple-element.143), channel_id=1, source_target_pairs={{0,4},{2,6},{4,0},{6,2},{8,12},{10,14},{12,8},{14,10},{16,20},{18,... | collective-permute-start | bytes 1572872 | tf_op jit(solution)/shard_map/ppermute | solution.py:254
  52.5 5.2 %collective-permute-start.21 = (bf16[112,2048]{1,0:T(8,128)(2,1)S(1)}, bf16[112,2048]{1,0:T(8,128)(2,1)S(1)}, u32[]{:S(2)}, u32[]{:S(2)}) collective-permute-start(bf16[112,2048]{1,0:T(8,128)(2,1)S(1)} %get-tuple-element.164), channel_id=1, source_target_pairs={{0,2},{2,0},{4,6},{6,4},{8,10},{10,8},{12,14},{14,12},{16,18},{18,... | collective-permute-start | bytes 1376264 | tf_op jit(solution)/shard_map/ppermute | solution.py:254
  56.3 14.8 %collective-permute-start.27 = (bf16[256,1024]{1,0:T(8,128)(2,1)S(1)}, bf16[256,1024]{1,0:T(8,128)(2,1)S(1)}, u32[]{:S(2)}, u32[]{:S(2)}) collective-permute-start(bf16[256,1024]{1,0:T(8,128)(2,1)S(1)} %get-tuple-element.188), channel_id=1, source_target_pairs={{0,1},{1,0},{2,3},{3,2},{4,5},{5,4},{6,7},{7,6},{8,9},{9,8},{10,11... | collective-permute-start | bytes 1572872 | tf_op jit(solution)/shard_map/ppermute | solution.py:257
  66.2 37.0 %collective-permute-start.22 = (bf16[128,1024]{1,0:T(8,128)(2,1)S(1)}, bf16[128,1024]{1,0:T(8,128)(2,1)S(1)}, u32[]{:S(2)}, u32[]{:S(2)}) collective-permute-start(bf16[128,1024]{1,0:T(8,128)(2,1)S(1)} %get-tuple-element.215), channel_id=1, source_target_pairs={{0,1},{1,0},{2,3},{3,2},{4,5},{5,4},{6,7},{7,6},{8,9},{9,8},{10,11... | collective-permute-start | bytes 786440 | tf_op jit(solution)/shard_map/ppermute | solution.py:257
  71.1 9.2 %collective-permute-start.29 = (bf16[128,1024]{1,0:T(8,128)(2,1)S(1)}, bf16[128,1024]{1,0:T(8,128)(2,1)S(1)}, u32[]{:S(2)}, u32[]{:S(2)}) collective-permute-start(bf16[128,1024]{1,0:T(8,128)(2,1)S(1)} %get-tuple-element.192), channel_id=1, source_target_pairs={{0,4},{2,6},{4,0},{6,2},{8,12},{10,14},{12,8},{14,10},{16,20},{18,... | collective-permute-start | bytes 786440 | tf_op jit(solution)/shard_map/ppermute | solution.py:254
  72.5 9.9 %collective-permute-start.30 = (bf16[128,1024]{1,0:T(8,128)(2,1)S(1)}, bf16[128,1024]{1,0:T(8,128)(2,1)S(1)}, u32[]{:S(2)}, u32[]{:S(2)}) collective-permute-start(bf16[128,1024]{1,0:T(8,128)(2,1)S(1)} %get-tuple-element.193), channel_id=1, source_target_pairs={{0,1},{1,0},{2,3},{3,2},{4,5},{5,4},{6,7},{7,6},{8,9},{9,8},{10,11... | collective-permute-start | bytes 786440 | tf_op jit(solution)/shard_map/ppermute | solution.py:257
  73.8 12.2 %collective-permute-start.28 = (bf16[128,1024]{1,0:T(8,128)(2,1)S(1)}, bf16[128,1024]{1,0:T(8,128)(2,1)S(1)}, u32[]{:S(2)}, u32[]{:S(2)}) collective-permute-start(bf16[128,1024]{1,0:T(8,128)(2,1)S(1)} %get-tuple-element.217), channel_id=1, source_target_pairs={{0,4},{2,6},{4,0},{6,2},{8,12},{10,14},{12,8},{14,10},{16,20},{18,... | collective-permute-start | bytes 786440 | tf_op jit(solution)/shard_map/ppermute | solution.py:254
  74.8 15.0 %collective-permute-start.25 = (bf16[128,1024]{1,0:T(8,128)(2,1)S(1)}, bf16[128,1024]{1,0:T(8,128)(2,1)S(1)}, u32[]{:S(2)}, u32[]{:S(2)}) collective-permute-start(bf16[128,1024]{1,0:T(8,128)(2,1)S(1)} %get-tuple-element.186), channel_id=1, source_target_pairs={{0,4},{2,6},{4,0},{6,2},{8,12},{10,14},{12,8},{14,10},{16,20},{18,... | collective-permute-start | bytes 786440 | tf_op jit(solution)/shard_map/ppermute | solution.py:254
  80.4 9.4 %collective-permute-start.26 = (bf16[128,1024]{1,0:T(8,128)(2,1)S(1)}, bf16[128,1024]{1,0:T(8,128)(2,1)S(1)}, u32[]{:S(2)}, u32[]{:S(2)}) collective-permute-start(bf16[128,1024]{1,0:T(8,128)(2,1)S(1)} %get-tuple-element.187), channel_id=1, source_target_pairs={{0,1},{1,0},{2,3},{3,2},{4,5},{5,4},{6,7},{7,6},{8,9},{9,8},{10,11... | collective-permute-start | bytes 786440 | tf_op jit(solution)/shard_map/ppermute | solution.py:257
  86.0 14.6 %collective-permute-start.33 = (bf16[128,1024]{1,0:T(8,128)(2,1)S(1)}, bf16[128,1024]{1,0:T(8,128)(2,1)S(1)}, u32[]{:S(2)}, u32[]{:S(2)}) collective-permute-start(bf16[128,1024]{1,0:T(8,128)(2,1)S(1)} %add_convert_fusion.7), channel_id=1, source_target_pairs={{0,16},{2,18},{4,20},{6,22},{8,24},{10,26},{12,28},{14,30},{16,0},... | collective-permute-start | bytes 786440 | tf_op jit(solution)/shard_map/ppermute | solution.py:254
  89.9 10.8 %collective-permute-start.31 = (bf16[64,1024]{1,0:T(8,128)(2,1)S(1)}, bf16[64,1024]{1,0:T(8,128)(2,1)S(1)}, u32[]{:S(2)}, u32[]{:S(2)}) collective-permute-start(bf16[64,1024]{1,0:T(8,128)(2,1)S(1)} %get-tuple-element.229), channel_id=1, source_target_pairs={{0,1},{1,0},{2,3},{3,2},{4,5},{5,4},{6,7},{7,6},{8,9},{9,8},{10,11... | collective-permute-start | bytes 393224 | tf_op jit(solution)/shard_map/ppermute | solution.py:257
  91.2 5.2 %collective-permute-start.34 = (bf16[64,1024]{1,0:T(8,128)(2,1)S(1)}, bf16[64,1024]{1,0:T(8,128)(2,1)S(1)}, u32[]{:S(2)}, u32[]{:S(2)}) collective-permute-start(bf16[64,1024]{1,0:T(8,128)(2,1)S(1)} %get-tuple-element.233), channel_id=1, source_target_pairs={{0,1},{1,0},{2,3},{3,2},{4,5},{5,4},{6,7},{7,6},{8,9},{9,8},{10,11... | collective-permute-start | bytes 393224 | tf_op jit(solution)/shard_map/ppermute | solution.py:257
  92.1 5.8 %collective-permute-start.35 = (bf16[64,1024]{1,0:T(8,128)(2,1)S(1)}, bf16[64,1024]{1,0:T(8,128)(2,1)S(1)}, u32[]{:S(2)}, u32[]{:S(2)}) collective-permute-start(bf16[64,1024]{1,0:T(8,128)(2,1)S(1)} %get-tuple-element.231), channel_id=1, source_target_pairs={{0,4},{2,6},{4,0},{6,2},{8,12},{10,14},{12,8},{14,10},{16,20},{18,... | collective-permute-start | bytes 393224 | tf_op jit(solution)/shard_map/ppermute | solution.py:254
  97.9 11.1 %collective-permute-start.37 = (bf16[128,1024]{1,0:T(8,128)(2,1)S(1)}, bf16[128,1024]{1,0:T(8,128)(2,1)S(1)}, u32[]{:S(2)}, u32[]{:S(2)}) collective-permute-start(bf16[128,1024]{1,0:T(8,128)(2,1)S(1)} %pad_maximum_fusion.9), channel_id=1, source_target_pairs={{0,24},{2,26},{4,28},{6,30},{8,16},{10,18},{12,20},{14,22},{16,8},... | collective-permute-start | bytes 786440 | tf_op jit(solution)/shard_map/ppermute | solution.py:254
  101.5 9.3 %collective-permute-start.36 = (bf16[128,1024]{1,0:T(8,128)(2,1)S(1)}, bf16[128,1024]{1,0:T(8,128)(2,1)S(1)}, u32[]{:S(2)}, u32[]{:S(2)}) collective-permute-start(bf16[128,1024]{1,0:T(8,128)(2,1)S(1)} %pad_maximum_fusion.10), channel_id=1, source_target_pairs={{0,8},{2,10},{4,12},{6,14},{8,0},{10,2},{12,4},{14,6},{16,24},{18,... | collective-permute-start | bytes 786440 | tf_op jit(solution)/shard_map/ppermute | solution.py:254
  (11 other events, 58.6 us)

commit v5 on v4

--- a/solution.py
+++ b/solution.py
@@ -9,11 +9,13 @@
 
 CORE, Y, NEAR, FAR = 1, 2, 4, 8
 VMEM_BYTES = 20 << 20
-ROUTE_FLOPS = 40_000_000_000
-PACK_FLOPS = 10_000_000_000
+ROUTE_FLOPS = 40000000000
+PACK_FLOPS = 3000000000
 MIX_FLOPS = 0
+REST_FLOPS = 0
+FFN_WEIGHT = 1
 FIRST_X = ("2",)
-ORDER = ["u1p", "gather12", "pack0", "gather2", "gather1", "expert0", "pack2", "gather3", "expert2", "mix0", "mix2", "pack1", "pack3", "expert31", "sum0", "mix3", "mix1", "sum2", "sum3", "out2", "sum1", "out3", "end2", "out1", "out0"]
+ORDER = ["u1p", "gather12", "pack0", "gather2", "gather1", "expert0", "pack2", "gather3", "expert2", "mix0", "mix2", "pack1", "pack3", "expert31", "sum0", "tops2", "tops3", "mix3", "mix1", "sum2", "sum3", "out2", "sum1", "out3", "end2", "out1", "out0"]
 F32, BF16 = jnp.float32, jnp.bfloat16
 
 
@@ -201,7 +203,7 @@
         functools.partial(ffn_kernel, count),
         (jax.ShapeDtypeStruct((n, width), BF16),) * count,
         count + 3,
-        count * n * width * ff,
+        FFN_WEIGHT * count * n * width * ff,
         0,
         scratch=(pltpu.VMEM((count * n, width), BF16), pltpu.VMEM((count * n, ff), BF16)),
     )(place, *inputs, w_gate, w_up, w_down)
@@ -303,7 +305,7 @@
     )
 
     def pack(key, units, layout, routes):
-        own, send, table = dispatch(place, take(*units), layout, routes, capacity, tok_rows, wide, PACK_FLOPS if key == "0" else 0)
+        own, send, table = dispatch(place, take(*units), layout, routes, capacity, tok_rows, wide, PACK_FLOPS if key == "0" else REST_FLOPS)
         put(**{"own" + key: own, "table" + key: table})
         held["other" + key] = hop(send, CORE)
 

time: 112 us -> 111 us (level)
  starting transfers between devices: 42.3 us -> 39.7 us
  waiting for transfers between devices: 43.6 us -> 45.4 us
    ppermute x26, starting transfers between devices: 29.5 us -> 25.4 us  [hop(): return lax.ppermute(value, 'wide', [(i, i ^ bit) for i in range(wide)])]
    ppermute x11, waiting for transfers between devices: 8.08 us -> 10.2 us  [hop_x(): return lax.ppermute(value, 'narrow', [(0, 1), (1, 0)])]
where the time goes in v5:
time: 111 us
  waiting for transfers between devices  45.4 us (41%)
  starting transfers between devices  39.7 us (36%)
  Pallas kernels  22 us (20%)
  other arithmetic  2.06 us (2%)
  local copies, waits for them, and re-layouts  1.3 us (1%)
    ppermute x26, waiting for transfers between devices, hop(): return lax.ppermute(value, 'wide', [(i, i ^ bit) for i in range(wide)])  35.2 us
    ppermute x26, starting transfers between devices, hop(): return lax.ppermute(value, 'wide', [(i, i ^ bit) for i in range(wide)])  25.4 us
    ppermute x11, starting transfers between devices, hop_x(): return lax.ppermute(value, 'narrow', [(0, 1), (1, 0)])  11.8 us
    pallas_call x3, Pallas kernels, ffn(): kernel_call(functools.partial(ffn_kernel, count), (jax.ShapeDtypeStruct((...  11.4 us
    ppermute x11, waiting for transfers between devices, hop_x(): return lax.ppermute(value, 'narrow', [(0, 1), (1, 0)])  10.2 us
    pallas_call x4, Pallas kernels, combine(): kernel_call(functools.partial(combine_kernel, capacity, layouts), tuple((...  4.56 us
    pallas_call x4, Pallas kernels, dispatch(): kernel_call(functools.partial(dispatch_kernel, capacity, toks, layout, ro...  4.26 us
    ppermute x1, starting transfers between devices, hop_xy(): return lax.ppermute(value, ('wide', 'narrow'), pairs)  2.45 us
  transfers between devices with their start and end apart: 38, of which 19 were waited for; matrix products, arithmetic and copies ran while one was open for 1% of the time, Pallas kernels for 18%

profile of v5, /device:TPU:0, one launch (start us, length us, event | category | flops | bytes accessed | tf_op | source)
XLA Modules:
  0.0 110.9 jit_solution(5144470518846516389)
XLA Ops:
  0.0 1.8 %shard_map.64.refs_0_ = bf16[144,1024]{1,0:T(8,128)(2,1)} custom-call(s32[6,128]{1,0:T(8,128)} %bitcast.4, bf16[6,128]{1,0:T(8,128)(2,1)} %bitcast.5, bf16[128,1024]{1,0:T(8,128)(2,1)} %tokens_ref.1), custom_call_target="tpu_custom_call" | custom-call | flops 40000000000 | bytes 65536 | tf_op jit(solution)/shard_map/pallas_call | solution.py:94
  1.8 3.0 %collective-permute-start.4 = (bf16[144,1024]{1,0:T(8,128)(2,1)}, bf16[144,1024]{1,0:T(8,128)(2,1)S(1)}, u32[]{:S(2)}, u32[]{:S(2)}) collective-permute-start(bf16[144,1024]{1,0:T(8,128)(2,1)} %shard_map.64.refs_0_), channel_id=1, source_target_pairs={{0,8},{2,10},{4,12},{6,14},{8,0},{10,2},{12,4},{14,6},{16,24},{18,... | collective-permute-start | bytes 884744 | tf_op jit(solution)/shard_map/ppermute | solution.py:256
  4.8 2.6 %collective-permute-start.3 = (bf16[144,1024]{1,0:T(8,128)(2,1)}, bf16[144,1024]{1,0:T(8,128)(2,1)S(1)}, u32[]{:S(2)}, u32[]{:S(2)}) collective-permute-start(bf16[144,1024]{1,0:T(8,128)(2,1)} %shard_map.64.refs_0_), channel_id=1, source_target_pairs={{0,16},{2,18},{4,20},{6,22},{8,24},{10,26},{12,28},{14,30},{16,0},... | collective-permute-start | bytes 884744 | tf_op jit(solution)/shard_map/ppermute | solution.py:256
  7.4 2.4 %collective-permute-start.2 = (bf16[128,1024]{1,0:T(8,128)(2,1)S(1)}, bf16[128,1024]{1,0:T(8,128)(2,1)S(1)}, u32[]{:S(2)}, u32[]{:S(2)}) collective-permute-start(bf16[128,1024]{1,0:T(8,128)(2,1)S(1)} %copy-done.4), channel_id=1, source_target_pairs={{0,5},{1,4},{2,7},{3,6},{4,1},{5,0},{6,3},{7,2},{8,13},{9,12},{10,... | collective-permute-start | bytes 786440 | tf_op jit(solution)/shard_map/ppermute | solution.py:263
  11.0 7.2 %collective-permute-done.4.refs_0_ = bf16[144,1024]{1,0:T(8,128)(2,1)S(1)} collective-permute-done((bf16[144,1024]{1,0:T(8,128)(2,1)}, bf16[144,1024]{1,0:T(8,128)(2,1)S(1)}, u32[]{:S(2)}, u32[]{:S(2)}) %collective-permute-start.4) | collective-permute-done | bytes 294944 | tf_op jit(solution)/shard_map/ppermute | solution.py:256
  18.2 2.6 %collective-permute-done.3.refs_0_ = bf16[144,1024]{1,0:T(8,128)(2,1)S(1)} collective-permute-done((bf16[144,1024]{1,0:T(8,128)(2,1)}, bf16[144,1024]{1,0:T(8,128)(2,1)S(1)}, u32[]{:S(2)}, u32[]{:S(2)}) %collective-permute-start.3) | collective-permute-done | bytes 294944 | tf_op jit(solution)/shard_map/ppermute | solution.py:256
  21.4 1.6 %collective-permute-start.7 = (bf16[160,1024]{1,0:T(8,128)(2,1)S(1)}, bf16[160,1024]{1,0:T(8,128)(2,1)S(1)}, u32[]{:S(2)}, u32[]{:S(2)}) collective-permute-start(bf16[160,1024]{1,0:T(8,128)(2,1)S(1)} %pad_maximum_fusion), channel_id=1, source_target_pairs={{0,4},{2,6},{4,0},{6,2},{8,12},{10,14},{12,8},{14,10},{16,20},{18,... | collective-permute-start | bytes 983048 | tf_op jit(solution)/shard_map/ppermute | solution.py:256
  23.0 1.6 %collective-permute-start.6 = (bf16[128,1024]{1,0:T(8,128)(2,1)S(1)}, bf16[128,1024]{1,0:T(8,128)(2,1)S(1)}, u32[]{:S(2)}, u32[]{:S(2)}) collective-permute-start(bf16[128,1024]{1,0:T(8,128)(2,1)S(1)} %pad_maximum_fusion.2), channel_id=1, source_target_pairs={{0,1},{1,0},{2,3},{3,2},{4,5},{5,4},{6,7},{7,6},{8,9},{9,8},{10,11... | collective-permute-start | bytes 786440 | tf_op jit(solution)/shard_map/ppermute | solution.py:259
  26.7 2.9 %collective-permute-done.6.refs_1_ = bf16[128,1024]{1,0:T(8,128)(2,1)S(1)} collective-permute-done((bf16[128,1024]{1,0:T(8,128)(2,1)S(1)}, bf16[128,1024]{1,0:T(8,128)(2,1)S(1)}, u32[]{:S(2)}, u32[]{:S(2)}) %collective-permute-start.6) | collective-permute-done | bytes 262176 | tf_op jit(solution)/shard_map/ppermute | solution.py:259
  29.8 1.6 %collective-permute-start.9 = (bf16[128,1024]{1,0:T(8,128)(2,1)S(1)}, bf16[128,1024]{1,0:T(8,128)(2,1)S(1)}, u32[]{:S(2)}, u32[]{:S(2)}) collective-permute-start(bf16[128,1024]{1,0:T(8,128)(2,1)S(1)} %pad_maximum_fusion.3), channel_id=1, source_target_pairs={{0,4},{2,6},{4,0},{6,2},{8,12},{10,14},{12,8},{14,10},{16,20},{18,... | collective-permute-start | bytes 786440 | tf_op jit(solution)/shard_map/ppermute | solution.py:256
  31.4 1.6 %collective-permute-start.10 = (bf16[128,1024]{1,0:T(8,128)(2,1)S(1)}, bf16[128,1024]{1,0:T(8,128)(2,1)S(1)}, u32[]{:S(2)}, u32[]{:S(2)}) collective-permute-start(bf16[128,1024]{1,0:T(8,128)(2,1)S(1)} %pad_maximum_fusion.4), channel_id=1, source_target_pairs={{0,1},{1,0},{2,3},{3,2},{4,5},{5,4},{6,7},{7,6},{8,9},{9,8},{10,11... | collective-permute-start | bytes 786440 | tf_op jit(solution)/shard_map/ppermute | solution.py:259
  34.0 3.2 %shard_map.66 = (bf16[112,2048]{1,0:T(8,128)(2,1)S(1)}, bf16[112,2048]{1,0:T(8,128)(2,1)S(1)}) custom-call(s32[2]{0:T(128)S(1)} %pad_add_fusion.place_ref, bf16[112,2048]{1,0:T(8,128)(2,1)S(1)} %get-tuple-element.122.refs_0_, bf16[112,2048]{1,0:T(8,128)(2,1)S(1)} %collective-permute-done.5.refs_1_, bf16[1,704,2048]{2,1,0:T(8,128)(2,1)S(1)} %copy-done, ...), custom_call_target="tpu_custom_call" | custom-call | flops 322961408 | tf_op jit(solution)/shard_map/pallas_call | solution.py:202
  39.6 1.6 %collective-permute-start.18 = (bf16[128,1024]{1,0:T(8,128)(2,1)S(1)}, bf16[128,1024]{1,0:T(8,128)(2,1)S(1)}, u32[]{:S(2)}, u32[]{:S(2)}) collective-permute-start(bf16[128,1024]{1,0:T(8,128)(2,1)S(1)} %pad_maximum_fusion.8), channel_id=1, source_target_pairs={{0,1},{1,0},{2,3},{3,2},{4,5},{5,4},{6,7},{7,6},{8,9},{9,8},{10,11... | collective-permute-start | bytes 786440 | tf_op jit(solution)/shard_map/ppermute | solution.py:259
  41.2 3.2 %shard_map.68 = (bf16[112,2048]{1,0:T(8,128)(2,1)S(1)}, bf16[112,2048]{1,0:T(8,128)(2,1)S(1)}) custom-call(s32[2]{0:T(128)S(1)} %pad_add_fusion.place_ref, bf16[112,2048]{1,0:T(8,128)(2,1)S(1)} %get-tuple-element.136.refs_0_, bf16[112,2048]{1,0:T(8,128)(2,1)S(1)} %collective-permute-done.11.refs_1_, bf16[1,704,2048]{2,1,0:T(8,128)(2,1)S(1)} %copy-done, ...), custom_call_target="tpu_custom_call" | custom-call | flops 322961408 | tf_op jit(solution)/shard_map/pallas_call | solution.py:202
  45.0 1.6 %collective-permute-start.15 = (bf16[128,1024]{1,0:T(8,128)(2,1)S(1)}, bf16[128,1024]{1,0:T(8,128)(2,1)S(1)}, u32[]{:S(2)}, u32[]{:S(2)}) collective-permute-start(bf16[128,1024]{1,0:T(8,128)(2,1)S(1)} %pad_maximum_fusion.5), channel_id=1, source_target_pairs={{0,4},{2,6},{4,0},{6,2},{8,12},{10,14},{12,8},{14,10},{16,20},{18,... | collective-permute-start | bytes 786440 | tf_op jit(solution)/shard_map/ppermute | solution.py:256
  51.4 2.8 %collective-permute-done.15.refs_2_ = bf16[128,1024]{1,0:T(8,128)(2,1)S(1)} collective-permute-done((bf16[128,1024]{1,0:T(8,128)(2,1)S(1)}, bf16[128,1024]{1,0:T(8,128)(2,1)S(1)}, u32[]{:S(2)}, u32[]{:S(2)}) %collective-permute-start.15) | collective-permute-done | bytes 262176 | tf_op jit(solution)/shard_map/ppermute | solution.py:256
  57.6 5.0 %shard_map.73 = (bf16[112,2048]{1,0:T(8,128)(2,1)S(1)}, bf16[112,2048]{1,0:T(8,128)(2,1)S(1)}, bf16[112,2048]{1,0:T(8,128)(2,1)S(1)}, bf16[112,2048]{1,0:T(8,128)(2,1)S(1)}) custom-call(s32[2]{0:T(128)S(1)} %pad_add_fusion.place_ref, bf16[112,2048]{1,0:T(8,128)(2,1)S(1)} %get-tuple-element.165.refs_0_, bf16[112,2048]{1,0:T(8,128)(2,1)S(1)} %get-tuple-element.166.refs_1_, ...), custom_call_target="tpu_custom_call" | custom-call | flops 645922816 | tf_op jit(solution)/shard_map/pallas_call | solution.py:202
  63.2 1.4 %collective-permute-done.14 = bf16[256,1024]{1,0:T(8,128)(2,1)S(1)} collective-permute-done((bf16[256,1024]{1,0:T(8,128)(2,1)S(1)}, bf16[256,1024]{1,0:T(8,128)(2,1)S(1)}, u32[]{:S(2)}, u32[]{:S(2)}) %collective-permute-start.14) | collective-permute-done | bytes 524320 | tf_op jit(solution)/shard_map/ppermute | solution.py:256
  64.9 1.6 %collective-permute-start.22 = (bf16[128,1024]{1,0:T(8,128)(2,1)S(1)}, bf16[128,1024]{1,0:T(8,128)(2,1)S(1)}, u32[]{:S(2)}, u32[]{:S(2)}) collective-permute-start(bf16[128,1024]{1,0:T(8,128)(2,1)S(1)} %get-tuple-element.215), channel_id=1, source_target_pairs={{0,1},{1,0},{2,3},{3,2},{4,5},{5,4},{6,7},{7,6},{8,9},{9,8},{10,11... | collective-permute-start | bytes 786440 | tf_op jit(solution)/shard_map/ppermute | solution.py:259
  68.7 1.8 %collective-permute-done.27 = bf16[256,1024]{1,0:T(8,128)(2,1)S(1)} collective-permute-done((bf16[256,1024]{1,0:T(8,128)(2,1)S(1)}, bf16[256,1024]{1,0:T(8,128)(2,1)S(1)}, u32[]{:S(2)}, u32[]{:S(2)}) %collective-permute-start.27) | collective-permute-done | bytes 524320 | tf_op jit(solution)/shard_map/ppermute | solution.py:259
  73.6 1.4 %collective-permute-start.25 = (bf16[128,1024]{1,0:T(8,128)(2,1)S(1)}, bf16[128,1024]{1,0:T(8,128)(2,1)S(1)}, u32[]{:S(2)}, u32[]{:S(2)}) collective-permute-start(bf16[128,1024]{1,0:T(8,128)(2,1)S(1)} %get-tuple-element.186), channel_id=1, source_target_pairs={{0,4},{2,6},{4,0},{6,2},{8,12},{10,14},{12,8},{14,10},{16,20},{18,... | collective-permute-start | bytes 786440 | tf_op jit(solution)/shard_map/ppermute | solution.py:256
  75.0 4.8 %collective-permute-done.29 = bf16[128,1024]{1,0:T(8,128)(2,1)S(1)} collective-permute-done((bf16[128,1024]{1,0:T(8,128)(2,1)S(1)}, bf16[128,1024]{1,0:T(8,128)(2,1)S(1)}, u32[]{:S(2)}, u32[]{:S(2)}) %collective-permute-start.29) | collective-permute-done | bytes 262176 | tf_op jit(solution)/shard_map/ppermute | solution.py:256
  80.5 1.3 %collective-permute-done.30 = bf16[128,1024]{1,0:T(8,128)(2,1)S(1)} collective-permute-done((bf16[128,1024]{1,0:T(8,128)(2,1)S(1)}, bf16[128,1024]{1,0:T(8,128)(2,1)S(1)}, u32[]{:S(2)}, u32[]{:S(2)}) %collective-permute-start.30) | collective-permute-done | bytes 262176 | tf_op jit(solution)/shard_map/ppermute | solution.py:259
  81.9 3.5 %collective-permute-done.28 = bf16[128,1024]{1,0:T(8,128)(2,1)S(1)} collective-permute-done((bf16[128,1024]{1,0:T(8,128)(2,1)S(1)}, bf16[128,1024]{1,0:T(8,128)(2,1)S(1)}, u32[]{:S(2)}, u32[]{:S(2)}) %collective-permute-start.28) | collective-permute-done | bytes 262176 | tf_op jit(solution)/shard_map/ppermute | solution.py:256
  85.5 2.1 %collective-permute-start.33 = (bf16[128,1024]{1,0:T(8,128)(2,1)S(1)}, bf16[128,1024]{1,0:T(8,128)(2,1)S(1)}, u32[]{:S(2)}, u32[]{:S(2)}) collective-permute-start(bf16[128,1024]{1,0:T(8,128)(2,1)S(1)} %add_convert_fusion.7), channel_id=1, source_target_pairs={{0,16},{2,18},{4,20},{6,22},{8,24},{10,26},{12,28},{14,30},{16,0},... | collective-permute-start | bytes 786440 | tf_op jit(solution)/shard_map/ppermute | solution.py:256
  87.6 1.6 %collective-permute-done.25 = bf16[128,1024]{1,0:T(8,128)(2,1)S(1)} collective-permute-done((bf16[128,1024]{1,0:T(8,128)(2,1)S(1)}, bf16[128,1024]{1,0:T(8,128)(2,1)S(1)}, u32[]{:S(2)}, u32[]{:S(2)}) %collective-permute-start.25) | collective-permute-done | bytes 262176 | tf_op jit(solution)/shard_map/ppermute | solution.py:256
  90.0 1.4 %collective-permute-start.34 = (bf16[64,1024]{1,0:T(8,128)(2,1)S(1)}, bf16[64,1024]{1,0:T(8,128)(2,1)S(1)}, u32[]{:S(2)}, u32[]{:S(2)}) collective-permute-start(bf16[64,1024]{1,0:T(8,128)(2,1)S(1)} %get-tuple-element.233), channel_id=1, source_target_pairs={{0,1},{1,0},{2,3},{3,2},{4,5},{5,4},{6,7},{7,6},{8,9},{9,8},{10,11... | collective-permute-start | bytes 393224 | tf_op jit(solution)/shard_map/ppermute | solution.py:259
  92.8 3.1 %collective-permute-done.34 = bf16[64,1024]{1,0:T(8,128)(2,1)S(1)} collective-permute-done((bf16[64,1024]{1,0:T(8,128)(2,1)S(1)}, bf16[64,1024]{1,0:T(8,128)(2,1)S(1)}, u32[]{:S(2)}, u32[]{:S(2)}) %collective-permute-start.34) | collective-permute-done | bytes 131104 | tf_op jit(solution)/shard_map/ppermute | solution.py:259
  97.4 1.6 %collective-permute-start.37 = (bf16[128,1024]{1,0:T(8,128)(2,1)S(1)}, bf16[128,1024]{1,0:T(8,128)(2,1)S(1)}, u32[]{:S(2)}, u32[]{:S(2)}) collective-permute-start(bf16[128,1024]{1,0:T(8,128)(2,1)S(1)} %pad_maximum_fusion.9), channel_id=1, source_target_pairs={{0,24},{2,26},{4,28},{6,30},{8,16},{10,18},{12,20},{14,22},{16,8},... | collective-permute-start | bytes 786440 | tf_op jit(solution)/shard_map/ppermute | solution.py:256
  99.0 1.8 %collective-permute-done.32 = bf16[64,1024]{1,0:T(8,128)(2,1)S(1)} collective-permute-done((bf16[64,1024]{1,0:T(8,128)(2,1)S(1)}, bf16[64,1024]{1,0:T(8,128)(2,1)S(1)}, u32[]{:S(2)}, u32[]{:S(2)}) %collective-permute-start.32) | collective-permute-done | bytes 131104 | tf_op jit(solution)/shard_map/ppermute | solution.py:256
  102.0 5.7 %collective-permute-done.37 = bf16[128,1024]{1,0:T(8,128)(2,1)S(1)} collective-permute-done((bf16[128,1024]{1,0:T(8,128)(2,1)S(1)}, bf16[128,1024]{1,0:T(8,128)(2,1)S(1)}, u32[]{:S(2)}, u32[]{:S(2)}) %collective-permute-start.37) | collective-permute-done | bytes 262176 | tf_op jit(solution)/shard_map/ppermute | solution.py:256
  107.7 2.3 %collective-permute-done.36 = bf16[128,1024]{1,0:T(8,128)(2,1)S(1)} collective-permute-done((bf16[128,1024]{1,0:T(8,128)(2,1)S(1)}, bf16[128,1024]{1,0:T(8,128)(2,1)S(1)}, u32[]{:S(2)}, u32[]{:S(2)}) %collective-permute-start.36) | collective-permute-done | bytes 262176 | tf_op jit(solution)/shard_map/ppermute | solution.py:256
  (108 shorter events, 28.7 us)
Async XLA Ops:
  1.8 16.4 %collective-permute-start.4 = (bf16[144,1024]{1,0:T(8,128)(2,1)}, bf16[144,1024]{1,0:T(8,128)(2,1)S(1)}, u32[]{:S(2)}, u32[]{:S(2)}) collective-permute-start(bf16[144,1024]{1,0:T(8,128)(2,1)} %shard_map.64.refs_0_), channel_id=1, source_target_pairs={{0,8},{2,10},{4,12},{6,14},{8,0},{10,2},{12,4},{14,6},{16,24},{18,... | collective-permute-start | bytes 884744 | tf_op jit(solution)/shard_map/ppermute | solution.py:256
  4.8 16.0 %collective-permute-start.3 = (bf16[144,1024]{1,0:T(8,128)(2,1)}, bf16[144,1024]{1,0:T(8,128)(2,1)S(1)}, u32[]{:S(2)}, u32[]{:S(2)}) collective-permute-start(bf16[144,1024]{1,0:T(8,128)(2,1)} %shard_map.64.refs_0_), channel_id=1, source_target_pairs={{0,16},{2,18},{4,20},{6,22},{8,24},{10,26},{12,28},{14,30},{16,0},... | collective-permute-start | bytes 884744 | tf_op jit(solution)/shard_map/ppermute | solution.py:256
  7.4 15.6 %collective-permute-start.2 = (bf16[128,1024]{1,0:T(8,128)(2,1)S(1)}, bf16[128,1024]{1,0:T(8,128)(2,1)S(1)}, u32[]{:S(2)}, u32[]{:S(2)}) collective-permute-start(bf16[128,1024]{1,0:T(8,128)(2,1)S(1)} %copy-done.4), channel_id=1, source_target_pairs={{0,5},{1,4},{2,7},{3,6},{4,1},{5,0},{6,3},{7,2},{8,13},{9,12},{10,... | collective-permute-start | bytes 786440 | tf_op jit(solution)/shard_map/ppermute | solution.py:263
  9.8 14.7 %collective-permute-start = (bf16[128,1024]{1,0:T(8,128)(2,1)S(1)}, bf16[128,1024]{1,0:T(8,128)(2,1)S(1)}, u32[]{:S(2)}, u32[]{:S(2)}) collective-permute-start(bf16[128,1024]{1,0:T(8,128)(2,1)S(1)} %copy-done.4), channel_id=1, source_target_pairs={{0,1},{1,0},{2,3},{3,2},{4,5},{5,4},{6,7},{7,6},{8,9},{9,8},{10,11... | collective-permute-start | bytes 786440 | tf_op jit(solution)/shard_map/ppermute | solution.py:259
  10.4 14.2 %collective-permute-start.1 = (bf16[144,1024]{1,0:T(8,128)(2,1)}, bf16[144,1024]{1,0:T(8,128)(2,1)S(1)}, u32[]{:S(2)}, u32[]{:S(2)}) collective-permute-start(bf16[144,1024]{1,0:T(8,128)(2,1)} %shard_map.64.refs_0_), channel_id=1, source_target_pairs={{0,4},{2,6},{4,0},{6,2},{8,12},{10,14},{12,8},{14,10},{16,20},{18,... | collective-permute-start | bytes 884744 | tf_op jit(solution)/shard_map/ppermute | solution.py:256
  20.8 20.3 %collective-permute-start.12 = (bf16[144,1024]{1,0:T(8,128)(2,1)S(1)}, bf16[144,1024]{1,0:T(8,128)(2,1)S(1)}, u32[]{:S(2)}, u32[]{:S(2)}) collective-permute-start(bf16[144,1024]{1,0:T(8,128)(2,1)S(1)} %collective-permute-done.3.refs_0_), channel_id=1, source_target_pairs={{0,8},{2,10},{4,12},{6,14},{8,0},{10,2},{12,4},{14,6},{16,24},{18,... | collective-permute-start | bytes 884744 | tf_op jit(solution)/shard_map/ppermute | solution.py:256
  21.4 8.3 %collective-permute-start.7 = (bf16[160,1024]{1,0:T(8,128)(2,1)S(1)}, bf16[160,1024]{1,0:T(8,128)(2,1)S(1)}, u32[]{:S(2)}, u32[]{:S(2)}) collective-permute-start(bf16[160,1024]{1,0:T(8,128)(2,1)S(1)} %pad_maximum_fusion), channel_id=1, source_target_pairs={{0,4},{2,6},{4,0},{6,2},{8,12},{10,14},{12,8},{14,10},{16,20},{18,... | collective-permute-start | bytes 983048 | tf_op jit(solution)/shard_map/ppermute | solution.py:256
  23.0 6.6 %collective-permute-start.6 = (bf16[128,1024]{1,0:T(8,128)(2,1)S(1)}, bf16[128,1024]{1,0:T(8,128)(2,1)S(1)}, u32[]{:S(2)}, u32[]{:S(2)}) collective-permute-start(bf16[128,1024]{1,0:T(8,128)(2,1)S(1)} %pad_maximum_fusion.2), channel_id=1, source_target_pairs={{0,1},{1,0},{2,3},{3,2},{4,5},{5,4},{6,7},{7,6},{8,9},{9,8},{10,11... | collective-permute-start | bytes 786440 | tf_op jit(solution)/shard_map/ppermute | solution.py:259
  26.6 7.4 %collective-permute-start.5 = (bf16[112,2048]{1,0:T(8,128)(2,1)S(1)}, bf16[112,2048]{1,0:T(8,128)(2,1)S(1)}, u32[]{:S(2)}, u32[]{:S(2)}) collective-permute-start(bf16[112,2048]{1,0:T(8,128)(2,1)S(1)} %get-tuple-element.117), channel_id=1, source_target_pairs={{0,2},{2,0},{4,6},{6,4},{8,10},{10,8},{12,14},{14,12},{16,18},{18,... | collective-permute-start | bytes 1376264 | tf_op jit(solution)/shard_map/ppermute | solution.py:256
  29.8 7.4 %collective-permute-start.9 = (bf16[128,1024]{1,0:T(8,128)(2,1)S(1)}, bf16[128,1024]{1,0:T(8,128)(2,1)S(1)}, u32[]{:S(2)}, u32[]{:S(2)}) collective-permute-start(bf16[128,1024]{1,0:T(8,128)(2,1)S(1)} %pad_maximum_fusion.3), channel_id=1, source_target_pairs={{0,4},{2,6},{4,0},{6,2},{8,12},{10,14},{12,8},{14,10},{16,20},{18,... | collective-permute-start | bytes 786440 | tf_op jit(solution)/shard_map/ppermute | solution.py:256
  31.4 6.4 %collective-permute-start.10 = (bf16[128,1024]{1,0:T(8,128)(2,1)S(1)}, bf16[128,1024]{1,0:T(8,128)(2,1)S(1)}, u32[]{:S(2)}, u32[]{:S(2)}) collective-permute-start(bf16[128,1024]{1,0:T(8,128)(2,1)S(1)} %pad_maximum_fusion.4), channel_id=1, source_target_pairs={{0,1},{1,0},{2,3},{3,2},{4,5},{5,4},{6,7},{7,6},{8,9},{9,8},{10,11... | collective-permute-start | bytes 786440 | tf_op jit(solution)/shard_map/ppermute | solution.py:259
  33.0 8.2 %collective-permute-start.13 = (bf16[144,1024]{1,0:T(8,128)(2,1)S(1)}, bf16[144,1024]{1,0:T(8,128)(2,1)S(1)}, u32[]{:S(2)}, u32[]{:S(2)}) collective-permute-start(bf16[144,1024]{1,0:T(8,128)(2,1)S(1)} %pad_maximum_fusion.1), channel_id=1, source_target_pairs={{0,8},{2,10},{4,12},{6,14},{8,0},{10,2},{12,4},{14,6},{16,24},{18,... | collective-permute-start | bytes 884744 | tf_op jit(solution)/shard_map/ppermute | solution.py:256
  39.0 11.3 %collective-permute-start.17 = (bf16[128,1024]{1,0:T(8,128)(2,1)S(1)}, bf16[128,1024]{1,0:T(8,128)(2,1)S(1)}, u32[]{:S(2)}, u32[]{:S(2)}) collective-permute-start(bf16[128,1024]{1,0:T(8,128)(2,1)S(1)} %pad_maximum_fusion.7), channel_id=1, source_target_pairs={{0,4},{2,6},{4,0},{6,2},{8,12},{10,14},{12,8},{14,10},{16,20},{18,... | collective-permute-start | bytes 786440 | tf_op jit(solution)/shard_map/ppermute | solution.py:256
  39.6 10.7 %collective-permute-start.18 = (bf16[128,1024]{1,0:T(8,128)(2,1)S(1)}, bf16[128,1024]{1,0:T(8,128)(2,1)S(1)}, u32[]{:S(2)}, u32[]{:S(2)}) collective-permute-start(bf16[128,1024]{1,0:T(8,128)(2,1)S(1)} %pad_maximum_fusion.8), channel_id=1, source_target_pairs={{0,1},{1,0},{2,3},{3,2},{4,5},{5,4},{6,7},{7,6},{8,9},{9,8},{10,11... | collective-permute-start | bytes 786440 | tf_op jit(solution)/shard_map/ppermute | solution.py:259
  41.1 5.4 %collective-permute-start.8 = (bf16[112,2048]{1,0:T(8,128)(2,1)S(1)}, bf16[112,2048]{1,0:T(8,128)(2,1)S(1)}, u32[]{:S(2)}, u32[]{:S(2)}) collective-permute-start(bf16[112,2048]{1,0:T(8,128)(2,1)S(1)} %get-tuple-element.125), channel_id=1, source_target_pairs={{0,2},{2,0},{4,6},{6,4},{8,10},{10,8},{12,14},{14,12},{16,18},{18,... | collective-permute-start | bytes 1376264 | tf_op jit(solution)/shard_map/ppermute | solution.py:256
  45.0 9.2 %collective-permute-start.15 = (bf16[128,1024]{1,0:T(8,128)(2,1)S(1)}, bf16[128,1024]{1,0:T(8,128)(2,1)S(1)}, u32[]{:S(2)}, u32[]{:S(2)}) collective-permute-start(bf16[128,1024]{1,0:T(8,128)(2,1)S(1)} %pad_maximum_fusion.5), channel_id=1, source_target_pairs={{0,4},{2,6},{4,0},{6,2},{8,12},{10,14},{12,8},{14,10},{16,20},{18,... | collective-permute-start | bytes 786440 | tf_op jit(solution)/shard_map/ppermute | solution.py:256
  46.6 8.0 %collective-permute-start.16 = (bf16[128,1024]{1,0:T(8,128)(2,1)S(1)}, bf16[128,1024]{1,0:T(8,128)(2,1)S(1)}, u32[]{:S(2)}, u32[]{:S(2)}) collective-permute-start(bf16[128,1024]{1,0:T(8,128)(2,1)S(1)} %pad_maximum_fusion.6), channel_id=1, source_target_pairs={{0,1},{1,0},{2,3},{3,2},{4,5},{5,4},{6,7},{7,6},{8,9},{9,8},{10,11... | collective-permute-start | bytes 786440 | tf_op jit(solution)/shard_map/ppermute | solution.py:259
  48.4 16.3 %collective-permute-start.14 = (bf16[256,1024]{1,0:T(8,128)(2,1)S(1)}, bf16[256,1024]{1,0:T(8,128)(2,1)S(1)}, u32[]{:S(2)}, u32[]{:S(2)}) collective-permute-start(bf16[256,1024]{1,0:T(8,128)(2,1)S(1)} %get-tuple-element.143), channel_id=1, source_target_pairs={{0,4},{2,6},{4,0},{6,2},{8,12},{10,14},{12,8},{14,10},{16,20},{18,... | collective-permute-start | bytes 1572872 | tf_op jit(solution)/shard_map/ppermute | solution.py:256
  51.3 5.1 %collective-permute-start.21 = (bf16[112,2048]{1,0:T(8,128)(2,1)S(1)}, bf16[112,2048]{1,0:T(8,128)(2,1)S(1)}, u32[]{:S(2)}, u32[]{:S(2)}) collective-permute-start(bf16[112,2048]{1,0:T(8,128)(2,1)S(1)} %get-tuple-element.164), channel_id=1, source_target_pairs={{0,2},{2,0},{4,6},{6,4},{8,10},{10,8},{12,14},{14,12},{16,18},{18,... | collective-permute-start | bytes 1376264 | tf_op jit(solution)/shard_map/ppermute | solution.py:256
  55.8 14.8 %collective-permute-start.27 = (bf16[256,1024]{1,0:T(8,128)(2,1)S(1)}, bf16[256,1024]{1,0:T(8,128)(2,1)S(1)}, u32[]{:S(2)}, u32[]{:S(2)}) collective-permute-start(bf16[256,1024]{1,0:T(8,128)(2,1)S(1)} %get-tuple-element.188), channel_id=1, source_target_pairs={{0,1},{1,0},{2,3},{3,2},{4,5},{5,4},{6,7},{7,6},{8,9},{9,8},{10,11... | collective-permute-start | bytes 1572872 | tf_op jit(solution)/shard_map/ppermute | solution.py:259
  64.9 37.2 %collective-permute-start.22 = (bf16[128,1024]{1,0:T(8,128)(2,1)S(1)}, bf16[128,1024]{1,0:T(8,128)(2,1)S(1)}, u32[]{:S(2)}, u32[]{:S(2)}) collective-permute-start(bf16[128,1024]{1,0:T(8,128)(2,1)S(1)} %get-tuple-element.215), channel_id=1, source_target_pairs={{0,1},{1,0},{2,3},{3,2},{4,5},{5,4},{6,7},{7,6},{8,9},{9,8},{10,11... | collective-permute-start | bytes 786440 | tf_op jit(solution)/shard_map/ppermute | solution.py:259
  70.6 9.2 %collective-permute-start.29 = (bf16[128,1024]{1,0:T(8,128)(2,1)S(1)}, bf16[128,1024]{1,0:T(8,128)(2,1)S(1)}, u32[]{:S(2)}, u32[]{:S(2)}) collective-permute-start(bf16[128,1024]{1,0:T(8,128)(2,1)S(1)} %get-tuple-element.192), channel_id=1, source_target_pairs={{0,4},{2,6},{4,0},{6,2},{8,12},{10,14},{12,8},{14,10},{16,20},{18,... | collective-permute-start | bytes 786440 | tf_op jit(solution)/shard_map/ppermute | solution.py:256
  71.7 10.1 %collective-permute-start.30 = (bf16[128,1024]{1,0:T(8,128)(2,1)S(1)}, bf16[128,1024]{1,0:T(8,128)(2,1)S(1)}, u32[]{:S(2)}, u32[]{:S(2)}) collective-permute-start(bf16[128,1024]{1,0:T(8,128)(2,1)S(1)} %get-tuple-element.193), channel_id=1, source_target_pairs={{0,1},{1,0},{2,3},{3,2},{4,5},{5,4},{6,7},{7,6},{8,9},{9,8},{10,11... | collective-permute-start | bytes 786440 | tf_op jit(solution)/shard_map/ppermute | solution.py:259
  72.9 12.5 %collective-permute-start.28 = (bf16[128,1024]{1,0:T(8,128)(2,1)S(1)}, bf16[128,1024]{1,0:T(8,128)(2,1)S(1)}, u32[]{:S(2)}, u32[]{:S(2)}) collective-permute-start(bf16[128,1024]{1,0:T(8,128)(2,1)S(1)} %get-tuple-element.217), channel_id=1, source_target_pairs={{0,4},{2,6},{4,0},{6,2},{8,12},{10,14},{12,8},{14,10},{16,20},{18,... | collective-permute-start | bytes 786440 | tf_op jit(solution)/shard_map/ppermute | solution.py:256
  73.6 15.7 %collective-permute-start.25 = (bf16[128,1024]{1,0:T(8,128)(2,1)S(1)}, bf16[128,1024]{1,0:T(8,128)(2,1)S(1)}, u32[]{:S(2)}, u32[]{:S(2)}) collective-permute-start(bf16[128,1024]{1,0:T(8,128)(2,1)S(1)} %get-tuple-element.186), channel_id=1, source_target_pairs={{0,4},{2,6},{4,0},{6,2},{8,12},{10,14},{12,8},{14,10},{16,20},{18,... | collective-permute-start | bytes 786440 | tf_op jit(solution)/shard_map/ppermute | solution.py:256
  79.8 9.4 %collective-permute-start.26 = (bf16[128,1024]{1,0:T(8,128)(2,1)S(1)}, bf16[128,1024]{1,0:T(8,128)(2,1)S(1)}, u32[]{:S(2)}, u32[]{:S(2)}) collective-permute-start(bf16[128,1024]{1,0:T(8,128)(2,1)S(1)} %get-tuple-element.187), channel_id=1, source_target_pairs={{0,1},{1,0},{2,3},{3,2},{4,5},{5,4},{6,7},{7,6},{8,9},{9,8},{10,11... | collective-permute-start | bytes 786440 | tf_op jit(solution)/shard_map/ppermute | solution.py:259
  85.5 13.5 %collective-permute-start.33 = (bf16[128,1024]{1,0:T(8,128)(2,1)S(1)}, bf16[128,1024]{1,0:T(8,128)(2,1)S(1)}, u32[]{:S(2)}, u32[]{:S(2)}) collective-permute-start(bf16[128,1024]{1,0:T(8,128)(2,1)S(1)} %add_convert_fusion.7), channel_id=1, source_target_pairs={{0,16},{2,18},{4,20},{6,22},{8,24},{10,26},{12,28},{14,30},{16,0},... | collective-permute-start | bytes 786440 | tf_op jit(solution)/shard_map/ppermute | solution.py:256
  89.3 9.7 %collective-permute-start.31 = (bf16[64,1024]{1,0:T(8,128)(2,1)S(1)}, bf16[64,1024]{1,0:T(8,128)(2,1)S(1)}, u32[]{:S(2)}, u32[]{:S(2)}) collective-permute-start(bf16[64,1024]{1,0:T(8,128)(2,1)S(1)} %get-tuple-element.229), channel_id=1, source_target_pairs={{0,1},{1,0},{2,3},{3,2},{4,5},{5,4},{6,7},{7,6},{8,9},{9,8},{10,11... | collective-permute-start | bytes 393224 | tf_op jit(solution)/shard_map/ppermute | solution.py:259
  90.0 5.8 %collective-permute-start.34 = (bf16[64,1024]{1,0:T(8,128)(2,1)S(1)}, bf16[64,1024]{1,0:T(8,128)(2,1)S(1)}, u32[]{:S(2)}, u32[]{:S(2)}) collective-permute-start(bf16[64,1024]{1,0:T(8,128)(2,1)S(1)} %get-tuple-element.233), channel_id=1, source_target_pairs={{0,1},{1,0},{2,3},{3,2},{4,5},{5,4},{6,7},{7,6},{8,9},{9,8},{10,11... | collective-permute-start | bytes 393224 | tf_op jit(solution)/shard_map/ppermute | solution.py:259
  91.5 5.8 %collective-permute-start.35 = (bf16[64,1024]{1,0:T(8,128)(2,1)S(1)}, bf16[64,1024]{1,0:T(8,128)(2,1)S(1)}, u32[]{:S(2)}, u32[]{:S(2)}) collective-permute-start(bf16[64,1024]{1,0:T(8,128)(2,1)S(1)} %get-tuple-element.231), channel_id=1, source_target_pairs={{0,4},{2,6},{4,0},{6,2},{8,12},{10,14},{12,8},{14,10},{16,20},{18,... | collective-permute-start | bytes 393224 | tf_op jit(solution)/shard_map/ppermute | solution.py:256
  97.4 10.4 %collective-permute-start.37 = (bf16[128,1024]{1,0:T(8,128)(2,1)S(1)}, bf16[128,1024]{1,0:T(8,128)(2,1)S(1)}, u32[]{:S(2)}, u32[]{:S(2)}) collective-permute-start(bf16[128,1024]{1,0:T(8,128)(2,1)S(1)} %pad_maximum_fusion.9), channel_id=1, source_target_pairs={{0,24},{2,26},{4,28},{6,30},{8,16},{10,18},{12,20},{14,22},{16,8},... | collective-permute-start | bytes 786440 | tf_op jit(solution)/shard_map/ppermute | solution.py:256
  101.0 9.0 %collective-permute-start.36 = (bf16[128,1024]{1,0:T(8,128)(2,1)S(1)}, bf16[128,1024]{1,0:T(8,128)(2,1)S(1)}, u32[]{:S(2)}, u32[]{:S(2)}) collective-permute-start(bf16[128,1024]{1,0:T(8,128)(2,1)S(1)} %pad_maximum_fusion.10), channel_id=1, source_target_pairs={{0,8},{2,10},{4,12},{6,14},{8,0},{10,2},{12,4},{14,6},{16,24},{18,... | collective-permute-start | bytes 786440 | tf_op jit(solution)/shard_map/ppermute | solution.py:256
  (11 other events, 54.4 us)

commit v6 on v5

--- a/solution.py
+++ b/solution.py
@@ -76,7 +76,7 @@
     )
 
 
-def route_kernel(ids_ref, weights_ref, tokens_ref, out_ref):
+def route_kernel(ids_ref, weights_ref, tokens_ref, out_ref, own_ref):
     toks = tokens_ref.shape[0]
     experts = out_ref.shape[0] - toks
     total = jnp.zeros((experts, toks), F32)
@@ -87,15 +87,16 @@
     out_ref[:toks] = tokens_ref[...]
     out_ref[toks:] = jnp.zeros((experts, out_ref.shape[1]), BF16)
     out_ref[toks:, :toks] = total.astype(BF16)
+    own_ref[...] = out_ref[...]
 
 
 def route(ids, weights, tokens, experts):
     vmem = pl.BlockSpec(memory_space=pltpu.VMEM)
     return pl.pallas_call(
         route_kernel,
-        out_shape=jax.ShapeDtypeStruct((tokens.shape[0] + experts, tokens.shape[1]), BF16),
+        out_shape=(jax.ShapeDtypeStruct((tokens.shape[0] + experts, tokens.shape[1]), BF16),) * 2,
         in_specs=[vmem] * 3,
-        out_specs=vmem,
+        out_specs=(vmem, vmem),
         cost_estimate=pl.CostEstimate(flops=ROUTE_FLOPS, bytes_accessed=1 << 16, transcendentals=0),
     )(ids, weights, tokens)
 
@@ -317,8 +318,8 @@
     def mix(key, layout):
         return combine(place, [take("table" + key, "own" + key, "back" + key)], [layout], capacity)
 
-    u0p = route(expert_ids.T, route_weights.T, tokens, wide)
-    held.update(u0p=u0p, u2p=hop(u0p, FAR), u1p=hop(u0p, NEAR), u0p_y=hop(u0p, Y))
+    u0p, u0_own = route(expert_ids.T, route_weights.T, tokens, wide)
+    held.update(u0p=u0_own, u2p=hop(u0p, FAR), u1p=hop(u0p, NEAR), u0p_y=hop(u0p, Y))
     held.update(u0_x=hop_x(tokens), u0_yx=hop_xy(tokens))
 
     def gather12():

time: 111 us -> 111 us (level)
  no operation moved by 1% of the time
where the time goes in v6:
time: 111 us
  waiting for transfers between devices  45.3 us (41%)
  starting transfers between devices  39.8 us (36%)
  Pallas kernels  22.1 us (20%)
  other arithmetic  2.07 us (2%)
  local copies, waits for them, and re-layouts  1.3 us (1%)
    ppermute x26, waiting for transfers between devices, hop(): return lax.ppermute(value, 'wide', [(i, i ^ bit) for i in range(wide)])  35.1 us
    ppermute x26, starting transfers between devices, hop(): return lax.ppermute(value, 'wide', [(i, i ^ bit) for i in range(wide)])  25.6 us
    ppermute x11, starting transfers between devices, hop_x(): return lax.ppermute(value, 'narrow', [(0, 1), (1, 0)])  11.8 us
    pallas_call x3, Pallas kernels, ffn(): kernel_call(functools.partial(ffn_kernel, count), (jax.ShapeDtypeStruct((...  11.4 us
    ppermute x11, waiting for transfers between devices, hop_x(): return lax.ppermute(value, 'narrow', [(0, 1), (1, 0)])  10.2 us
    pallas_call x4, Pallas kernels, combine(): kernel_call(functools.partial(combine_kernel, capacity, layouts), tuple((...  4.56 us
    pallas_call x4, Pallas kernels, dispatch(): kernel_call(functools.partial(dispatch_kernel, capacity, toks, layout, ro...  4.26 us
    ppermute x1, starting transfers between devices, hop_xy(): return lax.ppermute(value, ('wide', 'narrow'), pairs)  2.45 us
  transfers between devices with their start and end apart: 38, of which 19 were waited for; matrix products, arithmetic and copies ran while one was open for 1% of the time, Pallas kernels for 18%

profile of v6, /device:TPU:0, one launch (start us, length us, event | category | flops | bytes accessed | tf_op | source)
XLA Modules:
  0.0 111.0 jit_solution(11972975635673661641)
XLA Ops:
  0.0 1.9 %shard_map.64 = (bf16[144,1024]{1,0:T(8,128)(2,1)}, bf16[144,1024]{1,0:T(8,128)(2,1)}) custom-call(s32[6,128]{1,0:T(8,128)} %bitcast.4, bf16[6,128]{1,0:T(8,128)(2,1)} %bitcast.5, bf16[128,1024]{1,0:T(8,128)(2,1)} %tokens_ref.1), custom_call_target="tpu_custom_call" | custom-call | flops 40000000000 | bytes 65536 | tf_op jit(solution)/shard_map/pallas_call | solution.py:95
  1.9 3.0 %collective-permute-start.4 = (bf16[144,1024]{1,0:T(8,128)(2,1)}, bf16[144,1024]{1,0:T(8,128)(2,1)S(1)}, u32[]{:S(2)}, u32[]{:S(2)}) collective-permute-start(bf16[144,1024]{1,0:T(8,128)(2,1)} %get-tuple-element.113), channel_id=1, source_target_pairs={{0,8},{2,10},{4,12},{6,14},{8,0},{10,2},{12,4},{14,6},{16,24},{18,... | collective-permute-start | bytes 884744 | tf_op jit(solution)/shard_map/ppermute | solution.py:257
  4.9 2.6 %collective-permute-start.3 = (bf16[144,1024]{1,0:T(8,128)(2,1)}, bf16[144,1024]{1,0:T(8,128)(2,1)S(1)}, u32[]{:S(2)}, u32[]{:S(2)}) collective-permute-start(bf16[144,1024]{1,0:T(8,128)(2,1)} %get-tuple-element.113), channel_id=1, source_target_pairs={{0,16},{2,18},{4,20},{6,22},{8,24},{10,26},{12,28},{14,30},{16,0},... | collective-permute-start | bytes 884744 | tf_op jit(solution)/shard_map/ppermute | solution.py:257
  7.5 2.4 %collective-permute-start.2 = (bf16[128,1024]{1,0:T(8,128)(2,1)S(1)}, bf16[128,1024]{1,0:T(8,128)(2,1)S(1)}, u32[]{:S(2)}, u32[]{:S(2)}) collective-permute-start(bf16[128,1024]{1,0:T(8,128)(2,1)S(1)} %copy-done.4), channel_id=1, source_target_pairs={{0,5},{1,4},{2,7},{3,6},{4,1},{5,0},{6,3},{7,2},{8,13},{9,12},{10,... | collective-permute-start | bytes 786440 | tf_op jit(solution)/shard_map/ppermute | solution.py:264
  11.1 7.2 %collective-permute-done.4.refs_0_ = bf16[144,1024]{1,0:T(8,128)(2,1)S(1)} collective-permute-done((bf16[144,1024]{1,0:T(8,128)(2,1)}, bf16[144,1024]{1,0:T(8,128)(2,1)S(1)}, u32[]{:S(2)}, u32[]{:S(2)}) %collective-permute-start.4) | collective-permute-done | bytes 294944 | tf_op jit(solution)/shard_map/ppermute | solution.py:257
  18.3 2.6 %collective-permute-done.3.refs_0_ = bf16[144,1024]{1,0:T(8,128)(2,1)S(1)} collective-permute-done((bf16[144,1024]{1,0:T(8,128)(2,1)}, bf16[144,1024]{1,0:T(8,128)(2,1)S(1)}, u32[]{:S(2)}, u32[]{:S(2)}) %collective-permute-start.3) | collective-permute-done | bytes 294944 | tf_op jit(solution)/shard_map/ppermute | solution.py:257
  21.5 1.6 %collective-permute-start.7 = (bf16[160,1024]{1,0:T(8,128)(2,1)S(1)}, bf16[160,1024]{1,0:T(8,128)(2,1)S(1)}, u32[]{:S(2)}, u32[]{:S(2)}) collective-permute-start(bf16[160,1024]{1,0:T(8,128)(2,1)S(1)} %pad_maximum_fusion), channel_id=1, source_target_pairs={{0,4},{2,6},{4,0},{6,2},{8,12},{10,14},{12,8},{14,10},{16,20},{18,... | collective-permute-start | bytes 983048 | tf_op jit(solution)/shard_map/ppermute | solution.py:257
  23.1 1.6 %collective-permute-start.6 = (bf16[128,1024]{1,0:T(8,128)(2,1)S(1)}, bf16[128,1024]{1,0:T(8,128)(2,1)S(1)}, u32[]{:S(2)}, u32[]{:S(2)}) collective-permute-start(bf16[128,1024]{1,0:T(8,128)(2,1)S(1)} %pad_maximum_fusion.2), channel_id=1, source_target_pairs={{0,1},{1,0},{2,3},{3,2},{4,5},{5,4},{6,7},{7,6},{8,9},{9,8},{10,11... | collective-permute-start | bytes 786440 | tf_op jit(solution)/shard_map/ppermute | solution.py:260
  26.8 2.9 %collective-permute-done.6.refs_1_ = bf16[128,1024]{1,0:T(8,128)(2,1)S(1)} collective-permute-done((bf16[128,1024]{1,0:T(8,128)(2,1)S(1)}, bf16[128,1024]{1,0:T(8,128)(2,1)S(1)}, u32[]{:S(2)}, u32[]{:S(2)}) %collective-permute-start.6) | collective-permute-done | bytes 262176 | tf_op jit(solution)/shard_map/ppermute | solution.py:260
  29.9 1.6 %collective-permute-start.9 = (bf16[128,1024]{1,0:T(8,128)(2,1)S(1)}, bf16[128,1024]{1,0:T(8,128)(2,1)S(1)}, u32[]{:S(2)}, u32[]{:S(2)}) collective-permute-start(bf16[128,1024]{1,0:T(8,128)(2,1)S(1)} %pad_maximum_fusion.3), channel_id=1, source_target_pairs={{0,4},{2,6},{4,0},{6,2},{8,12},{10,14},{12,8},{14,10},{16,20},{18,... | collective-permute-start | bytes 786440 | tf_op jit(solution)/shard_map/ppermute | solution.py:257
  31.5 1.6 %collective-permute-start.10 = (bf16[128,1024]{1,0:T(8,128)(2,1)S(1)}, bf16[128,1024]{1,0:T(8,128)(2,1)S(1)}, u32[]{:S(2)}, u32[]{:S(2)}) collective-permute-start(bf16[128,1024]{1,0:T(8,128)(2,1)S(1)} %pad_maximum_fusion.4), channel_id=1, source_target_pairs={{0,1},{1,0},{2,3},{3,2},{4,5},{5,4},{6,7},{7,6},{8,9},{9,8},{10,11... | collective-permute-start | bytes 786440 | tf_op jit(solution)/shard_map/ppermute | solution.py:260
  34.1 3.2 %shard_map.66 = (bf16[112,2048]{1,0:T(8,128)(2,1)S(1)}, bf16[112,2048]{1,0:T(8,128)(2,1)S(1)}) custom-call(s32[2]{0:T(128)S(1)} %pad_add_fusion.place_ref, bf16[112,2048]{1,0:T(8,128)(2,1)S(1)} %get-tuple-element.126.refs_0_, bf16[112,2048]{1,0:T(8,128)(2,1)S(1)} %collective-permute-done.5.refs_1_, bf16[1,704,2048]{2,1,0:T(8,128)(2,1)S(1)} %copy-done, ...), custom_call_target="tpu_custom_call" | custom-call | flops 322961408 | tf_op jit(solution)/shard_map/pallas_call | solution.py:203
  39.7 1.6 %collective-permute-start.18 = (bf16[128,1024]{1,0:T(8,128)(2,1)S(1)}, bf16[128,1024]{1,0:T(8,128)(2,1)S(1)}, u32[]{:S(2)}, u32[]{:S(2)}) collective-permute-start(bf16[128,1024]{1,0:T(8,128)(2,1)S(1)} %pad_maximum_fusion.8), channel_id=1, source_target_pairs={{0,1},{1,0},{2,3},{3,2},{4,5},{5,4},{6,7},{7,6},{8,9},{9,8},{10,11... | collective-permute-start | bytes 786440 | tf_op jit(solution)/shard_map/ppermute | solution.py:260
  41.3 3.2 %shard_map.68 = (bf16[112,2048]{1,0:T(8,128)(2,1)S(1)}, bf16[112,2048]{1,0:T(8,128)(2,1)S(1)}) custom-call(s32[2]{0:T(128)S(1)} %pad_add_fusion.place_ref, bf16[112,2048]{1,0:T(8,128)(2,1)S(1)} %get-tuple-element.140.refs_0_, bf16[112,2048]{1,0:T(8,128)(2,1)S(1)} %collective-permute-done.11.refs_1_, bf16[1,704,2048]{2,1,0:T(8,128)(2,1)S(1)} %copy-done, ...), custom_call_target="tpu_custom_call" | custom-call | flops 322961408 | tf_op jit(solution)/shard_map/pallas_call | solution.py:203
  45.1 1.6 %collective-permute-start.15 = (bf16[128,1024]{1,0:T(8,128)(2,1)S(1)}, bf16[128,1024]{1,0:T(8,128)(2,1)S(1)}, u32[]{:S(2)}, u32[]{:S(2)}) collective-permute-start(bf16[128,1024]{1,0:T(8,128)(2,1)S(1)} %pad_maximum_fusion.5), channel_id=1, source_target_pairs={{0,4},{2,6},{4,0},{6,2},{8,12},{10,14},{12,8},{14,10},{16,20},{18,... | collective-permute-start | bytes 786440 | tf_op jit(solution)/shard_map/ppermute | solution.py:257
  51.5 2.8 %collective-permute-done.15.refs_2_ = bf16[128,1024]{1,0:T(8,128)(2,1)S(1)} collective-permute-done((bf16[128,1024]{1,0:T(8,128)(2,1)S(1)}, bf16[128,1024]{1,0:T(8,128)(2,1)S(1)}, u32[]{:S(2)}, u32[]{:S(2)}) %collective-permute-start.15) | collective-permute-done | bytes 262176 | tf_op jit(solution)/shard_map/ppermute | solution.py:257
  57.7 5.0 %shard_map.73 = (bf16[112,2048]{1,0:T(8,128)(2,1)S(1)}, bf16[112,2048]{1,0:T(8,128)(2,1)S(1)}, bf16[112,2048]{1,0:T(8,128)(2,1)S(1)}, bf16[112,2048]{1,0:T(8,128)(2,1)S(1)}) custom-call(s32[2]{0:T(128)S(1)} %pad_add_fusion.place_ref, bf16[112,2048]{1,0:T(8,128)(2,1)S(1)} %get-tuple-element.169.refs_0_, bf16[112,2048]{1,0:T(8,128)(2,1)S(1)} %get-tuple-element.170.refs_1_, ...), custom_call_target="tpu_custom_call" | custom-call | flops 645922816 | tf_op jit(solution)/shard_map/pallas_call | solution.py:203
  63.5 1.2 %collective-permute-done.14 = bf16[256,1024]{1,0:T(8,128)(2,1)S(1)} collective-permute-done((bf16[256,1024]{1,0:T(8,128)(2,1)S(1)}, bf16[256,1024]{1,0:T(8,128)(2,1)S(1)}, u32[]{:S(2)}, u32[]{:S(2)}) %collective-permute-start.14) | collective-permute-done | bytes 524320 | tf_op jit(solution)/shard_map/ppermute | solution.py:257
  65.0 1.6 %collective-permute-start.22 = (bf16[128,1024]{1,0:T(8,128)(2,1)S(1)}, bf16[128,1024]{1,0:T(8,128)(2,1)S(1)}, u32[]{:S(2)}, u32[]{:S(2)}) collective-permute-start(bf16[128,1024]{1,0:T(8,128)(2,1)S(1)} %get-tuple-element.219), channel_id=1, source_target_pairs={{0,1},{1,0},{2,3},{3,2},{4,5},{5,4},{6,7},{7,6},{8,9},{9,8},{10,11... | collective-permute-start | bytes 786440 | tf_op jit(solution)/shard_map/ppermute | solution.py:260
  68.8 1.8 %collective-permute-done.27 = bf16[256,1024]{1,0:T(8,128)(2,1)S(1)} collective-permute-done((bf16[256,1024]{1,0:T(8,128)(2,1)S(1)}, bf16[256,1024]{1,0:T(8,128)(2,1)S(1)}, u32[]{:S(2)}, u32[]{:S(2)}) %collective-permute-start.27) | collective-permute-done | bytes 524320 | tf_op jit(solution)/shard_map/ppermute | solution.py:260
  73.7 1.4 %collective-permute-start.25 = (bf16[128,1024]{1,0:T(8,128)(2,1)S(1)}, bf16[128,1024]{1,0:T(8,128)(2,1)S(1)}, u32[]{:S(2)}, u32[]{:S(2)}) collective-permute-start(bf16[128,1024]{1,0:T(8,128)(2,1)S(1)} %get-tuple-element.190), channel_id=1, source_target_pairs={{0,4},{2,6},{4,0},{6,2},{8,12},{10,14},{12,8},{14,10},{16,20},{18,... | collective-permute-start | bytes 786440 | tf_op jit(solution)/shard_map/ppermute | solution.py:257
  75.1 4.8 %collective-permute-done.29 = bf16[128,1024]{1,0:T(8,128)(2,1)S(1)} collective-permute-done((bf16[128,1024]{1,0:T(8,128)(2,1)S(1)}, bf16[128,1024]{1,0:T(8,128)(2,1)S(1)}, u32[]{:S(2)}, u32[]{:S(2)}) %collective-permute-start.29) | collective-permute-done | bytes 262176 | tf_op jit(solution)/shard_map/ppermute | solution.py:257
  80.6 1.3 %collective-permute-done.30 = bf16[128,1024]{1,0:T(8,128)(2,1)S(1)} collective-permute-done((bf16[128,1024]{1,0:T(8,128)(2,1)S(1)}, bf16[128,1024]{1,0:T(8,128)(2,1)S(1)}, u32[]{:S(2)}, u32[]{:S(2)}) %collective-permute-start.30) | collective-permute-done | bytes 262176 | tf_op jit(solution)/shard_map/ppermute | solution.py:260
  82.0 3.5 %collective-permute-done.28 = bf16[128,1024]{1,0:T(8,128)(2,1)S(1)} collective-permute-done((bf16[128,1024]{1,0:T(8,128)(2,1)S(1)}, bf16[128,1024]{1,0:T(8,128)(2,1)S(1)}, u32[]{:S(2)}, u32[]{:S(2)}) %collective-permute-start.28) | collective-permute-done | bytes 262176 | tf_op jit(solution)/shard_map/ppermute | solution.py:257
  85.6 2.1 %collective-permute-start.33 = (bf16[128,1024]{1,0:T(8,128)(2,1)S(1)}, bf16[128,1024]{1,0:T(8,128)(2,1)S(1)}, u32[]{:S(2)}, u32[]{:S(2)}) collective-permute-start(bf16[128,1024]{1,0:T(8,128)(2,1)S(1)} %add_convert_fusion.7), channel_id=1, source_target_pairs={{0,16},{2,18},{4,20},{6,22},{8,24},{10,26},{12,28},{14,30},{16,0},... | collective-permute-start | bytes 786440 | tf_op jit(solution)/shard_map/ppermute | solution.py:257
  87.7 1.6 %collective-permute-done.25 = bf16[128,1024]{1,0:T(8,128)(2,1)S(1)} collective-permute-done((bf16[128,1024]{1,0:T(8,128)(2,1)S(1)}, bf16[128,1024]{1,0:T(8,128)(2,1)S(1)}, u32[]{:S(2)}, u32[]{:S(2)}) %collective-permute-start.25) | collective-permute-done | bytes 262176 | tf_op jit(solution)/shard_map/ppermute | solution.py:257
  90.2 1.4 %collective-permute-start.34 = (bf16[64,1024]{1,0:T(8,128)(2,1)S(1)}, bf16[64,1024]{1,0:T(8,128)(2,1)S(1)}, u32[]{:S(2)}, u32[]{:S(2)}) collective-permute-start(bf16[64,1024]{1,0:T(8,128)(2,1)S(1)} %get-tuple-element.237), channel_id=1, source_target_pairs={{0,1},{1,0},{2,3},{3,2},{4,5},{5,4},{6,7},{7,6},{8,9},{9,8},{10,11... | collective-permute-start | bytes 393224 | tf_op jit(solution)/shard_map/ppermute | solution.py:260
  92.9 3.1 %collective-permute-done.34 = bf16[64,1024]{1,0:T(8,128)(2,1)S(1)} collective-permute-done((bf16[64,1024]{1,0:T(8,128)(2,1)S(1)}, bf16[64,1024]{1,0:T(8,128)(2,1)S(1)}, u32[]{:S(2)}, u32[]{:S(2)}) %collective-permute-start.34) | collective-permute-done | bytes 131104 | tf_op jit(solution)/shard_map/ppermute | solution.py:260
  97.5 1.6 %collective-permute-start.37 = (bf16[128,1024]{1,0:T(8,128)(2,1)S(1)}, bf16[128,1024]{1,0:T(8,128)(2,1)S(1)}, u32[]{:S(2)}, u32[]{:S(2)}) collective-permute-start(bf16[128,1024]{1,0:T(8,128)(2,1)S(1)} %pad_maximum_fusion.9), channel_id=1, source_target_pairs={{0,24},{2,26},{4,28},{6,30},{8,16},{10,18},{12,20},{14,22},{16,8},... | collective-permute-start | bytes 786440 | tf_op jit(solution)/shard_map/ppermute | solution.py:257
  99.1 1.8 %collective-permute-done.32 = bf16[64,1024]{1,0:T(8,128)(2,1)S(1)} collective-permute-done((bf16[64,1024]{1,0:T(8,128)(2,1)S(1)}, bf16[64,1024]{1,0:T(8,128)(2,1)S(1)}, u32[]{:S(2)}, u32[]{:S(2)}) %collective-permute-start.32) | collective-permute-done | bytes 131104 | tf_op jit(solution)/shard_map/ppermute | solution.py:257
  102.2 5.7 %collective-permute-done.37 = bf16[128,1024]{1,0:T(8,128)(2,1)S(1)} collective-permute-done((bf16[128,1024]{1,0:T(8,128)(2,1)S(1)}, bf16[128,1024]{1,0:T(8,128)(2,1)S(1)}, u32[]{:S(2)}, u32[]{:S(2)}) %collective-permute-start.37) | collective-permute-done | bytes 262176 | tf_op jit(solution)/shard_map/ppermute | solution.py:257
  107.9 2.3 %collective-permute-done.36 = bf16[128,1024]{1,0:T(8,128)(2,1)S(1)} collective-permute-done((bf16[128,1024]{1,0:T(8,128)(2,1)S(1)}, bf16[128,1024]{1,0:T(8,128)(2,1)S(1)}, u32[]{:S(2)}, u32[]{:S(2)}) %collective-permute-start.36) | collective-permute-done | bytes 262176 | tf_op jit(solution)/shard_map/ppermute | solution.py:257
  (108 shorter events, 28.9 us)
Async XLA Ops:
  1.9 16.4 %collective-permute-start.4 = (bf16[144,1024]{1,0:T(8,128)(2,1)}, bf16[144,1024]{1,0:T(8,128)(2,1)S(1)}, u32[]{:S(2)}, u32[]{:S(2)}) collective-permute-start(bf16[144,1024]{1,0:T(8,128)(2,1)} %get-tuple-element.113), channel_id=1, source_target_pairs={{0,8},{2,10},{4,12},{6,14},{8,0},{10,2},{12,4},{14,6},{16,24},{18,... | collective-permute-start | bytes 884744 | tf_op jit(solution)/shard_map/ppermute | solution.py:257
  4.9 16.0 %collective-permute-start.3 = (bf16[144,1024]{1,0:T(8,128)(2,1)}, bf16[144,1024]{1,0:T(8,128)(2,1)S(1)}, u32[]{:S(2)}, u32[]{:S(2)}) collective-permute-start(bf16[144,1024]{1,0:T(8,128)(2,1)} %get-tuple-element.113), channel_id=1, source_target_pairs={{0,16},{2,18},{4,20},{6,22},{8,24},{10,26},{12,28},{14,30},{16,0},... | collective-permute-start | bytes 884744 | tf_op jit(solution)/shard_map/ppermute | solution.py:257
  7.5 15.6 %collective-permute-start.2 = (bf16[128,1024]{1,0:T(8,128)(2,1)S(1)}, bf16[128,1024]{1,0:T(8,128)(2,1)S(1)}, u32[]{:S(2)}, u32[]{:S(2)}) collective-permute-start(bf16[128,1024]{1,0:T(8,128)(2,1)S(1)} %copy-done.4), channel_id=1, source_target_pairs={{0,5},{1,4},{2,7},{3,6},{4,1},{5,0},{6,3},{7,2},{8,13},{9,12},{10,... | collective-permute-start | bytes 786440 | tf_op jit(solution)/shard_map/ppermute | solution.py:264
  10.0 14.7 %collective-permute-start = (bf16[128,1024]{1,0:T(8,128)(2,1)S(1)}, bf16[128,1024]{1,0:T(8,128)(2,1)S(1)}, u32[]{:S(2)}, u32[]{:S(2)}) collective-permute-start(bf16[128,1024]{1,0:T(8,128)(2,1)S(1)} %copy-done.4), channel_id=1, source_target_pairs={{0,1},{1,0},{2,3},{3,2},{4,5},{5,4},{6,7},{7,6},{8,9},{9,8},{10,11... | collective-permute-start | bytes 786440 | tf_op jit(solution)/shard_map/ppermute | solution.py:260
  10.5 14.2 %collective-permute-start.1 = (bf16[144,1024]{1,0:T(8,128)(2,1)}, bf16[144,1024]{1,0:T(8,128)(2,1)S(1)}, u32[]{:S(2)}, u32[]{:S(2)}) collective-permute-start(bf16[144,1024]{1,0:T(8,128)(2,1)} %get-tuple-element.113), channel_id=1, source_target_pairs={{0,4},{2,6},{4,0},{6,2},{8,12},{10,14},{12,8},{14,10},{16,20},{18,... | collective-permute-start | bytes 884744 | tf_op jit(solution)/shard_map/ppermute | solution.py:257
  21.0 20.3 %collective-permute-start.12 = (bf16[144,1024]{1,0:T(8,128)(2,1)S(1)}, bf16[144,1024]{1,0:T(8,128)(2,1)S(1)}, u32[]{:S(2)}, u32[]{:S(2)}) collective-permute-start(bf16[144,1024]{1,0:T(8,128)(2,1)S(1)} %collective-permute-done.3.refs_0_), channel_id=1, source_target_pairs={{0,8},{2,10},{4,12},{6,14},{8,0},{10,2},{12,4},{14,6},{16,24},{18,... | collective-permute-start | bytes 884744 | tf_op jit(solution)/shard_map/ppermute | solution.py:257
  21.5 8.3 %collective-permute-start.7 = (bf16[160,1024]{1,0:T(8,128)(2,1)S(1)}, bf16[160,1024]{1,0:T(8,128)(2,1)S(1)}, u32[]{:S(2)}, u32[]{:S(2)}) collective-permute-start(bf16[160,1024]{1,0:T(8,128)(2,1)S(1)} %pad_maximum_fusion), channel_id=1, source_target_pairs={{0,4},{2,6},{4,0},{6,2},{8,12},{10,14},{12,8},{14,10},{16,20},{18,... | collective-permute-start | bytes 983048 | tf_op jit(solution)/shard_map/ppermute | solution.py:257
  23.1 6.6 %collective-permute-start.6 = (bf16[128,1024]{1,0:T(8,128)(2,1)S(1)}, bf16[128,1024]{1,0:T(8,128)(2,1)S(1)}, u32[]{:S(2)}, u32[]{:S(2)}) collective-permute-start(bf16[128,1024]{1,0:T(8,128)(2,1)S(1)} %pad_maximum_fusion.2), channel_id=1, source_target_pairs={{0,1},{1,0},{2,3},{3,2},{4,5},{5,4},{6,7},{7,6},{8,9},{9,8},{10,11... | collective-permute-start | bytes 786440 | tf_op jit(solution)/shard_map/ppermute | solution.py:260
  26.7 7.4 %collective-permute-start.5 = (bf16[112,2048]{1,0:T(8,128)(2,1)S(1)}, bf16[112,2048]{1,0:T(8,128)(2,1)S(1)}, u32[]{:S(2)}, u32[]{:S(2)}) collective-permute-start(bf16[112,2048]{1,0:T(8,128)(2,1)S(1)} %get-tuple-element.121), channel_id=1, source_target_pairs={{0,2},{2,0},{4,6},{6,4},{8,10},{10,8},{12,14},{14,12},{16,18},{18,... | collective-permute-start | bytes 1376264 | tf_op jit(solution)/shard_map/ppermute | solution.py:257
  29.9 7.4 %collective-permute-start.9 = (bf16[128,1024]{1,0:T(8,128)(2,1)S(1)}, bf16[128,1024]{1,0:T(8,128)(2,1)S(1)}, u32[]{:S(2)}, u32[]{:S(2)}) collective-permute-start(bf16[128,1024]{1,0:T(8,128)(2,1)S(1)} %pad_maximum_fusion.3), channel_id=1, source_target_pairs={{0,4},{2,6},{4,0},{6,2},{8,12},{10,14},{12,8},{14,10},{16,20},{18,... | collective-permute-start | bytes 786440 | tf_op jit(solution)/shard_map/ppermute | solution.py:257
  31.5 6.4 %collective-permute-start.10 = (bf16[128,1024]{1,0:T(8,128)(2,1)S(1)}, bf16[128,1024]{1,0:T(8,128)(2,1)S(1)}, u32[]{:S(2)}, u32[]{:S(2)}) collective-permute-start(bf16[128,1024]{1,0:T(8,128)(2,1)S(1)} %pad_maximum_fusion.4), channel_id=1, source_target_pairs={{0,1},{1,0},{2,3},{3,2},{4,5},{5,4},{6,7},{7,6},{8,9},{9,8},{10,11... | collective-permute-start | bytes 786440 | tf_op jit(solution)/shard_map/ppermute | solution.py:260
  33.1 8.2 %collective-permute-start.13 = (bf16[144,1024]{1,0:T(8,128)(2,1)S(1)}, bf16[144,1024]{1,0:T(8,128)(2,1)S(1)}, u32[]{:S(2)}, u32[]{:S(2)}) collective-permute-start(bf16[144,1024]{1,0:T(8,128)(2,1)S(1)} %pad_maximum_fusion.1), channel_id=1, source_target_pairs={{0,8},{2,10},{4,12},{6,14},{8,0},{10,2},{12,4},{14,6},{16,24},{18,... | collective-permute-start | bytes 884744 | tf_op jit(solution)/shard_map/ppermute | solution.py:257
  39.1 11.2 %collective-permute-start.17 = (bf16[128,1024]{1,0:T(8,128)(2,1)S(1)}, bf16[128,1024]{1,0:T(8,128)(2,1)S(1)}, u32[]{:S(2)}, u32[]{:S(2)}) collective-permute-start(bf16[128,1024]{1,0:T(8,128)(2,1)S(1)} %pad_maximum_fusion.7), channel_id=1, source_target_pairs={{0,4},{2,6},{4,0},{6,2},{8,12},{10,14},{12,8},{14,10},{16,20},{18,... | collective-permute-start | bytes 786440 | tf_op jit(solution)/shard_map/ppermute | solution.py:257
  39.7 10.7 %collective-permute-start.18 = (bf16[128,1024]{1,0:T(8,128)(2,1)S(1)}, bf16[128,1024]{1,0:T(8,128)(2,1)S(1)}, u32[]{:S(2)}, u32[]{:S(2)}) collective-permute-start(bf16[128,1024]{1,0:T(8,128)(2,1)S(1)} %pad_maximum_fusion.8), channel_id=1, source_target_pairs={{0,1},{1,0},{2,3},{3,2},{4,5},{5,4},{6,7},{7,6},{8,9},{9,8},{10,11... | collective-permute-start | bytes 786440 | tf_op jit(solution)/shard_map/ppermute | solution.py:260
  41.3 5.4 %collective-permute-start.8 = (bf16[112,2048]{1,0:T(8,128)(2,1)S(1)}, bf16[112,2048]{1,0:T(8,128)(2,1)S(1)}, u32[]{:S(2)}, u32[]{:S(2)}) collective-permute-start(bf16[112,2048]{1,0:T(8,128)(2,1)S(1)} %get-tuple-element.129), channel_id=1, source_target_pairs={{0,2},{2,0},{4,6},{6,4},{8,10},{10,8},{12,14},{14,12},{16,18},{18,... | collective-permute-start | bytes 1376264 | tf_op jit(solution)/shard_map/ppermute | solution.py:257
  45.1 9.2 %collective-permute-start.15 = (bf16[128,1024]{1,0:T(8,128)(2,1)S(1)}, bf16[128,1024]{1,0:T(8,128)(2,1)S(1)}, u32[]{:S(2)}, u32[]{:S(2)}) collective-permute-start(bf16[128,1024]{1,0:T(8,128)(2,1)S(1)} %pad_maximum_fusion.5), channel_id=1, source_target_pairs={{0,4},{2,6},{4,0},{6,2},{8,12},{10,14},{12,8},{14,10},{16,20},{18,... | collective-permute-start | bytes 786440 | tf_op jit(solution)/shard_map/ppermute | solution.py:257
  46.7 8.0 %collective-permute-start.16 = (bf16[128,1024]{1,0:T(8,128)(2,1)S(1)}, bf16[128,1024]{1,0:T(8,128)(2,1)S(1)}, u32[]{:S(2)}, u32[]{:S(2)}) collective-permute-start(bf16[128,1024]{1,0:T(8,128)(2,1)S(1)} %pad_maximum_fusion.6), channel_id=1, source_target_pairs={{0,1},{1,0},{2,3},{3,2},{4,5},{5,4},{6,7},{7,6},{8,9},{9,8},{10,11... | collective-permute-start | bytes 786440 | tf_op jit(solution)/shard_map/ppermute | solution.py:260
  48.5 16.2 %collective-permute-start.14 = (bf16[256,1024]{1,0:T(8,128)(2,1)S(1)}, bf16[256,1024]{1,0:T(8,128)(2,1)S(1)}, u32[]{:S(2)}, u32[]{:S(2)}) collective-permute-start(bf16[256,1024]{1,0:T(8,128)(2,1)S(1)} %get-tuple-element.147), channel_id=1, source_target_pairs={{0,4},{2,6},{4,0},{6,2},{8,12},{10,14},{12,8},{14,10},{16,20},{18,... | collective-permute-start | bytes 1572872 | tf_op jit(solution)/shard_map/ppermute | solution.py:257
  51.5 5.2 %collective-permute-start.21 = (bf16[112,2048]{1,0:T(8,128)(2,1)S(1)}, bf16[112,2048]{1,0:T(8,128)(2,1)S(1)}, u32[]{:S(2)}, u32[]{:S(2)}) collective-permute-start(bf16[112,2048]{1,0:T(8,128)(2,1)S(1)} %get-tuple-element.168), channel_id=1, source_target_pairs={{0,2},{2,0},{4,6},{6,4},{8,10},{10,8},{12,14},{14,12},{16,18},{18,... | collective-permute-start | bytes 1376264 | tf_op jit(solution)/shard_map/ppermute | solution.py:257
  55.9 14.8 %collective-permute-start.27 = (bf16[256,1024]{1,0:T(8,128)(2,1)S(1)}, bf16[256,1024]{1,0:T(8,128)(2,1)S(1)}, u32[]{:S(2)}, u32[]{:S(2)}) collective-permute-start(bf16[256,1024]{1,0:T(8,128)(2,1)S(1)} %get-tuple-element.192), channel_id=1, source_target_pairs={{0,1},{1,0},{2,3},{3,2},{4,5},{5,4},{6,7},{7,6},{8,9},{9,8},{10,11... | collective-permute-start | bytes 1572872 | tf_op jit(solution)/shard_map/ppermute | solution.py:260
  65.0 37.2 %collective-permute-start.22 = (bf16[128,1024]{1,0:T(8,128)(2,1)S(1)}, bf16[128,1024]{1,0:T(8,128)(2,1)S(1)}, u32[]{:S(2)}, u32[]{:S(2)}) collective-permute-start(bf16[128,1024]{1,0:T(8,128)(2,1)S(1)} %get-tuple-element.219), channel_id=1, source_target_pairs={{0,1},{1,0},{2,3},{3,2},{4,5},{5,4},{6,7},{7,6},{8,9},{9,8},{10,11... | collective-permute-start | bytes 786440 | tf_op jit(solution)/shard_map/ppermute | solution.py:260
  70.7 9.2 %collective-permute-start.29 = (bf16[128,1024]{1,0:T(8,128)(2,1)S(1)}, bf16[128,1024]{1,0:T(8,128)(2,1)S(1)}, u32[]{:S(2)}, u32[]{:S(2)}) collective-permute-start(bf16[128,1024]{1,0:T(8,128)(2,1)S(1)} %get-tuple-element.196), channel_id=1, source_target_pairs={{0,4},{2,6},{4,0},{6,2},{8,12},{10,14},{12,8},{14,10},{16,20},{18,... | collective-permute-start | bytes 786440 | tf_op jit(solution)/shard_map/ppermute | solution.py:257
  71.8 10.1 %collective-permute-start.30 = (bf16[128,1024]{1,0:T(8,128)(2,1)S(1)}, bf16[128,1024]{1,0:T(8,128)(2,1)S(1)}, u32[]{:S(2)}, u32[]{:S(2)}) collective-permute-start(bf16[128,1024]{1,0:T(8,128)(2,1)S(1)} %get-tuple-element.197), channel_id=1, source_target_pairs={{0,1},{1,0},{2,3},{3,2},{4,5},{5,4},{6,7},{7,6},{8,9},{9,8},{10,11... | collective-permute-start | bytes 786440 | tf_op jit(solution)/shard_map/ppermute | solution.py:260
  73.0 12.5 %collective-permute-start.28 = (bf16[128,1024]{1,0:T(8,128)(2,1)S(1)}, bf16[128,1024]{1,0:T(8,128)(2,1)S(1)}, u32[]{:S(2)}, u32[]{:S(2)}) collective-permute-start(bf16[128,1024]{1,0:T(8,128)(2,1)S(1)} %get-tuple-element.221), channel_id=1, source_target_pairs={{0,4},{2,6},{4,0},{6,2},{8,12},{10,14},{12,8},{14,10},{16,20},{18,... | collective-permute-start | bytes 786440 | tf_op jit(solution)/shard_map/ppermute | solution.py:257
  73.7 15.7 %collective-permute-start.25 = (bf16[128,1024]{1,0:T(8,128)(2,1)S(1)}, bf16[128,1024]{1,0:T(8,128)(2,1)S(1)}, u32[]{:S(2)}, u32[]{:S(2)}) collective-permute-start(bf16[128,1024]{1,0:T(8,128)(2,1)S(1)} %get-tuple-element.190), channel_id=1, source_target_pairs={{0,4},{2,6},{4,0},{6,2},{8,12},{10,14},{12,8},{14,10},{16,20},{18,... | collective-permute-start | bytes 786440 | tf_op jit(solution)/shard_map/ppermute | solution.py:257
  79.9 9.4 %collective-permute-start.26 = (bf16[128,1024]{1,0:T(8,128)(2,1)S(1)}, bf16[128,1024]{1,0:T(8,128)(2,1)S(1)}, u32[]{:S(2)}, u32[]{:S(2)}) collective-permute-start(bf16[128,1024]{1,0:T(8,128)(2,1)S(1)} %get-tuple-element.191), channel_id=1, source_target_pairs={{0,1},{1,0},{2,3},{3,2},{4,5},{5,4},{6,7},{7,6},{8,9},{9,8},{10,11... | collective-permute-start | bytes 786440 | tf_op jit(solution)/shard_map/ppermute | solution.py:260
  85.6 13.5 %collective-permute-start.33 = (bf16[128,1024]{1,0:T(8,128)(2,1)S(1)}, bf16[128,1024]{1,0:T(8,128)(2,1)S(1)}, u32[]{:S(2)}, u32[]{:S(2)}) collective-permute-start(bf16[128,1024]{1,0:T(8,128)(2,1)S(1)} %add_convert_fusion.7), channel_id=1, source_target_pairs={{0,16},{2,18},{4,20},{6,22},{8,24},{10,26},{12,28},{14,30},{16,0},... | collective-permute-start | bytes 786440 | tf_op jit(solution)/shard_map/ppermute | solution.py:257
  89.4 9.7 %collective-permute-start.31 = (bf16[64,1024]{1,0:T(8,128)(2,1)S(1)}, bf16[64,1024]{1,0:T(8,128)(2,1)S(1)}, u32[]{:S(2)}, u32[]{:S(2)}) collective-permute-start(bf16[64,1024]{1,0:T(8,128)(2,1)S(1)} %get-tuple-element.233), channel_id=1, source_target_pairs={{0,1},{1,0},{2,3},{3,2},{4,5},{5,4},{6,7},{7,6},{8,9},{9,8},{10,11... | collective-permute-start | bytes 393224 | tf_op jit(solution)/shard_map/ppermute | solution.py:260
  90.2 5.8 %collective-permute-start.34 = (bf16[64,1024]{1,0:T(8,128)(2,1)S(1)}, bf16[64,1024]{1,0:T(8,128)(2,1)S(1)}, u32[]{:S(2)}, u32[]{:S(2)}) collective-permute-start(bf16[64,1024]{1,0:T(8,128)(2,1)S(1)} %get-tuple-element.237), channel_id=1, source_target_pairs={{0,1},{1,0},{2,3},{3,2},{4,5},{5,4},{6,7},{7,6},{8,9},{9,8},{10,11... | collective-permute-start | bytes 393224 | tf_op jit(solution)/shard_map/ppermute | solution.py:260
  91.6 5.8 %collective-permute-start.35 = (bf16[64,1024]{1,0:T(8,128)(2,1)S(1)}, bf16[64,1024]{1,0:T(8,128)(2,1)S(1)}, u32[]{:S(2)}, u32[]{:S(2)}) collective-permute-start(bf16[64,1024]{1,0:T(8,128)(2,1)S(1)} %get-tuple-element.235), channel_id=1, source_target_pairs={{0,4},{2,6},{4,0},{6,2},{8,12},{10,14},{12,8},{14,10},{16,20},{18,... | collective-permute-start | bytes 393224 | tf_op jit(solution)/shard_map/ppermute | solution.py:257
  97.5 10.3 %collective-permute-start.37 = (bf16[128,1024]{1,0:T(8,128)(2,1)S(1)}, bf16[128,1024]{1,0:T(8,128)(2,1)S(1)}, u32[]{:S(2)}, u32[]{:S(2)}) collective-permute-start(bf16[128,1024]{1,0:T(8,128)(2,1)S(1)} %pad_maximum_fusion.9), channel_id=1, source_target_pairs={{0,24},{2,26},{4,28},{6,30},{8,16},{10,18},{12,20},{14,22},{16,8},... | collective-permute-start | bytes 786440 | tf_op jit(solution)/shard_map/ppermute | solution.py:257
  101.1 9.0 %collective-permute-start.36 = (bf16[128,1024]{1,0:T(8,128)(2,1)S(1)}, bf16[128,1024]{1,0:T(8,128)(2,1)S(1)}, u32[]{:S(2)}, u32[]{:S(2)}) collective-permute-start(bf16[128,1024]{1,0:T(8,128)(2,1)S(1)} %pad_maximum_fusion.10), channel_id=1, source_target_pairs={{0,8},{2,10},{4,12},{6,14},{8,0},{10,2},{12,4},{14,6},{16,24},{18,... | collective-permute-start | bytes 786440 | tf_op jit(solution)/shard_map/ppermute | solution.py:257
  (11 other events, 54.4 us)
